TPU v7x, 32 devices: a whole 2x2x4 slice. The times are simulated.
32 devices in a mesh: ctx: 8 (over y, x, core), fsdp: 4 (over z).
Axes of the slice: x: 2, y: 2, z: 4, core: 2. Of those that a mesh axis runs over, the one named last changes fastest.
Arguments:
- tokens: bfloat16 [4096, 960], P(('ctx', 'fsdp')), may hold values from -6 to 6
- pair_order: int32 [32], replicated, may hold values from 0 to 31, each once
- gain_attn: bfloat16 [960], P('fsdp'), may hold values from 0.5 to 1.5
- gain_mlp: bfloat16 [960], P('fsdp'), may hold values from 0.5 to 1.5
- w_query: bfloat16 [960, 960], P('fsdp'), may hold values from -0.3125 to 0.3125
- w_key: bfloat16 [960, 320], P('fsdp'), may hold values from -0.3125 to 0.3125
- w_value: bfloat16 [960, 320], P('fsdp'), may hold values from -0.1875 to 0.1875
- w_out: bfloat16 [960, 960], P('fsdp'), may hold values from -0.75 to 0.75
- w_gate: bfloat16 [960, 2560], P('fsdp'), may hold values from -0.1875 to 0.1875
- w_up: bfloat16 [960, 2560], P('fsdp'), may hold values from -0.1875 to 0.1875
- w_down: bfloat16 [2560, 960], P('fsdp'), may hold values from -0.125 to 0.125
- cotangent: bfloat16 [4096, 960], P(('ctx', 'fsdp')), may hold values from -6 to 6
Outputs:
- layer_out: bfloat16 [4096, 960], P(('ctx', 'fsdp'))
- grad_tokens: float32 [4096, 960], P(('ctx', 'fsdp'))
- grad_gain_attn: float32 [960], P('fsdp')
- grad_gain_mlp: float32 [960], P('fsdp')
- grad_w_query: float32 [960, 960], P('fsdp')
- grad_w_key: float32 [960, 320], P('fsdp')
- grad_w_value: float32 [960, 320], P('fsdp')
- grad_w_out: float32 [960, 960], P('fsdp')
- grad_w_gate: float32 [960, 2560], P('fsdp')
- grad_w_up: float32 [960, 2560], P('fsdp')
- grad_w_down: float32 [2560, 960], P('fsdp')
Inputs may be any that keep to these rules, and one draw needn't show every extreme that they name: Slot d holds sequence blocks pair_order[d] and 63 - pair_order[d]; each value appears once.
All inputs are finite; a program needn't handle non-finite values.
Results may differ from a plain program's by a relative error of at most 0.025.
Values may be sent and summed in bfloat16 or wider, within the bound.
No kernel may reach another device: no remote copies, remote signals or barrier semaphores. Data moves between devices by JAX's collectives and lax.ppermute only.
A program may use at most 256 MiB of HBM per device.

v0:
```python
import functools

import jax
import jax.numpy as jnp
from jax import lax
from jax.experimental import pallas as pl
from jax.experimental.pallas import tpu as pltpu
from jax.sharding import PartitionSpec as P

HEADS = 15
KV_HEADS = 5
HEAD = 64
TP = 8
GROUP = HEADS // KV_HEADS
OWN = 2 * HEAD
epsilon = 1e-05
base_theta = 100000.0
far_below = -1e30
f32 = jnp.float32
bf16 = jnp.bfloat16
i32 = jnp.int32
AXES = ("ctx", "fsdp")
MIB = 1024 * 1024
smem = pl.BlockSpec(memory_space=pltpu.SMEM)
vmem = pl.BlockSpec(memory_space=pltpu.VMEM)


def exchange(array, mask, count):
    return lax.ppermute(array, AXES, [(i, i ^ mask) for i in range(count)])


def nn(left, right):
    return lax.dot_general(left, right, (((1,), (0,)), ((), ())), preferred_element_type=f32)


def tn(left, right):
    return lax.dot_general(left, right, (((0,), (0,)), ((), ())), preferred_element_type=f32)


def nt(left, right):
    return lax.dot_general(left, right, (((1,), (1,)), ((), ())), preferred_element_type=f32)


def shape(dims, dtype):
    return jax.ShapeDtypeStruct(dims, dtype)


def call(kernel, outs, inputs, scalars=1, scratch=(), limit=56, cost=1.0, far=()):
    specs = [smem] * scalars + [vmem] * (len(inputs) - scalars)
    for i in far:
        specs[i] = pl.BlockSpec(memory_space=pl.ANY)
    return pl.pallas_call(
        kernel,
        out_shape=tuple(outs),
        in_specs=specs,
        out_specs=tuple(vmem for unused in outs),
        scratch_shapes=list(scratch),
        compiler_params=pltpu.CompilerParams(vmem_limit_bytes=limit * MIB),
        cost_estimate=pl.CostEstimate(
            flops=int(cost * 1e9), bytes_accessed=int(cost * 1e6), transcendentals=0
        ),
    )(*inputs)


def one_hot(rows, columns, start):
    row = lax.broadcasted_iota(i32, (rows, columns), 0)
    column = lax.broadcasted_iota(i32, (rows, columns), 1)
    return jnp.where(row == column + start, 1.0, 0.0).astype(bf16)


def query_positions(base_ref, at, width, half_rows):
    lane = lax.broadcasted_iota(i32, (1, width), 1)
    place = jnp.zeros((1, width), i32)
    for block in range(width // half_rows):
        start = base_ref[at + block] - block * half_rows
        place = jnp.where(lane >= block * half_rows, start + lane, place)
    return place


def key_positions(base_ref, row, at, count, half_rows, width):
    offset = lax.broadcasted_iota(i32, (half_rows, width), 0)
    return jnp.concatenate([offset + base_ref[row, at + b] for b in range(count)], axis=0)


def swap_halves(matrix):
    lane = lax.broadcasted_iota(i32, matrix.shape, 1)
    ahead = pltpu.roll(matrix, matrix.shape[1] - HEAD // 2, 1)
    behind = pltpu.roll(matrix, HEAD // 2, 1)
    return jnp.where(lane % HEAD < HEAD // 2, ahead, behind)


def norm_scale(matrix):
    return lax.rsqrt(jnp.mean(matrix * matrix, axis=1, keepdims=True) + epsilon)


def slice_attention_weights(at, w_query, w_key, w_value, w_out, gain_one, gain_two):
    d_rows, width = w_query.shape
    lanes = 2 * OWN + OWN
    rest = width - (TP - 1) * OWN

    def kernel(at_ref, q_ref, k_ref, v_ref, o_ref, g_ref, out_ref, cols, heads, whole, sems):
        tp = at_ref[0]
        kv = at_ref[2]
        wides, narrows = (q_ref, o_ref), (k_ref, v_ref)

        @pl.when(tp < TP - 1)
        def most():
            columns = pl.ds(pl.multiple_of(tp * OWN, OWN), OWN)
            copies = [
                pltpu.make_async_copy(ref.at[:, columns], cols.at[i], sems.at[i])
                for i, ref in enumerate(wides)
            ]
            for copy in copies:
                copy.start()
            for copy in copies:
                copy.wait()

        @pl.when(tp == TP - 1)
        def last():
            copies = [
                pltpu.make_async_copy(ref, whole.at[i], sems.at[i]) for i, ref in enumerate(wides)
            ]
            for copy in copies:
                copy.start()
            for copy in copies:
                copy.wait()
            for i in range(2):
                cols[i] = jnp.zeros((d_rows, OWN), bf16)
                cols[i, :, pl.ds(0, rest)] = whole[i, :, pl.ds(width - rest, rest)]

        @pl.when(kv < KV_HEADS)
        def real():
            rows = pl.ds(pl.multiple_of(kv * HEAD, HEAD), HEAD)
            copies = [
                pltpu.make_async_copy(ref.at[rows, :], heads.at[i], sems.at[2 + i])
                for i, ref in enumerate(narrows)
            ]
            for copy in copies:
                copy.start()
            for copy in copies:
                copy.wait()

        @pl.when(kv >= KV_HEADS)
        def none():
            heads[...] = jnp.zeros_like(heads)

        out_ref[pl.ds(0, d_rows), pl.ds(0, OWN)] = cols[0]
        turned = jnp.concatenate([heads[0], heads[1]], axis=0).astype(f32).T
        out_ref[pl.ds(0, d_rows), pl.ds(OWN, OWN)] = turned.astype(bf16)
        out_ref[pl.ds(0, d_rows), pl.ds(2 * OWN, OWN)] = cols[1]
        out_ref[pl.ds(d_rows, 16), :] = jnp.zeros((16, lanes), bf16)
        out_ref[pl.ds(d_rows, 2), pl.ds(0, d_rows)] = g_ref[...]

    return call(
        kernel,
        [shape((d_rows + 16, lanes), bf16)],
        [at, w_query, w_key.T, w_value.T, w_out, jnp.stack([gain_one, gain_two])],
        scratch=[
            pltpu.VMEM((2, d_rows, OWN), bf16),
            pltpu.VMEM((2, HEAD, d_rows), bf16),
            pltpu.VMEM((2, d_rows, width), bf16),
            pltpu.SemaphoreType.DMA((4,)),
        ],
        limit=8,
        cost=2.0,
        far=(1, 2, 3, 4),
    )[0]


def slice_ff_weights(at, w_gate, w_up, w_down, nz):
    d_rows = w_gate.shape[0]
    ff_z, width = w_down.shape
    part = ff_z // TP
    own = part * nz

    def kernel(at_ref, g_ref, u_ref, d_ref, out_ref):
        pick = one_hot(ff_z, part, at_ref[0] * part)
        for ref, start in ((g_ref, 0), (u_ref, own)):
            pieces = [nn(ref[:, pl.ds(s * ff_z, ff_z)], pick) for s in range(nz)]
            out_ref[:, pl.ds(start, own)] = jnp.concatenate(pieces, axis=1).astype(bf16)
        pieces = [nn(d_ref[pl.ds(s * d_rows, d_rows), :], pick) for s in range(nz)]
        out_ref[:, pl.ds(2 * own, own)] = jnp.concatenate(pieces, axis=1).astype(bf16)

    return call(
        kernel,
        [shape((d_rows, 3 * own), bf16)],
        [at, w_gate, w_up, w_down.T],
        limit=16,
        cost=4.0,
    )[0]


def project(at, tokens, packs, cosine, sine, cotangent):
    local, width = tokens[0].shape
    half_rows = local // 2
    rows = TP * local
    nz = len(packs)
    pack_rows, lanes = packs[0].shape
    d_rows = pack_rows - 16

    def kernel(at_ref, *refs):
        toks, refs = refs[:TP], refs[TP:]
        pack, refs = refs[:nz], refs[nz:]
        cos_ref, sin_ref, cot_ref, x_ref, hid_ref, qt_ref, kv_ref, w_ref, cot_out, wo_out, gain_ref, hold = refs
        z = at_ref[1]
        for s in range(nz):
            hold[z ^ s] = pack[s][...]
        for s in range(nz):
            w_ref[pl.ds(s * d_rows, d_rows), :] = hold[s, pl.ds(0, d_rows), pl.ds(0, 2 * OWN)]
        gains = [hold[s, pl.ds(d_rows, 16), pl.ds(0, d_rows)].astype(f32) for s in range(nz)]
        gain_ref[...] = jnp.concatenate(gains, axis=1)[:8]
        gain = gain_ref[pl.ds(0, 1), :]
        cot_out[:, pl.ds(0, width)] = cot_ref[...]
        turned = [
            hold[s, pl.ds(0, d_rows), pl.ds(2 * OWN, OWN)].astype(f32) for s in range(nz)
        ]
        wo_out[:, pl.ds(0, width)] = jnp.concatenate(turned, axis=0).T.astype(bf16)
        per = 4
        for tile in range(2 * TP // per):
            side, first = (tile * per) // TP, (tile * per) % TP
            at_rows = pl.ds(tile * per * half_rows, per * half_rows)
            block = jnp.concatenate(
                [toks[first + j][pl.ds(side * half_rows, half_rows), :] for j in range(per)], axis=0
            )
            x_ref[at_rows, :] = block
            inputs = block.astype(f32)
            hidden = (inputs * norm_scale(inputs) * gain).astype(bf16)
            hid_ref[at_rows, :] = hidden
            out = nn(hidden, w_ref[...])
            cos, sin = cos_ref[at_rows, :], sin_ref[at_rows, :]
            query = out[:, :OWN]
            query = query * cos + swap_halves(query) * sin
            qt_ref[:, at_rows] = (query.astype(bf16).astype(f32) * HEAD**-0.5).T.astype(bf16)
            pair = out[:, OWN:]
            turned = pair * cos + swap_halves(pair) * sin
            lane = lax.broadcasted_iota(i32, pair.shape, 1)
            kv_ref[at_rows, :] = jnp.where(lane < HEAD, turned, pair).astype(bf16)

    return call(
        kernel,
        [
            shape((rows, width), bf16),
            shape((rows, width), bf16),
            shape((OWN, rows), bf16),
            shape((rows, OWN), bf16),
            shape((width, 2 * OWN), bf16),
            shape((local, TP * OWN), bf16),
            shape((OWN, TP * OWN), bf16),
            shape((8, width), f32),
        ],
        [at, *tokens, *packs, cosine, sine, cotangent],
        scratch=[pltpu.VMEM((nz, pack_rows, lanes), bf16)],
        limit=24,
        cost=6.0,
    )


def attention_forward(select, key_base, query_base, turned_query, own_kv, other_kv, half_rows):
    groups = len(own_kv)
    rows = own_kv[0].shape[0]
    half = rows // 2
    blocks = half // half_rows
    wide, deep = 128, 128

    def kernel(sel_ref, key_ref, query_ref, q_ref, *refs):
        own, other = refs[:groups], refs[groups : 2 * groups]
        out_ref, low_ref, lse_ref, kv_ref, kvt_ref, top_ref, mass_ref, place_ref = refs[2 * groups :]
        for head in range(2):
            chosen = sel_ref[head] == 0
            for group in range(groups):

                @pl.when(chosen)
                def take_own():
                    kv_ref[head, group] = own[group][...]
                    kvt_ref[head, group] = own[group][...].T

                @pl.when(jnp.logical_not(chosen))
                def take_other():
                    kv_ref[head, group] = other[group][...]
                    kvt_ref[head, group] = other[group][...].T

        top_ref[...] = jnp.full_like(top_ref, far_below)
        mass_ref[...] = jnp.zeros_like(mass_ref)
        out_ref[...] = jnp.zeros_like(out_ref)

        def one_group(group, unused):
            for head in range(2):
                row = sel_ref[head] * groups + group
                own_rows = pl.ds(head * HEAD, HEAD)
                stat = pl.ds(head, 1)
                place_ref[...] = key_positions(key_ref, row, 0, 2 * blocks, half_rows, 128)
                for k_start in range(0, rows, deep):
                    keys_at = pl.ds(k_start, deep)
                    k_side = k_start // half
                    block = kv_ref[head, group, keys_at, :]
                    values = kvt_ref[head, group, pl.ds(HEAD, HEAD), keys_at]
                    for start in range(k_side * half, rows, wide):
                        lanes = pl.ds(start, wide)
                        turned = q_ref[own_rows, lanes]
                        padded = jnp.concatenate([turned, jnp.zeros_like(turned)], axis=0)
                        scores = nn(block, padded)
                        if start // half == k_side:
                            places = query_positions(
                                query_ref, start // half_rows, wide, half_rows
                            )
                            scores = jnp.where(place_ref[keys_at, :] <= places, scores, far_below)
                        before = top_ref[stat, lanes]
                        top = jnp.maximum(before, jnp.max(scores, axis=0, keepdims=True))
                        weights = jnp.exp(scores - top)
                        fade = jnp.exp(before - top)
                        top_ref[stat, lanes] = top
                        mass_ref[stat, lanes] = mass_ref[stat, lanes] * fade + jnp.sum(
                            weights, axis=0, keepdims=True
                        )
                        out_ref[own_rows, lanes] = out_ref[own_rows, lanes] * fade + nn(
                            values, weights.astype(bf16)
                        )
            return unused

        lax.fori_loop(0, groups, one_group, 0)
        for head in range(2):
            own_rows = pl.ds(head * HEAD, HEAD)
            mass = mass_ref[pl.ds(head, 1), :]
            out_ref[own_rows, :] = out_ref[own_rows, :] / mass
            lse_ref[pl.ds(head, 1), :] = top_ref[pl.ds(head, 1), :] + jnp.log(mass)
        low_ref[...] = out_ref[...].T.astype(bf16)

    return call(
        kernel,
        [shape((OWN, rows), f32), shape((rows, OWN), bf16), shape((2, rows), f32)],
        [select, key_base, query_base, turned_query, *own_kv, *other_kv],
        scalars=3,
        scratch=[
            pltpu.VMEM((2, groups, rows, OWN), bf16),
            pltpu.VMEM((2, groups, OWN, rows), bf16),
            pltpu.VMEM((2, rows), f32),
            pltpu.VMEM((2, rows), f32),
            pltpu.VMEM((rows, 128), i32),
        ],
        limit=24,
        cost=14.0,
    )


def attention_backward(
    select, key_base, query_base, turned_query, own_kv, other_kv, traded, attended, log_mass, half_rows
):
    groups = len(own_kv)
    rows = own_kv[0].shape[0]
    half = rows // 2
    blocks = half // half_rows
    wide, deep = 512, 256

    def kernel(sel_ref, key_ref, query_ref, q_ref, *refs):
        own, other = refs[:groups], refs[groups : 2 * groups]
        refs = refs[2 * groups :]
        local = 2 * half_rows
        parts = [refs[0], refs[1]] + [
            refs[2 + j].at[pl.ds(k * local, local), :] for j in range(TP // 2 - 1) for k in range(2)
        ]
        refs = refs[1 + TP // 2 :]
        att_ref, lse_ref, dq_ref, keep_ref, pass_ref, gb_ref = refs[:6]
        kv_ref, sum_ref, g_ref, rq_ref, rg_ref, delta_ref, pos_ref = refs[6:]
        for group in range(groups):
            kv_ref[0, group] = own[group][...]
            kv_ref[1, group] = other[group][...]
        sum_ref[...] = jnp.zeros_like(sum_ref)
        dq_ref[...] = jnp.zeros_like(dq_ref)
        zeros = jnp.zeros((rows, HEAD), bf16)
        for j in range(0, TP, 2):
            for side in range(2):
                at = pl.ds(side * half + j * half_rows, 2 * half_rows)
                pair = jnp.concatenate(
                    [parts[j + k][pl.ds(side * half_rows, half_rows), :] for k in range(2)], axis=0
                )
                g_ref[:, at] = pair[:, :OWN].T
                gb_ref[at, :] = pair[:, OWN:]
        for head in range(2):
            own_rows = pl.ds(head * HEAD, HEAD)
            rq_ref[head] = jnp.concatenate([q_ref[own_rows, :].T, zeros], axis=1)
            grad = g_ref[own_rows, :]
            rg_ref[head] = jnp.concatenate([zeros, grad.T], axis=1)
            delta_ref[pl.ds(head, 1), :] = jnp.sum(
                grad.astype(f32) * att_ref[own_rows, :], axis=0, keepdims=True
            )

        def one_group(group, unused):
            for head in range(2):
                which = sel_ref[head]
                own_rows = pl.ds(head * HEAD, HEAD)
                stat = pl.ds(head, 1)
                pos_ref[...] = key_positions(
                    key_ref, which * groups + group, 0, 2 * blocks, half_rows, 128
                )
                for k_start in range(0, rows, deep):
                    keys_at = pl.ds(k_start, deep)
                    k_side = k_start // half
                    block = kv_ref[which, group, keys_at, :]
                    turned_keys = block.T[:HEAD]
                    for start in range(k_side * half, rows, wide):
                        lanes = pl.ds(start, wide)
                        turned = q_ref[own_rows, lanes]
                        padded = jnp.concatenate([turned, jnp.zeros_like(turned)], axis=0)
                        scores = nn(block, padded)
                        if start // half == k_side:
                            places = query_positions(
                                query_ref, start // half_rows, wide, half_rows
                            )
                            at = jnp.concatenate([pos_ref[keys_at, :]] * (wide // 128), axis=1)
                            scores = jnp.where(at <= places, scores, far_below)
                        probs = jnp.exp(scores - lse_ref[stat, lanes])
                        grads = g_ref[own_rows, lanes]
                        padded = jnp.concatenate([jnp.zeros_like(grads), grads], axis=0)
                        grad_probs = nn(block, padded)
                        grad_scores = probs * (grad_probs - delta_ref[stat, lanes])
                        probs = probs.astype(bf16)
                        grad_scores = grad_scores.astype(bf16)
                        sum_ref[which, group, keys_at, :] += nn(
                            grad_scores, rq_ref[head, lanes, :]
                        ) + nn(probs, rg_ref[head, lanes, :])
                        dq_ref[own_rows, lanes] += nn(turned_keys, grad_scores)
            return unused

        lax.fori_loop(0, groups, one_group, 0)
        for group in range(groups):
            keep_ref[pl.ds(group * rows, rows), :] = sum_ref[0, group]
            pass_ref[pl.ds(group * rows, rows), :] = sum_ref[1, group].astype(bf16)

    return call(
        kernel,
        [
            shape((OWN, rows), f32),
            shape((groups * rows, OWN), f32),
            shape((groups * rows, OWN), bf16),
            shape((rows, OWN), bf16),
        ],
        [
            select,
            key_base,
            query_base,
            turned_query,
            *own_kv,
            *other_kv,
            *traded,
            attended,
            log_mass,
        ],
        scalars=3,
        scratch=[
            pltpu.VMEM((2, groups, rows, OWN), bf16),
            pltpu.VMEM((2, groups, rows, OWN), f32),
            pltpu.VMEM((OWN, rows), bf16),
            pltpu.VMEM((2, rows, OWN), bf16),
            pltpu.VMEM((2, rows, OWN), bf16),
            pltpu.VMEM((2, rows), f32),
            pltpu.VMEM((rows, 128), i32),
        ],
        limit=40,
        cost=18.0,
    )


def store_blocks(part, tile, per, half_rows, keep_ref, pass_ref):
    side = (tile * per) // TP
    first = lax.rem(tile * per, TP) // 2
    for j in range(per):
        piece = part[j * half_rows : (j + 1) * half_rows]
        row = (2 * (first + j // 2) + side) * half_rows
        at = pl.ds(pl.multiple_of(row, half_rows), half_rows)
        target = keep_ref if j % 2 == 0 else pass_ref
        target[at, pl.ds(0, piece.shape[1])] = piece.astype(target.dtype)


def feed_forward(at, inputs, attended, sides, packs, gains, nz):
    rows, width = inputs.shape
    local = rows // TP
    half_rows = local // 2
    half = rows // 2
    d_rows, lanes = packs[0].shape[0] // 2, packs[0].shape[1]
    ff = lanes // 3
    part_rows = ff // nz
    per = 4
    tile_rows = per * half_rows

    def kernel(at_ref, x_ref, *refs):
        att, refs = refs[:TP], refs[TP:]
        cot_even, wo_even, odd, pack_near, pack_far = refs[:5]
        refs = refs[5:]
        gain_ref, refs = refs[0], refs[1:]
        att_out, wo_out, resid_out, gk_ref, gp_ref, lk_ref, lp_ref, gain_out, own_ref = refs[:9]
        send_ref, refs = refs[9], refs[10:]
        gu_w, dn_w, cot_ref, acc_gu, acc_dn, hold, blocks = refs
        tp = at_ref[0]
        z = at_ref[1]
        for j in range(TP):
            columns = pl.ds(pl.multiple_of((tp ^ j) * OWN, OWN), OWN)
            from_wo, row = (odd, local * TP // 2) if j % 2 else (wo_even, 0)
            row += OWN * (2 * (j // 2 % 2) + j // 4)
            wo_out[columns, :] = from_wo[pl.ds(row, OWN), pl.ds(0, width)]
            from_cot = odd if j % 2 else cot_even
            for side in range(2):
                for k in range(TP):
                    att_out[pl.ds(side * half + k * half_rows, half_rows), columns] = att[j][
                        pl.ds(side * half + (k ^ j) * half_rows, half_rows), :
                    ]
                cot_ref[pl.ds(side * half + j * half_rows, half_rows), :] = from_cot[
                    pl.ds(local * (j // 2) + side * half_rows, half_rows), pl.ds(0, width)
                ]
        for s in range(nz):
            hold[z ^ s] = (pack_far if s % 2 else pack_near)[pl.ds(d_rows * (s // 2), d_rows), :]
        for s in range(nz):
            rows_at = pl.ds(s * d_rows, d_rows)
            gu_w[rows_at, :] = hold[s, :, pl.ds(0, 2 * ff)]
            dn_w[rows_at, :] = jnp.concatenate(
                [
                    hold[b][:, 2 * ff + s * part_rows : 2 * ff + (s + 1) * part_rows]
                    for b in range(nz)
                ],
                axis=1,
            )
        gain = gain_ref[pl.ds(1, 1), :]
        gain_out[...] = jnp.zeros_like(gain_out)
        acc_gu[...] = jnp.zeros_like(acc_gu)
        acc_dn[...] = jnp.zeros_like(acc_dn)

        def one_tile(tile, unused):
            at_rows = pl.ds(pl.multiple_of(tile * tile_rows, tile_rows), tile_rows)
            branch = nt(att_out[at_rows, :][:, :width], wo_out[pl.ds(0, width), :])
            resid = x_ref[at_rows, :].astype(f32) + branch
            side = (tile * per) // TP

            @pl.when(lax.rem(tile * per, TP) == 0)
            def keep_own():
                resid_out[pl.ds(pl.multiple_of(side * half_rows, half_rows), half_rows), :] = resid[
                    :half_rows
                ]

            normal = resid * norm_scale(resid)
            hidden = (normal * gain).astype(bf16)
            gate_up = nn(hidden, gu_w[...])
            gate, up = gate_up[:, :ff], gate_up[:, ff:]
            sigmoid = 1.0 / (1.0 + jnp.exp(-gate))
            activated = gate * sigmoid
            product = (activated * up).astype(bf16)
            cotangent = cot_ref[at_rows, :]
            grad_product = nn(cotangent, dn_w[...])
            grad_gate = grad_product * up * sigmoid * (1.0 + gate * (1.0 - sigmoid))
            grad_gu = jnp.concatenate([grad_gate, grad_product * activated], axis=1).astype(bf16)
            partial = nt(grad_gu, gu_w[...])
            gain_out[pl.ds(0, 1), :] += jnp.sum(partial * normal, axis=0, keepdims=True)
            store_blocks(partial, tile, per, half_rows, gk_ref, gp_ref)
            store_blocks(nt(product, dn_w[...]), tile, per, half_rows, lk_ref, lp_ref)
            acc_gu[...] += tn(hidden, grad_gu)
            acc_dn[...] += tn(cotangent, product)
            return unused

        lax.fori_loop(0, 2 * TP // per, one_tile, 0)
        for b in range(nz):
            blocks[b, :, pl.ds(0, 2 * ff)] = acc_gu[pl.ds(b * d_rows, d_rows), :]
            blocks[b, :, pl.ds(2 * ff, ff)] = jnp.concatenate(
                [
                    acc_dn[pl.ds(s * d_rows, d_rows), :][:, b * part_rows : (b + 1) * part_rows]
                    for s in range(nz)
                ],
                axis=1,
            )
        for s in range(nz):
            target = send_ref if s % 2 else own_ref
            target[pl.ds(d_rows * (s // 2), d_rows), :] = blocks[z ^ s].astype(target.dtype)

    keep = shape((TP // 2 * local, width), f32)
    passed = shape((TP // 2 * local, TP * OWN), bf16)
    return call(
        kernel,
        [
            shape((rows, TP * OWN), bf16),
            shape((TP * OWN, width), bf16),
            shape((local, width), f32),
            keep,
            passed,
            keep,
            passed,
            shape((8, width), f32),
            shape((2 * d_rows, lanes), f32),
            shape((2 * d_rows, lanes), bf16),
        ],
        [at, inputs, *attended, *sides, *packs, gains],
        scratch=[
            pltpu.VMEM((width, 2 * ff), bf16),
            pltpu.VMEM((width, ff), bf16),
            pltpu.VMEM((rows, width), bf16),
            pltpu.VMEM((width, 2 * ff), f32),
            pltpu.VMEM((width, ff), f32),
            pltpu.VMEM((nz, d_rows, lanes), bf16),
            pltpu.VMEM((nz, d_rows, lanes), f32),
        ],
        limit=48,
        cost=18.0,
    )


def add_crossed(keep, crossed, count):
    local, width = keep.shape[0] // count, keep.shape[1]

    def kernel(keep_ref, cross_ref, own_ref, *sends):
        for j in range(count):
            at = pl.ds(j * local, local)
            target = own_ref if j == 0 else sends[j - 1]
            target[...] = (
                keep_ref[at, :] + cross_ref[at, pl.ds(0, width)].astype(f32)
            ).astype(target.dtype)

    return call(
        kernel,
        [shape((local, width), f32)] + [shape((local, width), bf16)] * (count - 1),
        [keep, crossed],
        scalars=0,
        limit=12,
        cost=1.0,
    )


def branch_gradient(at, sums, resid, cotangent, w_out, gains):
    local, width = resid.shape

    def kernel(at_ref, *refs):
        parts, refs = refs[: len(sums)], refs[len(sums) :]
        resid_ref, cot_ref, wo_ref, gain_ref, grad_ref, keep_ref, pass_ref, ga_ref, gb_ref = refs
        tp = at_ref[0]
        grad_hidden = parts[0][...]
        for part in parts[1:]:
            grad_hidden = grad_hidden + part[...].astype(f32)
        resid = resid_ref[...]
        scale = norm_scale(resid)
        normal = resid * scale
        grad = grad_hidden * gain_ref[pl.ds(1, 1), :]
        grad = scale * (grad - normal * jnp.mean(grad * normal, axis=1, keepdims=True))
        grad = grad + cot_ref[...].astype(f32)
        grad_ref[...] = grad
        low = grad.astype(bf16)
        gb_ref[...] = jnp.zeros_like(gb_ref)
        gb_ref[:, pl.ds(0, width)] = low
        ga_ref[...] = jnp.zeros_like(ga_ref)
        ga_ref[:, pl.ds(0, width)] = nn(low, wo_ref[pl.ds(0, width), :]).astype(bf16)
        for j in range(TP):
            columns = pl.ds(pl.multiple_of((tp ^ j) * OWN, OWN), OWN)
            target = keep_ref if j % 2 == 0 else pass_ref
            rows = pl.ds((j // 2) * local, local)
            target[rows, pl.ds(0, OWN)] = ga_ref[:, columns]
            target[rows, pl.ds(OWN, OWN)] = gb_ref[:, columns]

    blocks = shape((TP // 2 * local, 2 * OWN), bf16)
    return call(
        kernel,
        [shape((local, width), f32), blocks, blocks],
        [at, *sums, resid, cotangent, w_out, gains],
        scratch=[pltpu.VMEM((local, TP * OWN), bf16), pltpu.VMEM((local, TP * OWN), bf16)],
        limit=16,
        cost=3.0,
    )


def pair_up(keep, crossed, count):
    local, width = keep.shape[0] // count, keep.shape[1]

    def kernel(keep_ref, cross_ref, *outs):
        for j in range(1, count):
            at = pl.ds(j * local, local)
            outs[j - 1][pl.ds(0, local), :] = keep_ref[at, :]
            outs[j - 1][pl.ds(local, local), :] = cross_ref[at, :]

    return call(
        kernel,
        [shape((2 * local, width), bf16)] * (count - 1),
        [keep, crossed],
        scalars=0,
        limit=8,
        cost=0.7,
    )


def projection_gradient(
    at, grad_query, grad_kv, inputs, hidden, w_qkv, gain_sums, cosine, sine, grad_out, nz
):
    rows, width = inputs.shape
    local = rows // TP
    half_rows = local // 2
    d_rows = width // nz
    per = 4
    tile_rows = per * half_rows
    pieces = len(grad_kv)

    def kernel(at_ref, dq_ref, *refs):
        kvs, refs = refs[:pieces], refs[pieces:]
        x_ref, hid_ref, w_ref, gain_two_ref, cos_ref, sin_ref, wo_ref = refs[:7]
        keep_ref, pass_ref, own_ref = refs[7:10]
        sends, refs = refs[10 : 10 + nz - 1], refs[10 + nz - 1 :]
        turn_ref, acc_ref, gain_acc, hold = refs
        z = at_ref[1]
        turn_ref[...] = dq_ref[...].T * HEAD**-0.5
        acc_ref[...] = jnp.zeros_like(acc_ref)
        gain_acc[...] = jnp.zeros_like(gain_acc)

        def one_tile(tile, unused):
            at_rows = pl.ds(pl.multiple_of(tile * tile_rows, tile_rows), tile_rows)
            cos, sin = cos_ref[at_rows, :], sin_ref[at_rows, :]
            query = turn_ref[at_rows, :]
            query = query * cos - swap_halves(query) * sin
            pair = kvs[0][at_rows, :].astype(f32)
            for piece in kvs[1:]:
                pair = pair + piece[at_rows, :].astype(f32)
            turned = pair * cos - swap_halves(pair) * sin
            lane = lax.broadcasted_iota(i32, pair.shape, 1)
            pair = jnp.where(lane < HEAD, turned, pair)
            grad = jnp.concatenate([query, pair], axis=1).astype(bf16)
            partial = nt(grad, w_ref[...])
            x = x_ref[at_rows, :].astype(f32)
            gain_acc[pl.ds(0, 1), :] += jnp.sum(partial * (x * norm_scale(x)), axis=0, keepdims=True)
            store_blocks(partial, tile, per, half_rows, keep_ref, pass_ref)
            acc_ref[...] += tn(hid_ref[at_rows, :], grad)
            return unused

        lax.fori_loop(0, 2 * TP // per, one_tile, 0)
        hold[...] = jnp.zeros_like(hold)
        for s in range(nz):
            columns = slice(s * d_rows, (s + 1) * d_rows)
            hold[s, pl.ds(0, 1), pl.ds(0, d_rows)] = gain_acc[pl.ds(0, 1), :][:, columns]
            hold[s, pl.ds(1, 1), pl.ds(0, d_rows)] = gain_two_ref[pl.ds(0, 1), :][:, columns]
        for s in range(nz):
            block = z ^ s
            target = own_ref if s == 0 else sends[s - 1]
            rows_at = pl.ds(pl.multiple_of(block * d_rows, 8), d_rows)
            part = pl.ds(0, d_rows)
            target[part, pl.ds(0, 2 * OWN)] = acc_ref[rows_at, :].astype(target.dtype)
            target[part, pl.ds(2 * OWN, OWN)] = wo_ref[rows_at, :].astype(target.dtype)
            target[pl.ds(d_rows, 16), :] = hold[block].astype(target.dtype)

    return call(
        kernel,
        [
            shape((TP // 2 * local, width), f32),
            shape((TP // 2 * local, TP * OWN), bf16),
            shape((d_rows + 16, 3 * OWN), f32),
        ]
        + [shape((d_rows + 16, 3 * OWN), bf16)] * (nz - 1),
        [at, grad_query, *grad_kv, inputs, hidden, w_qkv, gain_sums, cosine, sine, grad_out],
        scratch=[
            pltpu.VMEM((rows, OWN), f32),
            pltpu.VMEM((width, 2 * OWN), f32),
            pltpu.VMEM((8, width), f32),
            pltpu.VMEM((nz, 16, 3 * OWN), f32),
        ],
        limit=32,
        cost=8.0,
    )


def token_gradient(sums, tokens, grad_resid, gains):
    local, width = tokens.shape

    def kernel(*refs):
        parts, refs = refs[: len(sums)], refs[len(sums) :]
        x_ref, grad_ref, gain_ref, out_ref = refs
        grad_hidden = parts[0][...]
        for part in parts[1:]:
            grad_hidden = grad_hidden + part[...].astype(f32)
        x = x_ref[...].astype(f32)
        scale = norm_scale(x)
        normal = x * scale
        grad = grad_hidden * gain_ref[pl.ds(0, 1), :]
        grad = scale * (grad - normal * jnp.mean(grad * normal, axis=1, keepdims=True))
        out_ref[...] = (grad + grad_ref[...]).T

    return call(
        kernel,
        [shape((width, local), f32)],
        [*sums, tokens, grad_resid, gains],
        scalars=0,
        limit=8,
        cost=1.0,
    )[0].T


def layer_output(sums, resid):
    def kernel(*refs):
        parts, (resid_ref, out_ref) = refs[: len(sums)], refs[len(sums) :]
        total = resid_ref[...]
        for part in parts:
            total = total + part[...].astype(f32)
        out_ref[...] = total.T.astype(bf16)

    turned = shape(resid.shape[::-1], bf16)
    return call(kernel, [turned], [*sums, resid], scalars=0, limit=8, cost=1.0)[0].T


def split_rows(rows):
    first = (rows // 2 + 15) // 16 * 16
    return first, rows - first


def first_sum(keep, arrived):
    rows, lanes = keep.shape[0] // 2, keep.shape[1]

    def kernel(keep_ref, in_ref, own_ref, send_ref):
        for ref, start in ((own_ref, 0), (send_ref, rows)):
            at = pl.ds(start, rows)
            ref[...] = (keep_ref[at, :] + in_ref[at, :].astype(f32)).astype(ref.dtype)

    return call(
        kernel,
        [shape((rows, lanes), f32), shape((rows, lanes), bf16)],
        [keep, arrived],
        scalars=0,
        limit=8,
        cost=1.0,
    )


def last_sum(own, arrived):
    rows, lanes = own.shape
    first, second = split_rows(rows)

    def kernel(own_ref, in_ref, a_ref, b_ref):
        for ref, start, count in ((a_ref, 0, first), (b_ref, first, second)):
            at = pl.ds(start, count)
            ref[:, pl.ds(0, lanes)] = (own_ref[at, :] + in_ref[at, :].astype(f32)).astype(bf16)

    return call(
        kernel,
        [shape((first, TP * OWN), bf16), shape((second, TP * OWN), bf16)],
        [own, arrived],
        scalars=0,
        limit=8,
        cost=1.0,
    )


def ff_outputs(at, even_a, even_b, odd, d_rows, ff_z, nz):
    part = ff_z // TP
    ff = part * nz
    first, second = split_rows(d_rows)

    def kernel(at_ref, a_ref, b_ref, odd_ref, gate_ref, up_ref, down_ref, hold):
        tp = at_ref[0]
        for j in range(TP):
            from_a, from_b = (odd_ref, odd_ref) if j % 2 else (a_ref, b_ref)
            row_b = (first * TP // 2 if j % 2 else 0) + second * (2 * (j // 2 % 2) + j // 4)
            hold[tp ^ j, pl.ds(0, first), :] = from_a[pl.ds(first * (j // 2), first), pl.ds(0, 3 * ff)]
            hold[tp ^ j, pl.ds(first, second), :] = from_b[pl.ds(row_b, second), pl.ds(0, 3 * ff)]
        for s in range(nz):
            for start in (s * part, ff + s * part, 2 * ff + s * part):
                block = jnp.concatenate(
                    [hold[c][:, start : start + part] for c in range(TP)], axis=1
                ).astype(f32)
                if start < ff:
                    gate_ref[:, pl.ds(s * ff_z, ff_z)] = block
                elif start < 2 * ff:
                    up_ref[:, pl.ds(s * ff_z, ff_z)] = block
                else:
                    down_ref[pl.ds(s * d_rows, d_rows), :] = block

    gate, up, down = call(
        kernel,
        [
            shape((d_rows, nz * ff_z), f32),
            shape((d_rows, nz * ff_z), f32),
            shape((nz * d_rows, ff_z), f32),
        ],
        [at, even_a, even_b, odd],
        scratch=[pltpu.VMEM((TP, d_rows, 3 * ff), bf16)],
        limit=32,
        cost=7.0,
    )
    return gate, up, down.T


def projection_outputs(at, slots, width):
    d_rows = slots[0].shape[0] - 16

    def kernel(at_ref, *refs):
        parts, (q_ref, k_ref, v_ref, o_ref, one_ref, two_ref, hold) = refs[:TP], refs[TP:]
        tp = at_ref[0]
        total = jnp.zeros((16, 3 * OWN), f32)
        for j in range(TP):
            hold[tp ^ j] = parts[j][...].astype(f32)
            total = total + parts[j][pl.ds(d_rows, 16), :].astype(f32)
        one_ref[...] = total[0:1, :d_rows]
        two_ref[...] = total[1:2, :d_rows]
        heads = [hold[c][:d_rows, :OWN] for c in range(TP)]
        q_ref[...] = jnp.concatenate(heads, axis=1)[:, :width]
        heads = [hold[c][:d_rows, 2 * OWN :] for c in range(TP)]
        o_ref[...] = jnp.concatenate(heads, axis=1)[:, :width]
        kv = [hold[c][:d_rows, OWN : 2 * OWN] for c in range(TP)]
        kv = [kv[0], kv[1] + kv[2], kv[3] + kv[4], kv[5], kv[6]]
        for c in range(KV_HEADS):
            turned = kv[c].T
            k_ref[pl.ds(c * HEAD, HEAD), :] = turned[:HEAD]
            v_ref[pl.ds(c * HEAD, HEAD), :] = turned[HEAD:]

    query, key, value, out, one, two = call(
        kernel,
        [
            shape((d_rows, width), f32),
            shape((KV_HEADS * HEAD, d_rows), f32),
            shape((KV_HEADS * HEAD, d_rows), f32),
            shape((d_rows, width), f32),
            shape((1, d_rows), f32),
            shape((1, d_rows), f32),
        ],
        [at, *slots],
        scratch=[pltpu.VMEM((TP, d_rows + 16, 3 * OWN), f32)],
        limit=12,
        cost=2.0,
    )
    return query, key.T, value.T, out, one, two


def body(
    tokens,
    pair_order,
    gain_attn,
    gain_mlp,
    w_query,
    w_key,
    w_value,
    w_out,
    w_gate,
    w_up,
    w_down,
    cotangent,
):
    local_rows, width = tokens.shape
    half_rows = local_rows // 2
    nz = lax.axis_size("fsdp")
    outer = lax.axis_size("ctx") // TP
    count = lax.axis_size(AXES)
    groups = outer * nz
    me = lax.axis_index(AXES)
    z = lax.axis_index("fsdp")
    tp = lax.axis_index("ctx") % TP
    kv_index = (4 * (tp // 2)) // GROUP + tp % 2
    at = jnp.stack([tp, z, kv_index]).astype(i32)
    send = functools.partial(exchange, count=count)
    group_mask = [(g // nz) * TP * nz + g % nz for g in range(groups)]

    def after(value, *others):
        return lax.optimization_barrier((value, *others))[0]

    def both(left, right):
        return jnp.concatenate([left, right], axis=0)

    def plane_gather(block):
        even = [block] + [send(block, j * nz) for j in range(2, TP, 2)]
        odd = [send(e, nz) for e in even]
        return [piece for pair in zip(even, odd) for piece in pair]

    def plane_scatter(keep, passed):
        first, *rest = add_crossed(keep, send(passed, nz), TP // 2)
        return [first] + [send(piece, 2 * (j + 1) * nz) for j, piece in enumerate(rest)]

    def from_z(block):
        return [block] + [send(block, s) for s in range(1, nz)]

    pack_one = slice_attention_weights(at, w_query, w_key, w_value, w_out, gain_attn, gain_mlp)
    token_slots = plane_gather(tokens)
    pack_one = from_z(pack_one)

    slot_of = jnp.array([[m | (j * nz) for j in range(TP)] for m in group_mask], dtype=i32)
    low = pair_order[me ^ slot_of]
    base = jnp.stack([low, 2 * count - 1 - low], axis=1) * half_rows
    query_base = base[0].reshape(2 * TP)
    partner = jnp.array([j ^ 1 for j in range(TP)], dtype=i32)
    key_base = jnp.stack([base, base[:, :, partner]]).reshape(2 * groups, 2 * TP)
    places = (query_base[:, None] + jnp.arange(half_rows, dtype=i32)[None, :]).reshape(-1)
    lane = jnp.arange(OWN)
    freqs = base_theta ** (-2.0 * (lane % (HEAD // 2)).astype(f32) / HEAD)
    angles = places.astype(f32)[:, None] * freqs[None, :]
    cosine = jnp.cos(angles)
    sine = jnp.sin(angles) * jnp.where(lane % HEAD < HEAD // 2, -1.0, 1.0)[None, :]
    select = jnp.where((2 * tp + jnp.arange(2)) // GROUP == kv_index, 0, 1).astype(i32)

    inputs, hidden_one, turned_query, kv, w_qkv, cot_own, w_out_own, gains = project(
        at, token_slots, pack_one, cosine, sine, cotangent
    )
    own_kv = [kv] + [send(kv, m) for m in group_mask[1:]]
    other_kv = [send(slot, nz) for slot in own_kv]
    pack_two = slice_ff_weights(after(at, kv), w_gate, w_up, w_down, nz)
    mask_x, mask_y = 2 * nz, 4 * nz
    cot_even = both(cot_own, send(cot_own, mask_x))
    w_out_even = both(w_out_own, send(w_out_own, mask_y))
    attended, attended_own, log_mass = attention_forward(
        after(select, cot_even, w_out_even),
        key_base,
        query_base,
        turned_query,
        own_kv,
        other_kv,
        half_rows,
    )
    cot_even = both(cot_even, send(cot_even, mask_y))
    w_out_even = both(w_out_even, send(w_out_even, mask_x))
    pack_two = after(pack_two, *own_kv)
    pack_near = both(pack_two, send(pack_two, 2))
    attended_own = after(attended_own, cot_even, w_out_even, pack_near)
    pack_far = send(pack_near, 1)
    side_odd = send(both(cot_even, w_out_even), nz)
    attended_slots = plane_gather(attended_own)

    (
        attended_low,
        w_out_all,
        resid,
        grad_keep,
        grad_pass,
        out_keep,
        out_pass,
        gain_sums,
        ff_keep,
        ff_send,
    ) = feed_forward(
        at,
        inputs,
        attended_slots,
        [cot_even, w_out_even, side_odd],
        [pack_near, pack_far],
        gains,
        nz,
    )
    sums = plane_scatter(grad_keep, grad_pass)
    ff_own, ff_send = first_sum(ff_keep, send(ff_send, 1))
    out_first, *out_rest = add_crossed(
        out_keep, send(after(out_pass, sums[0]), nz), TP // 2
    )
    grad_resid, trade_keep, trade_pass = branch_gradient(
        at, sums, resid, cotangent, w_out_all, gains
    )
    crossed = send(after(trade_pass, ff_own), nz)
    pairs = [
        send(pair, 2 * (j + 1) * nz)
        for j, pair in enumerate(pair_up(trade_keep, crossed, TP // 2))
    ]
    ff_arrived = send(ff_send, 2)
    out_sums = [out_first] + [
        send(after(piece, pairs[0]), 2 * (j + 1) * nz) for j, piece in enumerate(out_rest)
    ]

    grad_query, kv_keep, kv_pass, branch_columns = attention_backward(
        after(select, out_first),
        key_base,
        query_base,
        turned_query,
        own_kv,
        other_kv,
        [trade_keep, crossed, *pairs],
        attended,
        log_mass,
        half_rows,
    )
    kv_crossed = send(after(kv_pass, *out_sums), nz)
    ff_a, ff_b = last_sum(ff_own, ff_arrived)
    first, *rest = add_crossed(kv_keep, after(kv_crossed, ff_a), groups)
    grad_kv = [first] + [send(piece, m) for piece, m in zip(rest, group_mask[1:])]

    for step in range(outer.bit_length() - 1):
        far = TP * nz << step
        ff_a, ff_b = (
            (part.astype(f32) + send(part, far).astype(f32)).astype(bf16) for part in (ff_a, ff_b)
        )
    ff_a, ff_b = after(ff_a, rest[0]), after(ff_b, rest[0])
    layer_out = layer_output(out_sums, after(resid, rest[0]))
    ff_even_a = both(ff_a, send(ff_a, mask_x))
    ff_even_b = both(ff_b, send(ff_b, mask_y))
    ff_even_a = both(ff_even_a, send(ff_even_a, mask_y))
    ff_even_b = both(ff_even_b, send(ff_even_b, mask_x))
    grad_out = tn(attended_low[:, :width], after(branch_columns, rest[0]))

    last_keep, last_pass, last_own, *last_sends = projection_gradient(
        at,
        grad_query,
        [after(first, ff_even_a, ff_even_b), *grad_kv[1:]],
        inputs,
        hidden_one,
        w_qkv,
        gain_sums,
        cosine,
        sine,
        grad_out,
        nz,
    )
    ff_odd = send(both(ff_even_a, ff_even_b), nz)
    sums = plane_scatter(last_keep, last_pass)
    last_total = last_own
    for s, piece in enumerate(last_sends):
        last_total = last_total + send(piece, s + 1).astype(f32)
    for step in range(outer.bit_length() - 1):
        last_total = last_total + send(last_total.astype(bf16), TP * nz << step).astype(f32)
    last_slots = plane_gather(last_total.astype(bf16))
    grad_gate, grad_up, grad_down = ff_outputs(
        at, ff_even_a, ff_even_b, ff_odd, w_gate.shape[0], w_down.shape[0], nz
    )
    grad_w_query, grad_w_key, grad_w_value, grad_out, gain_one, gain_two = projection_outputs(
        at, last_slots, width
    )
    grad_tokens = token_gradient(sums, tokens, grad_resid, gains)
    return (
        layer_out,
        grad_tokens,
        gain_one.reshape(-1),
        gain_two.reshape(-1),
        grad_w_query,
        grad_w_key,
        grad_w_value,
        grad_out,
        grad_gate,
        grad_up,
        grad_down,
    )


def solution(mesh):
    return jax.shard_map(
        body,
        mesh=mesh,
        in_specs=(
            P(("ctx", "fsdp"), None),
            P(),
            P("fsdp"),
            P("fsdp"),
            P("fsdp", None),
            P("fsdp", None),
            P("fsdp", None),
            P("fsdp", None),
            P("fsdp", None),
            P("fsdp", None),
            P("fsdp", None),
            P(("ctx", "fsdp"), None),
        ),
        out_specs=(
            P(("ctx", "fsdp"), None),
            P(("ctx", "fsdp"), None),
            P("fsdp"),
            P("fsdp"),
            P("fsdp", None),
            P("fsdp", None),
            P("fsdp", None),
            P("fsdp", None),
            P("fsdp", None),
            P("fsdp", None),
            P("fsdp", None),
        ),
        check_vma=False,
    )
```

profile of v0, /device:TPU:0, one launch (start us, length us, event | category | flops | bytes accessed | tf_op | source)
XLA Modules:
  0.0 320.0 jit_solution(380313385531185289)
XLA Ops:
  6.9 5.1 %collective-permute-start.9 = (bf16[256,384]{1,0:T(8,128)(2,1)S(1)}, bf16[256,384]{1,0:T(8,128)(2,1)S(1)}, u32[]{:S(2)}, u32[]{:S(2)}) collective-permute-start(bf16[256,384]{1,0:T(8,128)(2,1)S(1)} %shard_map.221.refs_8_), channel_id=1, source_target_pairs={{0,3},{1,2},{2,1},{3,0},{4,7},{5,6},{6,5},{7,4},{8,11},{9,10},{10,... | collective-permute-start | bytes 589832 | tf_op jit(solution)/shard_map/ppermute | solution.py:29
  12.1 2.5 collective-permute-start.5
  17.8 8.2 %collective-permute-start.7 = (bf16[256,384]{1,0:T(8,128)(2,1)S(1)}, bf16[256,384]{1,0:T(8,128)(2,1)S(1)}, u32[]{:S(2)}, u32[]{:S(2)}) collective-permute-start(bf16[256,384]{1,0:T(8,128)(2,1)S(1)} %shard_map.221.refs_8_), channel_id=1, source_target_pairs={{0,1},{1,0},{2,3},{3,2},{4,5},{5,4},{6,7},{7,6},{8,9},{9,8},{10,11... | collective-permute-start | bytes 589832 | tf_op jit(solution)/shard_map/ppermute | solution.py:29
  26.0 2.8 collective-permute-done.8.refs_10_
  29.8 1.9 fusion.2
  32.7 2.7 shard_map.222
  35.5 1.3 copy-done.13
  36.8 1.3 copy-done.15
  38.1 1.5 collective-permute-start.10
  40.5 5.7 %collective-permute-done.10 = bf16[128,1024]{1,0:T(8,128)(2,1)S(1)} collective-permute-done((bf16[128,1024]{1,0:T(8,128)(2,1)S(1)}, bf16[128,1024]{1,0:T(8,128)(2,1)S(1)}, u32[]{:S(2)}, u32[]{:S(2)}) %collective-permute-start.10) | collective-permute-done | bytes 262176 | tf_op jit(solution)/shard_map/ppermute | solution.py:29
  47.0 2.2 collective-permute-start.19
  49.3 2.5 collective-permute-start.14
  51.8 1.9 collective-permute-start.12
  54.6 1.3 copy-done.2
  55.9 1.3 copy-done.3
  57.2 1.3 copy-done.4
  58.5 1.9 shard_map.224
  60.5 12.1 %collective-permute-done.13.refs_2_ = bf16[1024,128]{1,0:T(8,128)(2,1)S(1)} collective-permute-done((bf16[1024,128]{1,0:T(8,128)(2,1)S(1)}, bf16[1024,128]{1,0:T(8,128)(2,1)S(1)}, u32[]{:S(2)}, u32[]{:S(2)}) %collective-permute-start.13) | collective-permute-done | bytes 262176 | tf_op jit(solution)/shard_map/ppermute | solution.py:29
  72.6 2.0 constant_dynamic-update-slice_fusion.15
  77.4 1.4 collective-permute-start.20
  80.4 15.0 %collective-permute-done.21 = bf16[240,960]{1,0:T(8,128)(2,1)} collective-permute-done((bf16[240,960]{1,0:T(8,128)(2,1)S(1)}, bf16[240,960]{1,0:T(8,128)(2,1)}, u32[]{:S(2)}, u32[]{:S(2)}) %collective-permute-start.21) | collective-permute-done | bytes 460832 | tf_op jit(solution)/shard_map/ppermute | solution.py:29
  96.5 2.2 constant_dynamic-update-slice_fusion.12
  100.2 12.7 %shard_map.223 = (f32[128,1024]{1,0:T(8,128)S(1)}, bf16[1024,128]{1,0:T(8,128)(2,1)S(1)}, f32[2,1024]{1,0:T(2,128)S(1)}) custom-call(s32[2]{0:T(128)S(1)} %compare_select_fusion.1.sel_ref, s32[8,16]{1,0:T(8,128)S(1)} %reshape.107.key_ref, s32[16]{0:T(128)S(1)} %add.85.query_ref, bf16[128,1024]{1,0:T(8,128)(2,1)S(1)} %copy-done.20, ...), custom_call_target="tpu_custom_call" | custom-call | flops 14000000000 | bytes 14000000 | tf_op jit(solution)/shard_map/pallas_call | solution.py:52
  112.9 2.0 collective-permute-start.27
  116.4 6.6 %collective-permute-done.27.refs_6_ = bf16[1024,128]{1,0:T(8,128)(2,1)S(1)} collective-permute-done((bf16[1024,128]{1,0:T(8,128)(2,1)S(1)}, bf16[1024,128]{1,0:T(8,128)(2,1)S(1)}, u32[]{:S(2)}, u32[]{:S(2)}) %collective-permute-start.27) | collective-permute-done | bytes 262176 | tf_op jit(solution)/shard_map/ppermute | solution.py:29
  123.0 4.6 %collective-permute-done.25.refs_4_ = bf16[1024,128]{1,0:T(8,128)(2,1)S(1)} collective-permute-done((bf16[1024,128]{1,0:T(8,128)(2,1)S(1)}, bf16[1024,128]{1,0:T(8,128)(2,1)S(1)}, u32[]{:S(2)}, u32[]{:S(2)}) %collective-permute-start.25) | collective-permute-done | bytes 262176 | tf_op jit(solution)/shard_map/ppermute | solution.py:29
  130.0 1.3 copy-done.30
  131.3 21.8 %shard_map.225 = (bf16[1024,1024]{1,0:T(8,128)(2,1)}, bf16[1024,960]{1,0:T(8,128)(2,1)}, f32[128,960]{1,0:T(8,128)S(1)}, f32[512,960]{1,0:T(8,128)}, bf16[512,10...) custom-call(s32[3]{0:T(128)S(1)} %pad_add_fusion.1.at_ref, ...), custom_call_target="tpu_custom_call" | custom-call | flops 17999998976 | bytes 18000000 | tf_op jit(solution)/shard_map/pallas_call | solution.py:52
  153.2 2.0 collective-permute-start.36
  156.0 1.6 copy-done.10
  160.0 1.2 collective-permute-start.34
  162.4 15.1 %collective-permute-done.36.in_ref = bf16[480,960]{1,0:T(8,128)(2,1)S(1)} collective-permute-done((bf16[480,960]{1,0:T(8,128)(2,1)S(1)}, bf16[480,960]{1,0:T(8,128)(2,1)S(1)}, u32[]{:S(2)}, u32[]{:S(2)}) %collective-permute-start.36) | collective-permute-done | bytes 921632 | tf_op jit(solution)/shard_map/ppermute | solution.py:29
  177.8 1.5 shard_map.228
  179.3 1.5 collective-permute-done.37.cross_ref.refs_9_
  184.6 2.6 collective-permute-done.38.refs_10_
  187.3 1.7 collective-permute-start.41
  190.8 2.1 collective-permute-done.42.refs_11_
  192.9 17.5 %shard_map.231 = (f32[128,1024]{1,0:T(8,128)S(1)}, f32[4096,128]{1,0:T(8,128)S(1)}, bf16[4096,128]{1,0:T(8,128)(2,1)S(1)}, bf16[1024,128]{1,0:T(8,128)(2,1)S(1)}) custom-call(s32[2]{0:T(128)S(1)} %compare_select_fusion.1.sel_ref, s32[8,16]{1,0:T(8,128)S(1)} %reshape.107.key_ref, s32[16]{0:T(128)S(1)} %add.85.query_ref, bf16[128,1024]{1,0:T(8,128)(2,1)S(1)} %copy-done.21, ...), custom_call_target="tpu_custom_call" | custom-call | flops 17999998976 | bytes 18000000 | tf_op jit(solution)/shard_map/pallas_call | solution.py:52
  210.5 1.7 collective-permute-start.45
  212.2 23.4 %collective-permute-done.45.in_ref = bf16[240,960]{1,0:T(8,128)(2,1)S(1)} collective-permute-done((bf16[240,960]{1,0:T(8,128)(2,1)S(1)}, bf16[240,960]{1,0:T(8,128)(2,1)S(1)}, u32[]{:S(2)}, u32[]{:S(2)}) %collective-permute-start.45) | collective-permute-done | bytes 460832 | tf_op jit(solution)/shard_map/ppermute | solution.py:29
  236.0 1.4 collective-permute-start.46
  237.4 3.0 collective-permute-start.48
  240.4 2.0 collective-permute-start.51
  242.4 2.4 collective-permute-start.52
  244.9 2.1 collective-permute-start.47
  247.8 1.4 collective-permute-start.49
  249.3 8.6 %collective-permute-done.47 = bf16[256,1024]{1,0:T(8,128)(2,1)S(1)} collective-permute-done((bf16[256,1024]{1,0:T(8,128)(2,1)S(1)}, bf16[256,1024]{1,0:T(8,128)(2,1)S(1)}, u32[]{:S(2)}, u32[]{:S(2)}) %collective-permute-start.47) | collective-permute-done | bytes 524320 | tf_op jit(solution)/shard_map/ppermute | solution.py:29
  258.9 2.5 collective-permute-done.51.refs_2_
  261.5 3.7 %shard_map.235 = (f32[512,960]{1,0:T(8,128)S(1)}, bf16[512,1024]{1,0:T(8,128)(2,1)S(1)}, f32[256,384]{1,0:T(8,128)S(1)}, bf16[256,384]{1,0:T(8,128)(2,1)S(1)}, b...) custom-call(s32[3]{0:T(128)S(1)} %pad_add_fusion.1.at_ref, f32[128,1024]{1,0:T(8,128)S(1)} %get-tuple-element.143.dq_ref, ...), custom_call_target="tpu_custom_call" | custom-call | flops 8000000000 | bytes 8000000 | tf_op jit(solution)/shard_map/pallas_call | solution.py:52
  265.3 4.7 %collective-permute-start.57 = (bf16[256,384]{1,0:T(8,128)(2,1)S(1)}, bf16[256,384]{1,0:T(8,128)(2,1)S(1)}, u32[]{:S(2)}, u32[]{:S(2)}) collective-permute-start(bf16[256,384]{1,0:T(8,128)(2,1)S(1)} %get-tuple-element.165), channel_id=1, source_target_pairs={{0,1},{1,0},{2,3},{3,2},{4,5},{5,4},{6,7},{7,6},{8,9},{9,8},{10,11... | collective-permute-start | bytes 589832 | tf_op jit(solution)/shard_map/ppermute | solution.py:29
  270.1 2.3 collective-permute-start.59
  272.4 6.2 %collective-permute-done.57 = bf16[256,384]{1,0:T(8,128)(2,1)S(1)} collective-permute-done((bf16[256,384]{1,0:T(8,128)(2,1)S(1)}, bf16[256,384]{1,0:T(8,128)(2,1)S(1)}, u32[]{:S(2)}, u32[]{:S(2)}) %collective-permute-start.57) | collective-permute-done | bytes 196640 | tf_op jit(solution)/shard_map/ppermute | solution.py:29
  278.6 8.5 %collective-permute-done.58 = bf16[256,384]{1,0:T(8,128)(2,1)S(1)} collective-permute-done((bf16[256,384]{1,0:T(8,128)(2,1)S(1)}, bf16[256,384]{1,0:T(8,128)(2,1)S(1)}, u32[]{:S(2)}, u32[]{:S(2)}) %collective-permute-start.58) | collective-permute-done | bytes 196640 | tf_op jit(solution)/shard_map/ppermute | solution.py:29
  287.6 1.7 collective-permute-start.63
  289.3 1.4 collective-permute-start.61
  290.7 5.0 %collective-permute-done.65.refs_6_ = bf16[256,384]{1,0:T(8,128)(2,1)S(1)} collective-permute-done((bf16[256,384]{1,0:T(8,128)(2,1)S(1)}, bf16[256,384]{1,0:T(8,128)(2,1)S(1)}, u32[]{:S(2)}, u32[]{:S(2)}) %collective-permute-start.65) | collective-permute-done | bytes 196640 | tf_op jit(solution)/shard_map/ppermute | solution.py:29
  295.7 1.2 collective-permute-done.63.refs_4_
  297.7 1.4 collective-permute-start.54
  299.7 1.5 collective-permute-start.56
  302.1 2.5 shard_map.238
  304.6 2.2 collective-permute-done.54.refs_1_
  306.8 6.3 %collective-permute-done.55.refs_2_ = bf16[128,960]{1,0:T(8,128)(2,1)S(1)} collective-permute-done((bf16[128,960]{1,0:T(8,128)(2,1)S(1)}, bf16[128,960]{1,0:T(8,128)(2,1)S(1)}, u32[]{:S(2)}, u32[]{:S(2)}) %collective-permute-start.55) | collective-permute-done | bytes 245792 | tf_op jit(solution)/shard_map/ppermute | solution.py:29
  313.1 1.3 shard_map.237
  314.4 5.6 %shard_map.239 = (f32[240,2560]{1,0:T(8,128)}, f32[240,2560]{1,0:T(8,128)}, f32[960,640]{1,0:T(8,128)}) custom-call(s32[3]{0:T(128)S(1)} %pad_add_fusion.1.at_ref, bf16[512,1024]{1,0:T(8,128)(2,1)S(1)} %get-tuple-element.178.a_ref, bf16[448,1024]{1,0:T(8,128)(2,1)S(1)} %get-tuple-element.184.b_ref, bf16[960,1024]{1,0:T(8,128)(2,1)S(1)} %collective-permute-done.67.odd_ref), custom_call_target="tpu_custom_call" | custom-call | flops 7000000000 | bytes 7000000 | tf_op jit(solution)/shard_map/pallas_call | solution.py:52
  (203 shorter events, 40.8 us)
Async XLA Ops:
  6.9 10.9 %collective-permute-start.9 = (bf16[256,384]{1,0:T(8,128)(2,1)S(1)}, bf16[256,384]{1,0:T(8,128)(2,1)S(1)}, u32[]{:S(2)}, u32[]{:S(2)}) collective-permute-start(bf16[256,384]{1,0:T(8,128)(2,1)S(1)} %shard_map.221.refs_8_), channel_id=1, source_target_pairs={{0,3},{1,2},{2,1},{3,0},{4,7},{5,6},{6,5},{7,4},{8,11},{9,10},{10,... | collective-permute-start | bytes 589832 | tf_op jit(solution)/shard_map/ppermute | solution.py:29
  12.0 16.8 %collective-permute-start.8 = (bf16[256,384]{1,0:T(8,128)(2,1)S(1)}, bf16[256,384]{1,0:T(8,128)(2,1)S(1)}, u32[]{:S(2)}, u32[]{:S(2)}) collective-permute-start(bf16[256,384]{1,0:T(8,128)(2,1)S(1)} %shard_map.221.refs_8_), channel_id=1, source_target_pairs={{0,2},{1,3},{2,0},{3,1},{4,6},{5,7},{6,4},{7,5},{8,10},{9,11},{10,... | collective-permute-start | bytes 589832 | tf_op jit(solution)/shard_map/ppermute | solution.py:29
  12.1 16.6 %collective-permute-start.5 = (bf16[128,960]{1,0:T(8,128)(2,1)S(1)}, bf16[128,960]{1,0:T(8,128)(2,1)S(1)}, u32[]{:S(2)}, u32[]{:S(2)}) collective-permute-start(bf16[128,960]{1,0:T(8,128)(2,1)S(1)} %copy.55.refs_0_.refs_4_), channel_id=1, source_target_pairs={{0,24},{1,25},{2,26},{3,27},{4,28},{5,29},{6,30},{7,31},{8,16},{9,... | collective-permute-start | bytes 737288 | tf_op jit(solution)/shard_map/ppermute | solution.py:29
  14.7 14.6 %collective-permute-start.3 = (bf16[128,960]{1,0:T(8,128)(2,1)S(1)}, bf16[128,960]{1,0:T(8,128)(2,1)S(1)}, u32[]{:S(2)}, u32[]{:S(2)}) collective-permute-start(bf16[128,960]{1,0:T(8,128)(2,1)S(1)} %copy.55.refs_0_.refs_4_), channel_id=1, source_target_pairs={{0,16},{1,17},{2,18},{3,19},{4,20},{5,21},{6,22},{7,23},{8,24},{9,... | collective-permute-start | bytes 737288 | tf_op jit(solution)/shard_map/ppermute | solution.py:29
  15.2 14.2 %collective-permute-start.1 = (bf16[128,960]{1,0:T(8,128)(2,1)S(1)}, bf16[128,960]{1,0:T(8,128)(2,1)S(1)}, u32[]{:S(2)}, u32[]{:S(2)}) collective-permute-start(bf16[128,960]{1,0:T(8,128)(2,1)S(1)} %copy.55.refs_0_.refs_4_), channel_id=1, source_target_pairs={{0,8},{1,9},{2,10},{3,11},{4,12},{5,13},{6,14},{7,15},{8,0},{9,1},... | collective-permute-start | bytes 737288 | tf_op jit(solution)/shard_map/ppermute | solution.py:29
  17.8 14.9 %collective-permute-start.7 = (bf16[256,384]{1,0:T(8,128)(2,1)S(1)}, bf16[256,384]{1,0:T(8,128)(2,1)S(1)}, u32[]{:S(2)}, u32[]{:S(2)}) collective-permute-start(bf16[256,384]{1,0:T(8,128)(2,1)S(1)} %shard_map.221.refs_8_), channel_id=1, source_target_pairs={{0,1},{1,0},{2,3},{3,2},{4,5},{5,4},{6,7},{7,6},{8,9},{9,8},{10,11... | collective-permute-start | bytes 589832 | tf_op jit(solution)/shard_map/ppermute | solution.py:29
  28.8 3.9 %collective-permute-start = (bf16[128,960]{1,0:T(8,128)(2,1)S(1)}, bf16[128,960]{1,0:T(8,128)(2,1)S(1)}, u32[]{:S(2)}, u32[]{:S(2)}) collective-permute-start(bf16[128,960]{1,0:T(8,128)(2,1)S(1)} %copy.55.refs_0_.refs_4_), channel_id=1, source_target_pairs={{0,4},{1,5},{2,6},{3,7},{4,0},{5,1},{6,2},{7,3},{8,12},{9,13},{10,... | collective-permute-start | bytes 737288 | tf_op jit(solution)/shard_map/ppermute | solution.py:29
  28.8 3.9 %collective-permute-start.6 = (bf16[128,960]{1,0:T(8,128)(2,1)S(1)}, bf16[128,960]{1,0:T(8,128)(2,1)S(1)}, u32[]{:S(2)}, u32[]{:S(2)}) collective-permute-start(bf16[128,960]{1,0:T(8,128)(2,1)S(1)} %collective-permute-done.5.refs_6_), channel_id=1, source_target_pairs={{0,4},{1,5},{2,6},{3,7},{4,0},{5,1},{6,2},{7,3},{8,12},{9,13},{10,... | collective-permute-start | bytes 737288 | tf_op jit(solution)/shard_map/ppermute | solution.py:29
  29.3 3.4 %collective-permute-start.4 = (bf16[128,960]{1,0:T(8,128)(2,1)S(1)}, bf16[128,960]{1,0:T(8,128)(2,1)S(1)}, u32[]{:S(2)}, u32[]{:S(2)}) collective-permute-start(bf16[128,960]{1,0:T(8,128)(2,1)S(1)} %collective-permute-done.3.refs_4_), channel_id=1, source_target_pairs={{0,4},{1,5},{2,6},{3,7},{4,0},{5,1},{6,2},{7,3},{8,12},{9,13},{10,... | collective-permute-start | bytes 737288 | tf_op jit(solution)/shard_map/ppermute | solution.py:29
  29.4 3.3 %collective-permute-start.2 = (bf16[128,960]{1,0:T(8,128)(2,1)S(1)}, bf16[128,960]{1,0:T(8,128)(2,1)S(1)}, u32[]{:S(2)}, u32[]{:S(2)}) collective-permute-start(bf16[128,960]{1,0:T(8,128)(2,1)S(1)} %collective-permute-done.1.refs_2_), channel_id=1, source_target_pairs={{0,4},{1,5},{2,6},{3,7},{4,0},{5,1},{6,2},{7,3},{8,12},{9,13},{10,... | collective-permute-start | bytes 737288 | tf_op jit(solution)/shard_map/ppermute | solution.py:29
  38.1 8.0 %collective-permute-start.10 = (bf16[128,1024]{1,0:T(8,128)(2,1)S(1)}, bf16[128,1024]{1,0:T(8,128)(2,1)S(1)}, u32[]{:S(2)}, u32[]{:S(2)}) collective-permute-start(bf16[128,1024]{1,0:T(8,128)(2,1)S(1)} %get-tuple-element.95), channel_id=1, source_target_pairs={{0,8},{1,9},{2,10},{3,11},{4,12},{5,13},{6,14},{7,15},{8,0},{9,1},... | collective-permute-start | bytes 786440 | tf_op jit(solution)/shard_map/ppermute | solution.py:29
  47.0 25.6 %collective-permute-start.19 = (bf16[256,1024]{1,0:T(8,128)(2,1)}, bf16[256,1024]{1,0:T(8,128)(2,1)}, u32[]{:S(2)}, u32[]{:S(2)}) collective-permute-start(bf16[256,1024]{1,0:T(8,128)(2,1)} %get-tuple-element.197), channel_id=1, source_target_pairs={{0,16},{1,17},{2,18},{3,19},{4,20},{5,21},{6,22},{7,23},{8,24},{9,... | collective-permute-start | bytes 1572872 | tf_op jit(solution)/shard_map/ppermute | solution.py:29
  49.3 11.1 %collective-permute-start.14 = (bf16[1024,128]{1,0:T(8,128)(2,1)S(1)}, bf16[1024,128]{1,0:T(8,128)(2,1)S(1)}, u32[]{:S(2)}, u32[]{:S(2)}) collective-permute-start(bf16[1024,128]{1,0:T(8,128)(2,1)S(1)} %get-tuple-element.99.refs_0_), channel_id=1, source_target_pairs={{0,3},{1,2},{2,1},{3,0},{4,7},{5,6},{6,5},{7,4},{8,11},{9,10},{10,... | collective-permute-start | bytes 786440 | tf_op jit(solution)/shard_map/ppermute | solution.py:29
  51.8 20.8 %collective-permute-start.13 = (bf16[1024,128]{1,0:T(8,128)(2,1)S(1)}, bf16[1024,128]{1,0:T(8,128)(2,1)S(1)}, u32[]{:S(2)}, u32[]{:S(2)}) collective-permute-start(bf16[1024,128]{1,0:T(8,128)(2,1)S(1)} %get-tuple-element.99.refs_0_), channel_id=1, source_target_pairs={{0,2},{1,3},{2,0},{3,1},{4,6},{5,7},{6,4},{7,5},{8,10},{9,11},{10,... | collective-permute-start | bytes 786440 | tf_op jit(solution)/shard_map/ppermute | solution.py:29
  51.8 20.8 %collective-permute-start.12 = (bf16[1024,128]{1,0:T(8,128)(2,1)S(1)}, bf16[1024,128]{1,0:T(8,128)(2,1)S(1)}, u32[]{:S(2)}, u32[]{:S(2)}) collective-permute-start(bf16[1024,128]{1,0:T(8,128)(2,1)S(1)} %get-tuple-element.99.refs_0_), channel_id=1, source_target_pairs={{0,1},{1,0},{2,3},{3,2},{4,5},{5,4},{6,7},{7,6},{8,9},{9,8},{10,11... | collective-permute-start | bytes 786440 | tf_op jit(solution)/shard_map/ppermute | solution.py:29
  53.7 21.8 %collective-permute-start.11 = (bf16[128,1024]{1,0:T(8,128)(2,1)S(1)}, bf16[128,1024]{1,0:T(8,128)(2,1)S(1)}, u32[]{:S(2)}, u32[]{:S(2)}) collective-permute-start(bf16[128,1024]{1,0:T(8,128)(2,1)S(1)} %get-tuple-element.96), channel_id=1, source_target_pairs={{0,16},{1,17},{2,18},{3,19},{4,20},{5,21},{6,22},{7,23},{8,24},{9,... | collective-permute-start | bytes 786440 | tf_op jit(solution)/shard_map/ppermute | solution.py:29
  72.6 22.8 %collective-permute-start.21 = (bf16[240,960]{1,0:T(8,128)(2,1)S(1)}, bf16[240,960]{1,0:T(8,128)(2,1)}, u32[]{:S(2)}, u32[]{:S(2)}) collective-permute-start(bf16[240,960]{1,0:T(8,128)(2,1)S(1)} %shard_map.224), channel_id=1, source_target_pairs={{0,2},{1,3},{2,0},{3,1},{4,6},{5,7},{6,4},{7,5},{8,10},{9,11},{10,... | collective-permute-start | bytes 1382408 | tf_op jit(solution)/shard_map/ppermute | solution.py:29
  77.4 19.0 %collective-permute-start.20 = (bf16[256,1024]{1,0:T(8,128)(2,1)}, bf16[256,1024]{1,0:T(8,128)(2,1)}, u32[]{:S(2)}, u32[]{:S(2)}) collective-permute-start(bf16[256,1024]{1,0:T(8,128)(2,1)} %get-tuple-element.191), channel_id=1, source_target_pairs={{0,8},{1,9},{2,10},{3,11},{4,12},{5,13},{6,14},{7,15},{8,0},{9,1},... | collective-permute-start | bytes 1572872 | tf_op jit(solution)/shard_map/ppermute | solution.py:29
  79.7 19.0 %collective-permute-start.15 = (bf16[1024,128]{1,0:T(8,128)(2,1)S(1)}, bf16[1024,128]{1,0:T(8,128)(2,1)S(1)}, u32[]{:S(2)}, u32[]{:S(2)}) collective-permute-start(bf16[1024,128]{1,0:T(8,128)(2,1)S(1)} %get-tuple-element.99.refs_0_), channel_id=1, source_target_pairs={{0,4},{1,5},{2,6},{3,7},{4,0},{5,1},{6,2},{7,3},{8,12},{9,13},{10,... | collective-permute-start | bytes 786440 | tf_op jit(solution)/shard_map/ppermute | solution.py:29
  79.8 19.4 %collective-permute-start.18 = (bf16[1024,128]{1,0:T(8,128)(2,1)S(1)}, bf16[1024,128]{1,0:T(8,128)(2,1)S(1)}, u32[]{:S(2)}, u32[]{:S(2)}) collective-permute-start(bf16[1024,128]{1,0:T(8,128)(2,1)S(1)} %collective-permute-done.14.refs_3_), channel_id=1, source_target_pairs={{0,4},{1,5},{2,6},{3,7},{4,0},{5,1},{6,2},{7,3},{8,12},{9,13},{10,... | collective-permute-start | bytes 786440 | tf_op jit(solution)/shard_map/ppermute | solution.py:29
  80.3 18.9 %collective-permute-start.17 = (bf16[1024,128]{1,0:T(8,128)(2,1)S(1)}, bf16[1024,128]{1,0:T(8,128)(2,1)S(1)}, u32[]{:S(2)}, u32[]{:S(2)}) collective-permute-start(bf16[1024,128]{1,0:T(8,128)(2,1)S(1)} %collective-permute-done.13.refs_2_), channel_id=1, source_target_pairs={{0,4},{1,5},{2,6},{3,7},{4,0},{5,1},{6,2},{7,3},{8,12},{9,13},{10,... | collective-permute-start | bytes 786440 | tf_op jit(solution)/shard_map/ppermute | solution.py:29
  95.4 3.8 %collective-permute-start.16 = (bf16[1024,128]{1,0:T(8,128)(2,1)S(1)}, bf16[1024,128]{1,0:T(8,128)(2,1)S(1)}, u32[]{:S(2)}, u32[]{:S(2)}) collective-permute-start(bf16[1024,128]{1,0:T(8,128)(2,1)S(1)} %collective-permute-done.12.refs_1_), channel_id=1, source_target_pairs={{0,4},{1,5},{2,6},{3,7},{4,0},{5,1},{6,2},{7,3},{8,12},{9,13},{10,... | collective-permute-start | bytes 786440 | tf_op jit(solution)/shard_map/ppermute | solution.py:29
  96.5 31.8 %collective-permute-start.30 = (bf16[480,960]{1,0:T(8,128)(2,1)S(1)}, bf16[480,960]{1,0:T(8,128)(2,1)S(1)}, u32[]{:S(2)}, u32[]{:S(2)}) collective-permute-start(bf16[480,960]{1,0:T(8,128)(2,1)S(1)} %constant_dynamic-update-slice_fusion.10.refs_11_), channel_id=1, source_target_pairs={{0,1},{1,0},{2,3},{3,2},{4,5},{5,4},{6,7},{7,6},{8,9},{9,8},{10,11... | collective-permute-start | bytes 2764808 | tf_op jit(solution)/shard_map/ppermute | solution.py:29
  98.7 31.3 %collective-permute-start.29 = (bf16[1024,1024]{1,0:T(8,128)(2,1)}, bf16[1024,1024]{1,0:T(8,128)(2,1)S(1)}, u32[]{:S(2)}, u32[]{:S(2)}) collective-permute-start(bf16[1024,1024]{1,0:T(8,128)(2,1)} %get-tuple-element.179), channel_id=1, source_target_pairs={{0,4},{1,5},{2,6},{3,7},{4,0},{5,1},{6,2},{7,3},{8,12},{9,13},{10,... | collective-permute-start | bytes 6291464 | tf_op jit(solution)/shard_map/ppermute | solution.py:29
  112.9 10.2 %collective-permute-start.27 = (bf16[1024,128]{1,0:T(8,128)(2,1)S(1)}, bf16[1024,128]{1,0:T(8,128)(2,1)S(1)}, u32[]{:S(2)}, u32[]{:S(2)}) collective-permute-start(bf16[1024,128]{1,0:T(8,128)(2,1)S(1)} %get-tuple-element.103.refs_0_), channel_id=1, source_target_pairs={{0,24},{1,25},{2,26},{3,27},{4,28},{5,29},{6,30},{7,31},{8,16},{9,... | collective-permute-start | bytes 786440 | tf_op jit(solution)/shard_map/ppermute | solution.py:29
  114.9 12.8 %collective-permute-start.25 = (bf16[1024,128]{1,0:T(8,128)(2,1)S(1)}, bf16[1024,128]{1,0:T(8,128)(2,1)S(1)}, u32[]{:S(2)}, u32[]{:S(2)}) collective-permute-start(bf16[1024,128]{1,0:T(8,128)(2,1)S(1)} %get-tuple-element.103.refs_0_), channel_id=1, source_target_pairs={{0,16},{1,17},{2,18},{3,19},{4,20},{5,21},{6,22},{7,23},{8,24},{9,... | collective-permute-start | bytes 786440 | tf_op jit(solution)/shard_map/ppermute | solution.py:29
  115.5 12.2 %collective-permute-start.23 = (bf16[1024,128]{1,0:T(8,128)(2,1)S(1)}, bf16[1024,128]{1,0:T(8,128)(2,1)S(1)}, u32[]{:S(2)}, u32[]{:S(2)}) collective-permute-start(bf16[1024,128]{1,0:T(8,128)(2,1)S(1)} %get-tuple-element.103.refs_0_), channel_id=1, source_target_pairs={{0,8},{1,9},{2,10},{3,11},{4,12},{5,13},{6,14},{7,15},{8,0},{9,1},... | collective-permute-start | bytes 786440 | tf_op jit(solution)/shard_map/ppermute | solution.py:29
  123.0 5.1 %collective-permute-start.22 = (bf16[1024,128]{1,0:T(8,128)(2,1)S(1)}, bf16[1024,128]{1,0:T(8,128)(2,1)S(1)}, u32[]{:S(2)}, u32[]{:S(2)}) collective-permute-start(bf16[1024,128]{1,0:T(8,128)(2,1)S(1)} %get-tuple-element.103.refs_0_), channel_id=1, source_target_pairs={{0,4},{1,5},{2,6},{3,7},{4,0},{5,1},{6,2},{7,3},{8,12},{9,13},{10,... | collective-permute-start | bytes 786440 | tf_op jit(solution)/shard_map/ppermute | solution.py:29
  153.1 2.9 collective-permute-start.31
  153.2 24.3 %collective-permute-start.36 = (bf16[480,960]{1,0:T(8,128)(2,1)S(1)}, bf16[480,960]{1,0:T(8,128)(2,1)S(1)}, u32[]{:S(2)}, u32[]{:S(2)}) collective-permute-start(bf16[480,960]{1,0:T(8,128)(2,1)S(1)} %get-tuple-element.121), channel_id=1, source_target_pairs={{0,1},{1,0},{2,3},{3,2},{4,5},{5,4},{6,7},{7,6},{8,9},{9,8},{10,11... | collective-permute-start | bytes 2764808 | tf_op jit(solution)/shard_map/ppermute | solution.py:29
  158.8 25.7 %collective-permute-start.32 = (bf16[512,1024]{1,0:T(8,128)(2,1)S(1)}, bf16[512,1024]{1,0:T(8,128)(2,1)S(1)}, u32[]{:S(2)}, u32[]{:S(2)}) collective-permute-start(bf16[512,1024]{1,0:T(8,128)(2,1)S(1)} %copy-done.31), channel_id=1, source_target_pairs={{0,4},{1,5},{2,6},{3,7},{4,0},{5,1},{6,2},{7,3},{8,12},{9,13},{10,... | collective-permute-start | bytes 3145736 | tf_op jit(solution)/shard_map/ppermute | solution.py:29
  158.9 18.8 %collective-permute-start.33 = (bf16[128,960]{1,0:T(8,128)(2,1)S(1)}, bf16[128,960]{1,0:T(8,128)(2,1)S(1)}, u32[]{:S(2)}, u32[]{:S(2)}) collective-permute-start(bf16[128,960]{1,0:T(8,128)(2,1)S(1)} %get-tuple-element.113), channel_id=1, source_target_pairs={{0,8},{1,9},{2,10},{3,11},{4,12},{5,13},{6,14},{7,15},{8,0},{9,1},... | collective-permute-start | bytes 737288 | tf_op jit(solution)/shard_map/ppermute | solution.py:29
  160.0 17.7 %collective-permute-start.34 = (bf16[128,960]{1,0:T(8,128)(2,1)S(1)}, bf16[128,960]{1,0:T(8,128)(2,1)S(1)}, u32[]{:S(2)}, u32[]{:S(2)}) collective-permute-start(bf16[128,960]{1,0:T(8,128)(2,1)S(1)} %get-tuple-element.114), channel_id=1, source_target_pairs={{0,16},{1,17},{2,18},{3,19},{4,20},{5,21},{6,22},{7,23},{8,24},{9,... | collective-permute-start | bytes 737288 | tf_op jit(solution)/shard_map/ppermute | solution.py:29
  161.2 16.5 %collective-permute-start.35 = (bf16[128,960]{1,0:T(8,128)(2,1)S(1)}, bf16[128,960]{1,0:T(8,128)(2,1)S(1)}, u32[]{:S(2)}, u32[]{:S(2)}) collective-permute-start(bf16[128,960]{1,0:T(8,128)(2,1)S(1)} %get-tuple-element.115), channel_id=1, source_target_pairs={{0,24},{1,25},{2,26},{3,27},{4,28},{5,29},{6,30},{7,31},{8,16},{9,... | collective-permute-start | bytes 737288 | tf_op jit(solution)/shard_map/ppermute | solution.py:29
  180.9 6.4 %collective-permute-start.38 = (bf16[256,256]{1,0:T(8,128)(2,1)S(1)}, bf16[256,256]{1,0:T(8,128)(2,1)S(1)}, u32[]{:S(2)}, u32[]{:S(2)}) collective-permute-start(bf16[256,256]{1,0:T(8,128)(2,1)S(1)} %get-tuple-element.124), channel_id=1, source_target_pairs={{0,8},{1,9},{2,10},{3,11},{4,12},{5,13},{6,14},{7,15},{8,0},{9,1},... | collective-permute-start | bytes 393224 | tf_op jit(solution)/shard_map/ppermute | solution.py:29
  182.1 10.8 %collective-permute-start.42 = (bf16[256,256]{1,0:T(8,128)(2,1)S(1)}, bf16[256,256]{1,0:T(8,128)(2,1)S(1)}, u32[]{:S(2)}, u32[]{:S(2)}) collective-permute-start(bf16[256,256]{1,0:T(8,128)(2,1)S(1)} %get-tuple-element.131), channel_id=1, source_target_pairs={{0,16},{1,17},{2,18},{3,19},{4,20},{5,21},{6,22},{7,23},{8,24},{9,... | collective-permute-start | bytes 393224 | tf_op jit(solution)/shard_map/ppermute | solution.py:29
  183.3 9.6 %collective-permute-start.43 = (bf16[256,256]{1,0:T(8,128)(2,1)S(1)}, bf16[256,256]{1,0:T(8,128)(2,1)S(1)}, u32[]{:S(2)}, u32[]{:S(2)}) collective-permute-start(bf16[256,256]{1,0:T(8,128)(2,1)S(1)} %get-tuple-element.132), channel_id=1, source_target_pairs={{0,24},{1,25},{2,26},{3,27},{4,28},{5,29},{6,30},{7,31},{8,16},{9,... | collective-permute-start | bytes 393224 | tf_op jit(solution)/shard_map/ppermute | solution.py:29
  187.3 23.1 %collective-permute-start.41 = (bf16[128,960]{1,0:T(8,128)(2,1)S(1)}, bf16[128,960]{1,0:T(8,128)(2,1)S(1)}, u32[]{:S(2)}, u32[]{:S(2)}) collective-permute-start(bf16[128,960]{1,0:T(8,128)(2,1)S(1)} %get-tuple-element.129), channel_id=1, source_target_pairs={{0,24},{1,25},{2,26},{3,27},{4,28},{5,29},{6,30},{7,31},{8,16},{9,... | collective-permute-start | bytes 737288 | tf_op jit(solution)/shard_map/ppermute | solution.py:29
  189.0 21.4 %collective-permute-start.40 = (bf16[128,960]{1,0:T(8,128)(2,1)S(1)}, bf16[128,960]{1,0:T(8,128)(2,1)S(1)}, u32[]{:S(2)}, u32[]{:S(2)}) collective-permute-start(bf16[128,960]{1,0:T(8,128)(2,1)S(1)} %get-tuple-element.127), channel_id=1, source_target_pairs={{0,16},{1,17},{2,18},{3,19},{4,20},{5,21},{6,22},{7,23},{8,24},{9,... | collective-permute-start | bytes 737288 | tf_op jit(solution)/shard_map/ppermute | solution.py:29
  189.9 20.6 %collective-permute-start.39 = (bf16[128,960]{1,0:T(8,128)(2,1)S(1)}, bf16[128,960]{1,0:T(8,128)(2,1)S(1)}, u32[]{:S(2)}, u32[]{:S(2)}) collective-permute-start(bf16[128,960]{1,0:T(8,128)(2,1)S(1)} %get-tuple-element.125), channel_id=1, source_target_pairs={{0,8},{1,9},{2,10},{3,11},{4,12},{5,13},{6,14},{7,15},{8,0},{9,1},... | collective-permute-start | bytes 737288 | tf_op jit(solution)/shard_map/ppermute | solution.py:29
  210.4 25.2 %collective-permute-start.44 = (bf16[4096,128]{1,0:T(8,128)(2,1)S(1)}, bf16[4096,128]{1,0:T(8,128)(2,1)S(1)}, u32[]{:S(2)}, u32[]{:S(2)}) collective-permute-start(bf16[4096,128]{1,0:T(8,128)(2,1)S(1)} %get-tuple-element.137), channel_id=1, source_target_pairs={{0,4},{1,5},{2,6},{3,7},{4,0},{5,1},{6,2},{7,3},{8,12},{9,13},{10,... | collective-permute-start | bytes 3145736 | tf_op jit(solution)/shard_map/ppermute | solution.py:29
  210.5 25.1 %collective-permute-start.45 = (bf16[240,960]{1,0:T(8,128)(2,1)S(1)}, bf16[240,960]{1,0:T(8,128)(2,1)S(1)}, u32[]{:S(2)}, u32[]{:S(2)}) collective-permute-start(bf16[240,960]{1,0:T(8,128)(2,1)S(1)} %get-tuple-element.138), channel_id=1, source_target_pairs={{0,2},{1,3},{2,0},{3,1},{4,6},{5,7},{6,4},{7,5},{8,10},{9,11},{10,... | collective-permute-start | bytes 1382408 | tf_op jit(solution)/shard_map/ppermute | solution.py:29
  236.0 8.9 %collective-permute-start.46 = (bf16[128,1024]{1,0:T(8,128)(2,1)S(1)}, bf16[128,1024]{1,0:T(8,128)(2,1)S(1)}, u32[]{:S(2)}, u32[]{:S(2)}) collective-permute-start(bf16[128,1024]{1,0:T(8,128)(2,1)S(1)} %get-tuple-element.145), channel_id=1, source_target_pairs={{0,8},{1,9},{2,10},{3,11},{4,12},{5,13},{6,14},{7,15},{8,0},{9,1},... | collective-permute-start | bytes 786440 | tf_op jit(solution)/shard_map/ppermute | solution.py:29
  237.4 24.1 %collective-permute-start.50 = (bf16[1024,128]{1,0:T(8,128)(2,1)S(1)}, bf16[1024,128]{1,0:T(8,128)(2,1)S(1)}, u32[]{:S(2)}, u32[]{:S(2)}) collective-permute-start(bf16[1024,128]{1,0:T(8,128)(2,1)S(1)} %get-tuple-element.141), channel_id=1, source_target_pairs={{0,1},{1,0},{2,3},{3,2},{4,5},{5,4},{6,7},{7,6},{8,9},{9,8},{10,11... | collective-permute-start | bytes 786440 | tf_op jit(solution)/shard_map/ppermute | solution.py:29
  237.4 10.3 %collective-permute-start.48 = (bf16[112,1024]{1,0:T(8,128)(2,1)S(1)}, bf16[112,1024]{1,0:T(8,128)(2,1)S(1)}, u32[]{:S(2)}, u32[]{:S(2)}) collective-permute-start(bf16[112,1024]{1,0:T(8,128)(2,1)S(1)} %get-tuple-element.147), channel_id=1, source_target_pairs={{0,16},{1,17},{2,18},{3,19},{4,20},{5,21},{6,22},{7,23},{8,24},{9,... | collective-permute-start | bytes 688136 | tf_op jit(solution)/shard_map/ppermute | solution.py:29
  240.4 21.1 %collective-permute-start.51 = (bf16[1024,128]{1,0:T(8,128)(2,1)S(1)}, bf16[1024,128]{1,0:T(8,128)(2,1)S(1)}, u32[]{:S(2)}, u32[]{:S(2)}) collective-permute-start(bf16[1024,128]{1,0:T(8,128)(2,1)S(1)} %get-tuple-element.149), channel_id=1, source_target_pairs={{0,2},{1,3},{2,0},{3,1},{4,6},{5,7},{6,4},{7,5},{8,10},{9,11},{10,... | collective-permute-start | bytes 786440 | tf_op jit(solution)/shard_map/ppermute | solution.py:29
  242.4 19.1 %collective-permute-start.52 = (bf16[1024,128]{1,0:T(8,128)(2,1)S(1)}, bf16[1024,128]{1,0:T(8,128)(2,1)S(1)}, u32[]{:S(2)}, u32[]{:S(2)}) collective-permute-start(bf16[1024,128]{1,0:T(8,128)(2,1)S(1)} %get-tuple-element.150), channel_id=1, source_target_pairs={{0,3},{1,2},{2,1},{3,0},{4,7},{5,6},{6,5},{7,4},{8,11},{9,10},{10,... | collective-permute-start | bytes 786440 | tf_op jit(solution)/shard_map/ppermute | solution.py:29
  244.9 12.9 %collective-permute-start.47 = (bf16[256,1024]{1,0:T(8,128)(2,1)S(1)}, bf16[256,1024]{1,0:T(8,128)(2,1)S(1)}, u32[]{:S(2)}, u32[]{:S(2)}) collective-permute-start(bf16[256,1024]{1,0:T(8,128)(2,1)S(1)} %pad_maximum_fusion), channel_id=1, source_target_pairs={{0,16},{1,17},{2,18},{3,19},{4,20},{5,21},{6,22},{7,23},{8,24},{9,... | collective-permute-start | bytes 1572872 | tf_op jit(solution)/shard_map/ppermute | solution.py:29
  247.8 11.0 %collective-permute-start.49 = (bf16[224,1024]{1,0:T(8,128)(2,1)S(1)}, bf16[224,1024]{1,0:T(8,128)(2,1)S(1)}, u32[]{:S(2)}, u32[]{:S(2)}) collective-permute-start(bf16[224,1024]{1,0:T(8,128)(2,1)S(1)} %pad_maximum_fusion.1), channel_id=1, source_target_pairs={{0,8},{1,9},{2,10},{3,11},{4,12},{5,13},{6,14},{7,15},{8,0},{9,1},... | collective-permute-start | bytes 1376264 | tf_op jit(solution)/shard_map/ppermute | solution.py:29
  258.8 55.5 %collective-permute-start.67 = (bf16[960,1024]{1,0:T(8,128)(2,1)S(1)}, bf16[960,1024]{1,0:T(8,128)(2,1)S(1)}, u32[]{:S(2)}, u32[]{:S(2)}) collective-permute-start(bf16[960,1024]{1,0:T(8,128)(2,1)S(1)} %get-tuple-element.183), channel_id=1, source_target_pairs={{0,4},{1,5},{2,6},{3,7},{4,0},{5,1},{6,2},{7,3},{8,12},{9,13},{10,... | collective-permute-start | bytes 5898248 | tf_op jit(solution)/shard_map/ppermute | solution.py:29
  265.2 32.2 %collective-permute-start.53 = (bf16[512,1024]{1,0:T(8,128)(2,1)S(1)}, bf16[512,1024]{1,0:T(8,128)(2,1)S(1)}, u32[]{:S(2)}, u32[]{:S(2)}) collective-permute-start(bf16[512,1024]{1,0:T(8,128)(2,1)S(1)} %get-tuple-element.158), channel_id=1, source_target_pairs={{0,4},{1,5},{2,6},{3,7},{4,0},{5,1},{6,2},{7,3},{8,12},{9,13},{10,... | collective-permute-start | bytes 3145736 | tf_op jit(solution)/shard_map/ppermute | solution.py:29
  265.3 13.3 %collective-permute-start.57 = (bf16[256,384]{1,0:T(8,128)(2,1)S(1)}, bf16[256,384]{1,0:T(8,128)(2,1)S(1)}, u32[]{:S(2)}, u32[]{:S(2)}) collective-permute-start(bf16[256,384]{1,0:T(8,128)(2,1)S(1)} %get-tuple-element.165), channel_id=1, source_target_pairs={{0,1},{1,0},{2,3},{3,2},{4,5},{5,4},{6,7},{7,6},{8,9},{9,8},{10,11... | collective-permute-start | bytes 589832 | tf_op jit(solution)/shard_map/ppermute | solution.py:29
  269.9 17.1 %collective-permute-start.58 = (bf16[256,384]{1,0:T(8,128)(2,1)S(1)}, bf16[256,384]{1,0:T(8,128)(2,1)S(1)}, u32[]{:S(2)}, u32[]{:S(2)}) collective-permute-start(bf16[256,384]{1,0:T(8,128)(2,1)S(1)} %get-tuple-element.166), channel_id=1, source_target_pairs={{0,2},{1,3},{2,0},{3,1},{4,6},{5,7},{6,4},{7,5},{8,10},{9,11},{10,... | collective-permute-start | bytes 589832 | tf_op jit(solution)/shard_map/ppermute | solution.py:29
  270.1 17.0 %collective-permute-start.59 = (bf16[256,384]{1,0:T(8,128)(2,1)S(1)}, bf16[256,384]{1,0:T(8,128)(2,1)S(1)}, u32[]{:S(2)}, u32[]{:S(2)}) collective-permute-start(bf16[256,384]{1,0:T(8,128)(2,1)S(1)} %get-tuple-element.167), channel_id=1, source_target_pairs={{0,3},{1,2},{2,1},{3,0},{4,7},{5,6},{6,5},{7,4},{8,11},{9,10},{10,... | collective-permute-start | bytes 589832 | tf_op jit(solution)/shard_map/ppermute | solution.py:29
  287.1 8.5 %collective-permute-start.65 = (bf16[256,384]{1,0:T(8,128)(2,1)S(1)}, bf16[256,384]{1,0:T(8,128)(2,1)S(1)}, u32[]{:S(2)}, u32[]{:S(2)}) collective-permute-start(bf16[256,384]{1,0:T(8,128)(2,1)S(1)} %add_convert_fusion.refs_0_), channel_id=1, source_target_pairs={{0,24},{1,25},{2,26},{3,27},{4,28},{5,29},{6,30},{7,31},{8,16},{9,... | collective-permute-start | bytes 589832 | tf_op jit(solution)/shard_map/ppermute | solution.py:29
  287.6 9.3 %collective-permute-start.63 = (bf16[256,384]{1,0:T(8,128)(2,1)S(1)}, bf16[256,384]{1,0:T(8,128)(2,1)S(1)}, u32[]{:S(2)}, u32[]{:S(2)}) collective-permute-start(bf16[256,384]{1,0:T(8,128)(2,1)S(1)} %add_convert_fusion.refs_0_), channel_id=1, source_target_pairs={{0,16},{1,17},{2,18},{3,19},{4,20},{5,21},{6,22},{7,23},{8,24},{9,... | collective-permute-start | bytes 589832 | tf_op jit(solution)/shard_map/ppermute | solution.py:29
  289.3 7.6 %collective-permute-start.61 = (bf16[256,384]{1,0:T(8,128)(2,1)S(1)}, bf16[256,384]{1,0:T(8,128)(2,1)S(1)}, u32[]{:S(2)}, u32[]{:S(2)}) collective-permute-start(bf16[256,384]{1,0:T(8,128)(2,1)S(1)} %add_convert_fusion.refs_0_), channel_id=1, source_target_pairs={{0,8},{1,9},{2,10},{3,11},{4,12},{5,13},{6,14},{7,15},{8,0},{9,1},... | collective-permute-start | bytes 589832 | tf_op jit(solution)/shard_map/ppermute | solution.py:29
  295.7 2.0 collective-permute-start.60
  296.9 2.2 collective-permute-start.66
  296.9 2.8 collective-permute-start.64
  297.4 4.7 %collective-permute-start.62 = (bf16[256,384]{1,0:T(8,128)(2,1)S(1)}, bf16[256,384]{1,0:T(8,128)(2,1)S(1)}, u32[]{:S(2)}, u32[]{:S(2)}) collective-permute-start(bf16[256,384]{1,0:T(8,128)(2,1)S(1)} %collective-permute-done.61.refs_2_), channel_id=1, source_target_pairs={{0,4},{1,5},{2,6},{3,7},{4,0},{5,1},{6,2},{7,3},{8,12},{9,13},{10,... | collective-permute-start | bytes 589832 | tf_op jit(solution)/shard_map/ppermute | solution.py:29
  297.7 9.2 %collective-permute-start.54 = (bf16[128,960]{1,0:T(8,128)(2,1)S(1)}, bf16[128,960]{1,0:T(8,128)(2,1)S(1)}, u32[]{:S(2)}, u32[]{:S(2)}) collective-permute-start(bf16[128,960]{1,0:T(8,128)(2,1)S(1)} %get-tuple-element.160), channel_id=1, source_target_pairs={{0,8},{1,9},{2,10},{3,11},{4,12},{5,13},{6,14},{7,15},{8,0},{9,1},... | collective-permute-start | bytes 737288 | tf_op jit(solution)/shard_map/ppermute | solution.py:29
  299.1 14.0 %collective-permute-start.55 = (bf16[128,960]{1,0:T(8,128)(2,1)S(1)}, bf16[128,960]{1,0:T(8,128)(2,1)S(1)}, u32[]{:S(2)}, u32[]{:S(2)}) collective-permute-start(bf16[128,960]{1,0:T(8,128)(2,1)S(1)} %get-tuple-element.161), channel_id=1, source_target_pairs={{0,16},{1,17},{2,18},{3,19},{4,20},{5,21},{6,22},{7,23},{8,24},{9,... | collective-permute-start | bytes 737288 | tf_op jit(solution)/shard_map/ppermute | solution.py:29
  299.7 13.4 %collective-permute-start.56 = (bf16[128,960]{1,0:T(8,128)(2,1)S(1)}, bf16[128,960]{1,0:T(8,128)(2,1)S(1)}, u32[]{:S(2)}, u32[]{:S(2)}) collective-permute-start(bf16[128,960]{1,0:T(8,128)(2,1)S(1)} %get-tuple-element.162), channel_id=1, source_target_pairs={{0,24},{1,25},{2,26},{3,27},{4,28},{5,29},{6,30},{7,31},{8,16},{9,... | collective-permute-start | bytes 737288 | tf_op jit(solution)/shard_map/ppermute | solution.py:29
  (37 other events, 205.1 us)
where the time goes:
time: 322 us; the launch traced here: 320 us
  waiting for transfers between devices  137 us (43%)
  starting transfers between devices  75.6 us (23%)
  Pallas kernels  74.1 us (23%)
  local copies, waits for them, and re-layouts  29.2 us (9%)
    ppermute x68, waiting for transfers between devices, exchange(): return lax.ppermute(array, AXES, [(i, i ^ mask) for i in range(count)])  137 us
    ppermute x68, starting transfers between devices, exchange(): return lax.ppermute(array, AXES, [(i, i ^ mask) for i in range(count)])  75.6 us
    pallas_call x19, Pallas kernels, call(): pl.pallas_call(kernel, out_shape=tuple(outs), in_specs=specs, out_specs=t...  74.1 us
    unnamed x79, local copies, waits for them, and re-layouts  22.6 us
  transfers between devices with their start and end apart: 68, of which 27 were waited for; matrix products, arithmetic and copies ran while one was open for 4% of the time, Pallas kernels for 13%

commit v1 on v0

--- a/solution.py
+++ b/solution.py
@@ -48,7 +48,7 @@
 def call(kernel, outs, inputs, scalars=1, scratch=(), limit=56, cost=1.0, far=()):
     specs = [smem] * scalars + [vmem] * (len(inputs) - scalars)
     for i in far:
-        specs[i] = pl.BlockSpec(memory_space=pl.ANY)
+        specs[i] = pl.BlockSpec(memory_space=pltpu.HBM)
     return pl.pallas_call(
         kernel,
         out_shape=tuple(outs),
@@ -62,6 +62,10 @@
     )(*inputs)
 
 
+def early_rows(rows):
+    return rows // 4 // 16 * 16 + 16
+
+
 def one_hot(rows, columns, start):
     row = lax.broadcasted_iota(i32, (rows, columns), 0)
     column = lax.broadcasted_iota(i32, (rows, columns), 1)
@@ -98,7 +102,7 @@
     lanes = 2 * OWN + OWN
     rest = width - (TP - 1) * OWN
 
-    def kernel(at_ref, q_ref, k_ref, v_ref, o_ref, g_ref, out_ref, cols, heads, whole, sems):
+    def kernel(at_ref, q_ref, k_ref, v_ref, o_ref, g1_ref, g2_ref, out_ref, cols, heads, whole, sems):
         tp = at_ref[0]
         kv = at_ref[2]
         wides, narrows = (q_ref, o_ref), (k_ref, v_ref)
@@ -149,19 +153,20 @@
         out_ref[pl.ds(0, d_rows), pl.ds(OWN, OWN)] = turned.astype(bf16)
         out_ref[pl.ds(0, d_rows), pl.ds(2 * OWN, OWN)] = cols[1]
         out_ref[pl.ds(d_rows, 16), :] = jnp.zeros((16, lanes), bf16)
-        out_ref[pl.ds(d_rows, 2), pl.ds(0, d_rows)] = g_ref[...]
+        out_ref[d_rows, pl.ds(0, d_rows)] = g1_ref[...]
+        out_ref[d_rows + 1, pl.ds(0, d_rows)] = g2_ref[...]
 
     return call(
         kernel,
         [shape((d_rows + 16, lanes), bf16)],
-        [at, w_query, w_key.T, w_value.T, w_out, jnp.stack([gain_one, gain_two])],
+        [at, w_query, w_key.T, w_value.T, w_out, gain_one, gain_two],
         scratch=[
             pltpu.VMEM((2, d_rows, OWN), bf16),
             pltpu.VMEM((2, HEAD, d_rows), bf16),
             pltpu.VMEM((2, d_rows, width), bf16),
             pltpu.SemaphoreType.DMA((4,)),
         ],
-        limit=8,
+        limit=60,
         cost=2.0,
         far=(1, 2, 3, 4),
     )[0]
@@ -173,21 +178,26 @@
     part = ff_z // TP
     own = part * nz
 
-    def kernel(at_ref, g_ref, u_ref, d_ref, out_ref):
+    upper = early_rows(d_rows)
+    lower = d_rows - upper
+
+    def kernel(at_ref, g_ref, u_ref, d_ref, out_ref, upper_ref, lower_ref):
         pick = one_hot(ff_z, part, at_ref[0] * part)
         for ref, start in ((g_ref, 0), (u_ref, own)):
             pieces = [nn(ref[:, pl.ds(s * ff_z, ff_z)], pick) for s in range(nz)]
             out_ref[:, pl.ds(start, own)] = jnp.concatenate(pieces, axis=1).astype(bf16)
         pieces = [nn(d_ref[pl.ds(s * d_rows, d_rows), :], pick) for s in range(nz)]
         out_ref[:, pl.ds(2 * own, own)] = jnp.concatenate(pieces, axis=1).astype(bf16)
-
-    return call(
-        kernel,
-        [shape((d_rows, 3 * own), bf16)],
+        upper_ref[...] = out_ref[pl.ds(0, upper), :]
+        lower_ref[...] = out_ref[pl.ds(upper, lower), :]
+
+    return call(
+        kernel,
+        [shape((rows, 3 * own), bf16) for rows in (d_rows, upper, lower)],
         [at, w_gate, w_up, w_down.T],
         limit=16,
         cost=4.0,
-    )[0]
+    )
 
 
 def project(at, tokens, packs, cosine, sine, cotangent):
@@ -201,7 +211,7 @@
     def kernel(at_ref, *refs):
         toks, refs = refs[:TP], refs[TP:]
         pack, refs = refs[:nz], refs[nz:]
-        cos_ref, sin_ref, cot_ref, x_ref, hid_ref, qt_ref, kv_ref, w_ref, cot_out, wo_out, gain_ref, hold = refs
+        cos_ref, sin_ref, cot_ref, x_ref, hid_ref, qt_ref, kv_ref, w_ref, side_ref, gain_ref, hold = refs
         z = at_ref[1]
         for s in range(nz):
             hold[z ^ s] = pack[s][...]
@@ -210,11 +220,11 @@
         gains = [hold[s, pl.ds(d_rows, 16), pl.ds(0, d_rows)].astype(f32) for s in range(nz)]
         gain_ref[...] = jnp.concatenate(gains, axis=1)[:8]
         gain = gain_ref[pl.ds(0, 1), :]
-        cot_out[:, pl.ds(0, width)] = cot_ref[...]
+        side_ref[pl.ds(0, local), pl.ds(0, width)] = cot_ref[...]
         turned = [
             hold[s, pl.ds(0, d_rows), pl.ds(2 * OWN, OWN)].astype(f32) for s in range(nz)
         ]
-        wo_out[:, pl.ds(0, width)] = jnp.concatenate(turned, axis=0).T.astype(bf16)
+        side_ref[pl.ds(local, OWN), pl.ds(0, width)] = jnp.concatenate(turned, axis=0).T.astype(bf16)
         per = 4
         for tile in range(2 * TP // per):
             side, first = (tile * per) // TP, (tile * per) % TP
@@ -244,13 +254,12 @@
             shape((OWN, rows), bf16),
             shape((rows, OWN), bf16),
             shape((width, 2 * OWN), bf16),
-            shape((local, TP * OWN), bf16),
-            shape((OWN, TP * OWN), bf16),
+            shape((local + OWN, TP * OWN), bf16),
             shape((8, width), f32),
         ],
         [at, *tokens, *packs, cosine, sine, cotangent],
         scratch=[pltpu.VMEM((nz, pack_rows, lanes), bf16)],
-        limit=24,
+        limit=60,
         cost=6.0,
     )
 
@@ -455,7 +464,7 @@
             pltpu.VMEM((2, rows), f32),
             pltpu.VMEM((rows, 128), i32),
         ],
-        limit=40,
+        limit=28,
         cost=18.0,
     )
 
@@ -476,7 +485,8 @@
     local = rows // TP
     half_rows = local // 2
     half = rows // 2
-    d_rows, lanes = packs[0].shape[0] // 2, packs[0].shape[1]
+    d_rows, lanes = packs[0].shape
+    upper, lower = packs[2].shape[0], packs[3].shape[0]
     ff = lanes // 3
     part_rows = ff // nz
     per = 4
@@ -484,30 +494,39 @@
 
     def kernel(at_ref, x_ref, *refs):
         att, refs = refs[:TP], refs[TP:]
-        cot_even, wo_even, odd, pack_near, pack_far = refs[:5]
-        refs = refs[5:]
+        mine, by_x, by_y, by_xy, odd, last_odd = refs[:6]
+        own_pack, one_pack, near_a, near_b, far_a, far_b = refs[6:12]
+        refs = refs[12:]
+        cot_at = pl.ds(0, local)
+        wo_at = pl.ds(local, OWN)
         gain_ref, refs = refs[0], refs[1:]
-        att_out, wo_out, resid_out, gk_ref, gp_ref, lk_ref, lp_ref, gain_out, own_ref = refs[:9]
-        send_ref, refs = refs[9], refs[10:]
+        att_out, wo_out, resid_out, gk_ref, gp_ref, lk_ref, lp_ref, gain_out = refs[:8]
+        targets, refs = refs[8:12], refs[12:]
         gu_w, dn_w, cot_ref, acc_gu, acc_dn, hold, blocks = refs
         tp = at_ref[0]
         z = at_ref[1]
         for j in range(TP):
             columns = pl.ds(pl.multiple_of((tp ^ j) * OWN, OWN), OWN)
-            from_wo, row = (odd, local * TP // 2) if j % 2 else (wo_even, 0)
-            row += OWN * (2 * (j // 2 % 2) + j // 4)
-            wo_out[columns, :] = from_wo[pl.ds(row, OWN), pl.ds(0, width)]
-            from_cot = odd if j % 2 else cot_even
+            even = (mine, by_x, by_y, by_xy)[j // 2]
+            from_cot, from_wo = even.at[cot_at, :], even.at[wo_at, :]
+            if j % 2:
+                source, start = (odd, (local + OWN) * (j // 2)) if j < TP - 1 else (last_odd, 0)
+                from_cot = source.at[pl.ds(start, local), :]
+                from_wo = source.at[pl.ds(start + local, OWN), :]
+            wo_out[columns, :] = from_wo[:, pl.ds(0, width)]
             for side in range(2):
                 for k in range(TP):
                     att_out[pl.ds(side * half + k * half_rows, half_rows), columns] = att[j][
                         pl.ds(side * half + (k ^ j) * half_rows, half_rows), :
                     ]
                 cot_ref[pl.ds(side * half + j * half_rows, half_rows), :] = from_cot[
-                    pl.ds(local * (j // 2) + side * half_rows, half_rows), pl.ds(0, width)
+                    pl.ds(side * half_rows, half_rows), pl.ds(0, width)
                 ]
-        for s in range(nz):
-            hold[z ^ s] = (pack_far if s % 2 else pack_near)[pl.ds(d_rows * (s // 2), d_rows), :]
+        hold[z] = own_pack[...]
+        hold[z ^ 1] = one_pack[...]
+        for s, first, second in ((2, near_a, near_b), (3, far_a, far_b)):
+            hold[z ^ s, pl.ds(0, upper), :] = first[...]
+            hold[z ^ s, pl.ds(upper, lower), :] = second[...]
         for s in range(nz):
             rows_at = pl.ds(s * d_rows, d_rows)
             gu_w[rows_at, :] = hold[s, :, pl.ds(0, 2 * ff)]
@@ -565,10 +584,9 @@
                 axis=1,
             )
         for s in range(nz):
-            target = send_ref if s % 2 else own_ref
-            target[pl.ds(d_rows * (s // 2), d_rows), :] = blocks[z ^ s].astype(target.dtype)
-
-    keep = shape((TP // 2 * local, width), f32)
+            targets[s][...] = blocks[z ^ s].astype(targets[s].dtype)
+
+    keep = shape((TP // 2 * local, width), bf16)
     passed = shape((TP // 2 * local, TP * OWN), bf16)
     return call(
         kernel,
@@ -581,8 +599,10 @@
             keep,
             passed,
             shape((8, width), f32),
-            shape((2 * d_rows, lanes), f32),
-            shape((2 * d_rows, lanes), bf16),
+            shape((d_rows, lanes), f32),
+            shape((d_rows, lanes), bf16),
+            shape((d_rows, lanes), f32),
+            shape((d_rows, lanes), bf16),
         ],
         [at, inputs, *attended, *sides, *packs, gains],
         scratch=[
@@ -594,7 +614,7 @@
             pltpu.VMEM((nz, d_rows, lanes), bf16),
             pltpu.VMEM((nz, d_rows, lanes), f32),
         ],
-        limit=48,
+        limit=44,
         cost=18.0,
     )
 
@@ -607,7 +627,7 @@
             at = pl.ds(j * local, local)
             target = own_ref if j == 0 else sends[j - 1]
             target[...] = (
-                keep_ref[at, :] + cross_ref[at, pl.ds(0, width)].astype(f32)
+                keep_ref[at, :].astype(f32) + cross_ref[at, pl.ds(0, width)].astype(f32)
             ).astype(target.dtype)
 
     return call(
@@ -738,7 +758,7 @@
     return call(
         kernel,
         [
-            shape((TP // 2 * local, width), f32),
+            shape((TP // 2 * local, width), bf16),
             shape((TP // 2 * local, TP * OWN), bf16),
             shape((d_rows + 16, 3 * OWN), f32),
         ]
@@ -793,60 +813,41 @@
     return call(kernel, [turned], [*sums, resid], scalars=0, limit=8, cost=1.0)[0].T
 
 
-def split_rows(rows):
-    first = (rows // 2 + 15) // 16 * 16
-    return first, rows - first
-
-
-def first_sum(keep, arrived):
-    rows, lanes = keep.shape[0] // 2, keep.shape[1]
-
-    def kernel(keep_ref, in_ref, own_ref, send_ref):
-        for ref, start in ((own_ref, 0), (send_ref, rows)):
-            at = pl.ds(start, rows)
-            ref[...] = (keep_ref[at, :] + in_ref[at, :].astype(f32)).astype(ref.dtype)
-
-    return call(
-        kernel,
-        [shape((rows, lanes), f32), shape((rows, lanes), bf16)],
-        [keep, arrived],
-        scalars=0,
-        limit=8,
-        cost=1.0,
-    )
-
-
-def last_sum(own, arrived):
+def first_sum(own, arrived):
+    def kernel(own_ref, in_ref, out_ref):
+        out_ref[...] = (own_ref[...] + in_ref[...].astype(f32)).astype(bf16)
+
+    return call(
+        kernel, [shape(own.shape, bf16)], [own, arrived], scalars=0, limit=8, cost=1.0
+    )[0]
+
+
+def last_sum(own, *arrived):
     rows, lanes = own.shape
-    first, second = split_rows(rows)
-
-    def kernel(own_ref, in_ref, a_ref, b_ref):
-        for ref, start, count in ((a_ref, 0, first), (b_ref, first, second)):
-            at = pl.ds(start, count)
-            ref[:, pl.ds(0, lanes)] = (own_ref[at, :] + in_ref[at, :].astype(f32)).astype(bf16)
-
-    return call(
-        kernel,
-        [shape((first, TP * OWN), bf16), shape((second, TP * OWN), bf16)],
-        [own, arrived],
-        scalars=0,
-        limit=8,
-        cost=1.0,
-    )
-
-
-def ff_outputs(at, even_a, even_b, odd, d_rows, ff_z, nz):
+
+    def kernel(own_ref, *refs):
+        total = own_ref[...]
+        for ref in refs[:-1]:
+            total = total + ref[...].astype(f32)
+        refs[-1][:, pl.ds(0, lanes)] = total.astype(bf16)
+
+    return call(
+        kernel, [shape((rows, TP * OWN), bf16)], [own, *arrived], scalars=0, limit=8, cost=1.0
+    )[0]
+
+
+def ff_outputs(at, mine, by_x, by_y, by_xy, odd, ff_z, nz):
+    d_rows = mine.shape[0]
     part = ff_z // TP
     ff = part * nz
-    first, second = split_rows(d_rows)
-
-    def kernel(at_ref, a_ref, b_ref, odd_ref, gate_ref, up_ref, down_ref, hold):
+
+    def kernel(at_ref, m_ref, x_ref, y_ref, xy_ref, odd_ref, gate_ref, up_ref, down_ref, hold):
         tp = at_ref[0]
-        for j in range(TP):
-            from_a, from_b = (odd_ref, odd_ref) if j % 2 else (a_ref, b_ref)
-            row_b = (first * TP // 2 if j % 2 else 0) + second * (2 * (j // 2 % 2) + j // 4)
-            hold[tp ^ j, pl.ds(0, first), :] = from_a[pl.ds(first * (j // 2), first), pl.ds(0, 3 * ff)]
-            hold[tp ^ j, pl.ds(first, second), :] = from_b[pl.ds(row_b, second), pl.ds(0, 3 * ff)]
+        lanes = pl.ds(0, 3 * ff)
+        for j, ref in enumerate((m_ref, x_ref, y_ref, xy_ref)):
+            hold[tp ^ (2 * j)] = ref[:, lanes]
+        for j in range(TP // 2):
+            hold[tp ^ (2 * j + 1)] = odd_ref[pl.ds(d_rows * j, d_rows), lanes]
         for s in range(nz):
             for start in (s * part, ff + s * part, 2 * ff + s * part):
                 block = jnp.concatenate(
@@ -866,7 +867,7 @@
             shape((d_rows, nz * ff_z), f32),
             shape((nz * d_rows, ff_z), f32),
         ],
-        [at, even_a, even_b, odd],
+        [at, mine, by_x, by_y, by_xy, odd],
         scratch=[pltpu.VMEM((TP, d_rows, 3 * ff), bf16)],
         limit=32,
         cost=7.0,
@@ -946,23 +947,24 @@
     def after(value, *others):
         return lax.optimization_barrier((value, *others))[0]
 
-    def both(left, right):
-        return jnp.concatenate([left, right], axis=0)
-
-    def plane_gather(block):
-        even = [block] + [send(block, j * nz) for j in range(2, TP, 2)]
-        odd = [send(e, nz) for e in even]
-        return [piece for pair in zip(even, odd) for piece in pair]
-
-    def plane_scatter(keep, passed):
-        first, *rest = add_crossed(keep, send(passed, nz), TP // 2)
-        return [first] + [send(piece, 2 * (j + 1) * nz) for j, piece in enumerate(rest)]
+    def level(*arrays):
+        return list(lax.optimization_barrier(arrays))
+
+    def gather_even(block):
+        return [block] + [send(block, j * nz) for j in range(2, TP, 2)]
+
+    def gather_odd(even):
+        return [piece for e in even for piece in (e, send(e, nz))]
+
+    def scatter_far(pieces):
+        return [send(piece, 2 * (j + 1) * nz) for j, piece in enumerate(pieces)]
 
     def from_z(block):
         return [block] + [send(block, s) for s in range(1, nz)]
 
     pack_one = slice_attention_weights(at, w_query, w_key, w_value, w_out, gain_attn, gain_mlp)
-    token_slots = plane_gather(tokens)
+    token_slots = gather_odd(level(*gather_even(tokens)))
+    pack_two = slice_ff_weights(after(at, pack_one), w_gate, w_up, w_down, nz)
     pack_one = from_z(pack_one)
 
     slot_of = jnp.array([[m | (j * nz) for j in range(TP)] for m in group_mask], dtype=i32)
@@ -979,32 +981,32 @@
     sine = jnp.sin(angles) * jnp.where(lane % HEAD < HEAD // 2, -1.0, 1.0)[None, :]
     select = jnp.where((2 * tp + jnp.arange(2)) // GROUP == kv_index, 0, 1).astype(i32)
 
-    inputs, hidden_one, turned_query, kv, w_qkv, cot_own, w_out_own, gains = project(
-        at, token_slots, pack_one, cosine, sine, cotangent
-    )
+    mask_x, mask_y = 2 * nz, 4 * nz
+    pack_two, pack_a, pack_b = pack_two
+    near_a = send(after(pack_a, *pack_one), 2)
+    inputs, hidden_one, turned_query, kv, w_qkv, side, gains = project(
+        after(at, pack_two), token_slots, pack_one, cosine, sine, cotangent
+    )
+    kv, side, near_a = level(kv, side, near_a)
     own_kv = [kv] + [send(kv, m) for m in group_mask[1:]]
-    other_kv = [send(slot, nz) for slot in own_kv]
-    pack_two = slice_ff_weights(after(at, kv), w_gate, w_up, w_down, nz)
-    mask_x, mask_y = 2 * nz, 4 * nz
-    cot_even = both(cot_own, send(cot_own, mask_x))
-    w_out_even = both(w_out_own, send(w_out_own, mask_y))
+    side_x, side_y = send(side, mask_x), send(side, mask_y)
+    side_x, side_y, *own_kv = level(side_x, side_y, *own_kv)
+    other_kv = level(*[send(slot, nz) for slot in own_kv])
+    one, near_b = send(after(pack_two, *own_kv), 1), send(after(pack_b, *own_kv), 2)
+    side_xy = send(side_x, mask_y)
+    side_odd = send(jnp.concatenate([side, side_x, side_y], axis=0), nz)
     attended, attended_own, log_mass = attention_forward(
-        after(select, cot_even, w_out_even),
-        key_base,
-        query_base,
-        turned_query,
-        own_kv,
-        other_kv,
-        half_rows,
-    )
-    cot_even = both(cot_even, send(cot_even, mask_y))
-    w_out_even = both(w_out_even, send(w_out_even, mask_x))
-    pack_two = after(pack_two, *own_kv)
-    pack_near = both(pack_two, send(pack_two, 2))
-    attended_own = after(attended_own, cot_even, w_out_even, pack_near)
-    pack_far = send(pack_near, 1)
-    side_odd = send(both(cot_even, w_out_even), nz)
-    attended_slots = plane_gather(attended_own)
+        select, key_base, query_base, turned_query, own_kv, other_kv, half_rows
+    )
+    attended_own, near_b, one, side_xy, side_odd = level(
+        attended_own, near_b, one, side_xy, side_odd
+    )
+    far_a, far_b, side_xy, *even = level(
+        send(after(near_a, attended_own), 1), send(near_b, 1), side_xy, *gather_even(attended_own)
+    )
+    attended_slots = gather_odd(even)
+    packs = [pack_two, one, near_a, near_b, far_a, far_b]
+    sides = [side, side_x, side_y, side_xy, side_odd, send(side_xy, nz)]
 
     (
         attended_low,
@@ -1015,34 +1017,32 @@
         out_keep,
         out_pass,
         gain_sums,
-        ff_keep,
-        ff_send,
+        ff_own,
+        ff_one,
+        ff_two,
+        ff_three,
     ) = feed_forward(
         at,
         inputs,
         attended_slots,
-        [cot_even, w_out_even, side_odd],
-        [pack_near, pack_far],
+        sides,
+        packs,
         gains,
         nz,
     )
-    sums = plane_scatter(grad_keep, grad_pass)
-    ff_own, ff_send = first_sum(ff_keep, send(ff_send, 1))
-    out_first, *out_rest = add_crossed(
-        out_keep, send(after(out_pass, sums[0]), nz), TP // 2
-    )
+    first, *rest = add_crossed(grad_keep, send(grad_pass, nz), TP // 2)
+    ff_three, first, *rest = level(send(after(ff_three, first), 1), first, *scatter_far(rest))
     grad_resid, trade_keep, trade_pass = branch_gradient(
-        at, sums, resid, cotangent, w_out_all, gains
-    )
-    crossed = send(after(trade_pass, ff_own), nz)
-    pairs = [
-        send(pair, 2 * (j + 1) * nz)
-        for j, pair in enumerate(pair_up(trade_keep, crossed, TP // 2))
-    ]
-    ff_arrived = send(ff_send, 2)
-    out_sums = [out_first] + [
-        send(after(piece, pairs[0]), 2 * (j + 1) * nz) for j, piece in enumerate(out_rest)
-    ]
+        at, [first, *rest], resid, cotangent, w_out_all, gains
+    )
+    crossed, out_crossed = level(send(trade_pass, nz), send(after(out_pass, first), nz))
+    ff_one, *pairs = level(
+        send(after(ff_one, crossed), 1),
+        *scatter_far(pair_up(trade_keep, crossed, TP // 2)),
+    )
+    out_first, *out_rest = add_crossed(out_keep, out_crossed, TP // 2)
+    ff_two = send(after(first_sum(ff_two, ff_three), *pairs), 2)
+    out_rest = scatter_far([after(piece, *pairs) for piece in out_rest])
 
     grad_query, kv_keep, kv_pass, branch_columns = attention_backward(
         after(select, out_first),
@@ -1056,28 +1056,26 @@
         log_mass,
         half_rows,
     )
-    kv_crossed = send(after(kv_pass, *out_sums), nz)
-    ff_a, ff_b = last_sum(ff_own, ff_arrived)
-    first, *rest = add_crossed(kv_keep, after(kv_crossed, ff_a), groups)
-    grad_kv = [first] + [send(piece, m) for piece, m in zip(rest, group_mask[1:])]
+    kv_pass, ff_two, *out_rest = level(kv_pass, ff_two, *out_rest)
+    kv_crossed = send(kv_pass, nz)
+    first, *rest = add_crossed(kv_keep, kv_crossed, groups)
+    ff_total = last_sum(after(ff_own, rest[0]), ff_one, ff_two)
 
     for step in range(outer.bit_length() - 1):
-        far = TP * nz << step
-        ff_a, ff_b = (
-            (part.astype(f32) + send(part, far).astype(f32)).astype(bf16) for part in (ff_a, ff_b)
-        )
-    ff_a, ff_b = after(ff_a, rest[0]), after(ff_b, rest[0])
-    layer_out = layer_output(out_sums, after(resid, rest[0]))
-    ff_even_a = both(ff_a, send(ff_a, mask_x))
-    ff_even_b = both(ff_b, send(ff_b, mask_y))
-    ff_even_a = both(ff_even_a, send(ff_even_a, mask_y))
-    ff_even_b = both(ff_even_b, send(ff_even_b, mask_x))
+        crossing = send(ff_total, TP * nz << step).astype(f32)
+        ff_total = (ff_total.astype(f32) + crossing).astype(bf16)
+    layer_out = layer_output([after(out_first, rest[0]), *out_rest], resid)
+    ff_x, ff_y, *grad_kv = level(
+        send(ff_total, mask_x),
+        send(ff_total, mask_y),
+        *[send(piece, m) for piece, m in zip(rest, group_mask[1:])],
+    )
     grad_out = tn(attended_low[:, :width], after(branch_columns, rest[0]))
 
     last_keep, last_pass, last_own, *last_sends = projection_gradient(
         at,
         grad_query,
-        [after(first, ff_even_a, ff_even_b), *grad_kv[1:]],
+        [first, *grad_kv],
         inputs,
         hidden_one,
         w_qkv,
@@ -1087,21 +1085,28 @@
         grad_out,
         nz,
     )
-    ff_odd = send(both(ff_even_a, ff_even_b), nz)
-    sums = plane_scatter(last_keep, last_pass)
+    near, far = add_crossed(last_keep, send(last_pass, nz), 2)
+    ff_xy, far, *arrived = level(
+        send(after(ff_x, last_own), mask_y),
+        send(far, mask_y),
+        *[send(piece, s + 1) for s, piece in enumerate(last_sends)],
+    )
+    near, far = add_crossed(near, far, 2)
     last_total = last_own
-    for s, piece in enumerate(last_sends):
-        last_total = last_total + send(piece, s + 1).astype(f32)
+    for piece in arrived:
+        last_total = last_total + piece.astype(f32)
     for step in range(outer.bit_length() - 1):
         last_total = last_total + send(last_total.astype(bf16), TP * nz << step).astype(f32)
-    last_slots = plane_gather(last_total.astype(bf16))
-    grad_gate, grad_up, grad_down = ff_outputs(
-        at, ff_even_a, ff_even_b, ff_odd, w_gate.shape[0], w_down.shape[0], nz
-    )
+    last_total = last_total.astype(bf16)
+    ff_slots = [ff_total, ff_x, ff_y, ff_xy]
+    ff_slots.append(send(jnp.concatenate(ff_slots, axis=0), nz))
+    grad_gate, grad_up, grad_down = ff_outputs(at, *ff_slots, w_down.shape[0], nz)
+    far, grad_gate, *even = level(send(far, mask_x), grad_gate, *gather_even(last_total))
+    last_slots = gather_odd(even)
     grad_w_query, grad_w_key, grad_w_value, grad_out, gain_one, gain_two = projection_outputs(
         at, last_slots, width
     )
-    grad_tokens = token_gradient(sums, tokens, grad_resid, gains)
+    grad_tokens = token_gradient([near, far], tokens, grad_resid, gains)
     return (
         layer_out,
         grad_tokens,

time: 322 us -> 277 us (0.86)
  waiting for transfers between devices: 137 us -> 111 us
  local copies, waits for them, and re-layouts: 29.2 us -> 11.5 us
  starting transfers between devices: 75.6 us -> 65.3 us
  Pallas kernels: 74.1 us -> 78.7 us
  other arithmetic: 2.28 us -> 6.46 us
    ppermute x68 -> x70, waiting for transfers between devices: 137 us -> 111 us  [exchange(): return lax.ppermute(array, AXES, [(i, i ^ mask) for i in range(count)])]
    unnamed x79 -> x86, local copies, waits for them, and re-layouts: 22.6 us -> 9.4 us
    ppermute x68 -> x70, starting transfers between devices: 75.6 us -> 65.3 us  [exchange(): return lax.ppermute(array, AXES, [(i, i ^ mask) for i in range(count)])]
    pallas_call x19 -> x20, Pallas kernels: 74.1 us -> 78.7 us  [call(): pl.pallas_call(kernel, out_shape=tuple(outs), in_specs=specs, out_specs=t...]
    concatenate x3 -> x0, local copies, waits for them, and re-layouts: 3.34 us -> none  [both(): return jnp.concatenate([left, right], axis=0)]
  transfers between devices with their start and end apart: 68 -> 70, of which waited for: 27 -> 31; matrix products, arithmetic and copies ran while one was open for 4% -> 3% of each run, Pallas kernels for 13% -> 18%
where the time goes in v1:
time: 277 us; the launch traced here: 275 us
  waiting for transfers between devices  111 us (40%)
  Pallas kernels  78.7 us (28%)
  starting transfers between devices  65.3 us (24%)
  local copies, waits for them, and re-layouts  11.5 us (4%)
  other arithmetic  6.46 us (2%)
    ppermute x70, waiting for transfers between devices, exchange(): return lax.ppermute(array, AXES, [(i, i ^ mask) for i in range(count)])  111 us
    pallas_call x20, Pallas kernels, call(): pl.pallas_call(kernel, out_shape=tuple(outs), in_specs=specs, out_specs=t...  78.7 us
    ppermute x70, starting transfers between devices, exchange(): return lax.ppermute(array, AXES, [(i, i ^ mask) for i in range(count)])  65.3 us
    unnamed x86, local copies, waits for them, and re-layouts  9.4 us
  transfers between devices with their start and end apart: 70, of which 31 were waited for; matrix products, arithmetic and copies ran while one was open for 3% of the time, Pallas kernels for 18%

profile of v1, /device:TPU:0, one launch (start us, length us, event | category | flops | bytes accessed | tf_op | source)
XLA Modules:
  0.0 275.3 jit_solution(3587455520235180012)
XLA Ops:
  1.4 3.3 %shard_map.221.refs_8_ = bf16[256,384]{1,0:T(8,128)(2,1)} custom-call(s32[3]{0:T(128)} %pad_add_fusion.1.at_ref, bf16[240,960]{1,0:T(8,128)(2,1)} %q_ref.1, bf16[320,240]{1,0:T(8,128)(2,1)} %bitcast.21, bf16[320,240]{1,0:T(8,128)(2,1)} %bitcast.22, bf16[240,960]{1,0:T(8,128)(2,1)} %o_ref.1, bf16[240]{0:T(256)(128)(2,1)} %g1_ref.1, bf16[240]{0:T(256)(128)(2,1)} %g2_ref.1), custom_call_target="tpu_custom_call" | custom-call | flops 2000000000 | bytes 2000000 | tf_op jit(solution)/shard_map/pallas_call | solution.py:52
  4.7 5.1 %collective-permute-start.9 = (bf16[256,384]{1,0:T(8,128)(2,1)}, bf16[256,384]{1,0:T(8,128)(2,1)}, u32[]{:S(2)}, u32[]{:S(2)}) collective-permute-start(bf16[256,384]{1,0:T(8,128)(2,1)} %shard_map.221.refs_8_), channel_id=1, source_target_pairs={{0,3},{1,2},{2,1},{3,0},{4,7},{5,6},{6,5},{7,4},{8,11},{9,10},{10,... | collective-permute-start | bytes 589832 | tf_op jit(solution)/shard_map/ppermute | solution.py:29
  9.9 2.5 collective-permute-start.2
  14.5 1.3 copy-done.9
  15.8 1.3 copy-done.10
  17.1 2.0 shard_map.222
  20.8 3.6 %collective-permute-done.1.refs_4_ = bf16[128,960]{1,0:T(8,128)(2,1)} collective-permute-done((bf16[128,960]{1,0:T(8,128)(2,1)S(1)}, bf16[128,960]{1,0:T(8,128)(2,1)}, u32[]{:S(2)}, u32[]{:S(2)}) %collective-permute-start.1) | collective-permute-done | bytes 245792 | tf_op jit(solution)/shard_map/ppermute | solution.py:29
  25.3 1.6 collective-permute-done.8.refs_10_
  26.9 3.0 %fusion.2 = (f32[1024,128]{1,0:T(8,128)}, f32[1024,128]{1,0:T(8,128)}) fusion(f32[128]{0:T(128)S(1)} %get-tuple-element.305, f32[128]{0:T(128)S(1)} %get-tuple-element.306, f32[1024]{0:T(1024)S(1)} %convert_element_type.30), kind=kLoop, calls=%fused_computation.8 | loop fusion | flops 262144 | bytes 1053696 | tf_op jit(solution)/shard_map/mul | solution.py:981
  30.0 1.5 collective-permute-start.10
  32.5 6.1 %shard_map.223 = (bf16[1024,960]{1,0:T(8,128)(2,1)}, bf16[1024,960]{1,0:T(8,128)(2,1)}, bf16[128,1024]{1,0:T(8,128)(2,1)}, bf16[1024,128]{1,0:T(8,128)(2,1)}, bf...) custom-call(s32[3]{0:T(128)} %pad_add_fusion.1.at_ref, bf16[128,960]{1,0:T(8,128)(2,1)} %copy-done.30, ...), custom_call_target="tpu_custom_call" | custom-call | flops 6000000000 | bytes 6000000 | tf_op jit(solution)/shard_map/pallas_call | solution.py:52
  39.4 1.5 collective-permute-start.12
  42.0 1.7 collective-permute-start.15
  44.2 2.2 collective-permute-start.13
  46.5 6.9 %collective-permute-done.15.refs_3_ = bf16[1024,128]{1,0:T(8,128)(2,1)S(1)} collective-permute-done((bf16[1024,128]{1,0:T(8,128)(2,1)}, bf16[1024,128]{1,0:T(8,128)(2,1)S(1)}, u32[]{:S(2)}, u32[]{:S(2)}) %collective-permute-start.15) | collective-permute-done | bytes 262176 | tf_op jit(solution)/shard_map/ppermute | solution.py:29
  53.4 13.9 %collective-permute-done.14.refs_2_ = bf16[1024,128]{1,0:T(8,128)(2,1)} collective-permute-done((bf16[1024,128]{1,0:T(8,128)(2,1)}, bf16[1024,128]{1,0:T(8,128)(2,1)}, u32[]{:S(2)}, u32[]{:S(2)}) %collective-permute-start.14) | collective-permute-done | bytes 262176 | tf_op jit(solution)/shard_map/ppermute | solution.py:29
  68.4 2.4 pad_maximum_fusion.1
  73.4 1.9 collective-permute-start.21
  78.1 13.3 %shard_map.224 = (f32[128,1024]{1,0:T(8,128)S(1)}, bf16[1024,128]{1,0:T(8,128)(2,1)S(1)}, f32[2,1024]{1,0:T(2,128)S(1)}) custom-call(s32[2]{0:T(128)S(1)} %compare_select_fusion.1.sel_ref, s32[8,16]{1,0:T(8,128)S(1)} %reshape.107.key_ref, s32[16]{0:T(128)S(1)} %add.85.query_ref, bf16[128,1024]{1,0:T(8,128)(2,1)S(1)} %copy-done.27, ...), custom_call_target="tpu_custom_call" | custom-call | flops 14000000000 | bytes 14000000 | tf_op jit(solution)/shard_map/pallas_call | solution.py:52
  91.5 3.0 %collective-permute-done.21.refs_15_ = bf16[240,960]{1,0:T(8,128)(2,1)S(1)} collective-permute-done((bf16[240,960]{1,0:T(8,128)(2,1)S(1)}, bf16[240,960]{1,0:T(8,128)(2,1)S(1)}, u32[]{:S(2)}, u32[]{:S(2)}) %collective-permute-start.21) | collective-permute-done | bytes 460832 | tf_op jit(solution)/shard_map/ppermute | solution.py:29
  94.7 1.5 collective-permute-start.28
  96.7 1.5 collective-permute-start.26
  98.2 1.8 collective-permute-start.24
  100.0 6.9 %collective-permute-done.24.refs_18_ = bf16[64,960]{1,0:T(8,128)(2,1)S(1)} collective-permute-done((bf16[64,960]{1,0:T(8,128)(2,1)S(1)}, bf16[64,960]{1,0:T(8,128)(2,1)S(1)}, u32[]{:S(2)}, u32[]{:S(2)}) %collective-permute-start.24) | collective-permute-done | bytes 122912 | tf_op jit(solution)/shard_map/ppermute | solution.py:29
  106.9 1.9 collective-permute-done.27.refs_4_
  112.2 19.4 %shard_map.225 = (bf16[1024,1024]{1,0:T(8,128)(2,1)}, bf16[1024,960]{1,0:T(8,128)(2,1)}, f32[128,960]{1,0:T(8,128)S(1)}, bf16[512,960]{1,0:T(8,128)(2,1)}, bf16[...) custom-call(s32[3]{0:T(128)S(1)} %copy-done.7, ...), custom_call_target="tpu_custom_call" | custom-call | flops 17999998976 | bytes 18000000 | tf_op jit(solution)/shard_map/pallas_call | solution.py:52
  131.8 2.7 collective-permute-done.34.cross_ref
  134.6 1.2 copy-done.21
  136.0 1.5 collective-permute-start.35
  138.2 1.4 collective-permute-start.37
  139.6 1.4 collective-permute-start.38
  141.0 5.7 %collective-permute-done.36.refs_1_ = bf16[128,960]{1,0:T(8,128)(2,1)S(1)} collective-permute-done((bf16[128,960]{1,0:T(8,128)(2,1)S(1)}, bf16[128,960]{1,0:T(8,128)(2,1)S(1)}, u32[]{:S(2)}, u32[]{:S(2)}) %collective-permute-start.36) | collective-permute-done | bytes 245792 | tf_op jit(solution)/shard_map/ppermute | solution.py:29
  146.7 3.8 %collective-permute-done.37.refs_2_ = bf16[128,960]{1,0:T(8,128)(2,1)S(1)} collective-permute-done((bf16[128,960]{1,0:T(8,128)(2,1)S(1)}, bf16[128,960]{1,0:T(8,128)(2,1)S(1)}, u32[]{:S(2)}, u32[]{:S(2)}) %collective-permute-start.37) | collective-permute-done | bytes 245792 | tf_op jit(solution)/shard_map/ppermute | solution.py:29
  151.6 1.5 shard_map.227
  155.4 1.5 collective-permute-start.42
  157.8 1.2 collective-permute-start.44
  159.4 2.0 collective-permute-done.42.refs_10_
  161.4 3.6 %collective-permute-done.43.refs_11_ = bf16[256,256]{1,0:T(8,128)(2,1)S(1)} collective-permute-done((bf16[256,256]{1,0:T(8,128)(2,1)S(1)}, bf16[256,256]{1,0:T(8,128)(2,1)S(1)}, u32[]{:S(2)}, u32[]{:S(2)}) %collective-permute-start.43) | collective-permute-done | bytes 131104 | tf_op jit(solution)/shard_map/ppermute | solution.py:29
  165.0 3.3 %collective-permute-done.41.refs_0_ = bf16[240,960]{1,0:T(8,128)(2,1)S(1)} collective-permute-done((bf16[240,960]{1,0:T(8,128)(2,1)S(1)}, bf16[240,960]{1,0:T(8,128)(2,1)S(1)}, u32[]{:S(2)}, u32[]{:S(2)}) %collective-permute-start.41) | collective-permute-done | bytes 460832 | tf_op jit(solution)/shard_map/ppermute | solution.py:29
  168.3 1.5 collective-permute-start.46
  170.6 1.2 collective-permute-start.48
  171.8 1.2 collective-permute-start.45
  173.1 17.9 %shard_map.230 = (f32[128,1024]{1,0:T(8,128)S(1)}, f32[4096,128]{1,0:T(8,128)S(1)}, bf16[4096,128]{1,0:T(8,128)(2,1)S(1)}, bf16[1024,128]{1,0:T(8,128)(2,1)S(1)}) custom-call(s32[2]{0:T(128)S(1)} %compare_select_fusion.1.sel_ref, s32[8,16]{1,0:T(8,128)S(1)} %reshape.107.key_ref, s32[16]{0:T(128)S(1)} %add.85.query_ref, bf16[128,1024]{1,0:T(8,128)(2,1)S(1)} %copy-done.28, ...), custom_call_target="tpu_custom_call" | custom-call | flops 17999998976 | bytes 18000000 | tf_op jit(solution)/shard_map/pallas_call | solution.py:52
  191.0 4.0 %collective-permute-done.45.refs_1_ = bf16[240,960]{1,0:T(8,128)(2,1)S(1)} collective-permute-done((bf16[240,960]{1,0:T(8,128)(2,1)S(1)}, bf16[240,960]{1,0:T(8,128)(2,1)S(1)}, u32[]{:S(2)}, u32[]{:S(2)}) %collective-permute-start.45) | collective-permute-done | bytes 460832 | tf_op jit(solution)/shard_map/ppermute | solution.py:29
  195.1 2.7 collective-permute-done.49.cross_ref
  198.2 1.6 collective-permute-start.51
  200.5 2.7 collective-permute-start.53
  203.2 1.7 collective-permute-start.54
  205.6 16.3 %collective-permute-done.53.refs_2_ = bf16[1024,128]{1,0:T(8,128)(2,1)S(1)} collective-permute-done((bf16[1024,128]{1,0:T(8,128)(2,1)S(1)}, bf16[1024,128]{1,0:T(8,128)(2,1)S(1)}, u32[]{:S(2)}, u32[]{:S(2)}) %collective-permute-start.53) | collective-permute-done | bytes 262176 | tf_op jit(solution)/shard_map/ppermute | solution.py:29
  221.9 3.7 %shard_map.235 = (bf16[512,960]{1,0:T(8,128)(2,1)S(1)}, bf16[512,1024]{1,0:T(8,128)(2,1)S(1)}, f32[256,384]{1,0:T(8,128)S(1)}, bf16[256,384]{1,0:T(8,128)(2,1)S(...) custom-call(s32[3]{0:T(128)S(1)} %copy-done.7, f32[128,1024]{1,0:T(8,128)S(1)} %get-tuple-element.250.dq_ref, ...), custom_call_target="tpu_custom_call" | custom-call | flops 8000000000 | bytes 8000000 | tf_op jit(solution)/shard_map/pallas_call | solution.py:52
  225.7 1.3 collective-permute-start.56
  227.0 1.4 collective-permute-done.55.cross_ref
  228.6 1.3 collective-permute-start.57
  229.9 4.8 %collective-permute-start.58 = (bf16[256,384]{1,0:T(8,128)(2,1)S(1)}, bf16[256,384]{1,0:T(8,128)(2,1)S(1)}, u32[]{:S(2)}, u32[]{:S(2)}) collective-permute-start(bf16[256,384]{1,0:T(8,128)(2,1)S(1)} %get-tuple-element.274), channel_id=1, source_target_pairs={{0,1},{1,0},{2,3},{3,2},{4,5},{5,4},{6,7},{7,6},{8,9},{9,8},{10,11... | collective-permute-start | bytes 589832 | tf_op jit(solution)/shard_map/ppermute | solution.py:29
  235.4 1.7 collective-permute-start.60
  237.0 5.8 %collective-permute-done.58 = bf16[256,384]{1,0:T(8,128)(2,1)S(1)} collective-permute-done((bf16[256,384]{1,0:T(8,128)(2,1)S(1)}, bf16[256,384]{1,0:T(8,128)(2,1)S(1)}, u32[]{:S(2)}, u32[]{:S(2)}) %collective-permute-start.58) | collective-permute-done | bytes 196640 | tf_op jit(solution)/shard_map/ppermute | solution.py:29
  242.9 8.9 %collective-permute-done.59 = bf16[256,384]{1,0:T(8,128)(2,1)S(1)} collective-permute-done((bf16[256,384]{1,0:T(8,128)(2,1)S(1)}, bf16[256,384]{1,0:T(8,128)(2,1)S(1)}, u32[]{:S(2)}, u32[]{:S(2)}) %collective-permute-start.59) | collective-permute-done | bytes 196640 | tf_op jit(solution)/shard_map/ppermute | solution.py:29
  252.2 1.6 collective-permute-start.65
  254.3 1.5 collective-permute-start.63
  256.4 5.6 %shard_map.238 = (f32[240,2560]{1,0:T(8,128)}, f32[240,2560]{1,0:T(8,128)}, f32[960,640]{1,0:T(8,128)}) custom-call(s32[3]{0:T(128)S(1)} %copy-done.7, bf16[240,1024]{1,0:T(8,128)(2,1)S(1)} %shard_map.234.m_ref, bf16[240,1024]{1,0:T(8,128)(2,1)S(1)} %collective-permute-done.50.x_ref, bf16[240,1024]{1,0:T(8,128)(2,1)S(1)} %collective-permute-done.51.y_ref, ...), custom_call_target="tpu_custom_call" | custom-call | flops 7000000000 | bytes 7000000 | tf_op jit(solution)/shard_map/pallas_call | solution.py:52
  262.1 2.6 collective-permute-done.64.refs_4_
  264.7 5.0 %collective-permute-done.61.refs_1_ = bf16[128,960]{1,0:T(8,128)(2,1)S(1)} collective-permute-done((bf16[128,960]{1,0:T(8,128)(2,1)S(1)}, bf16[128,960]{1,0:T(8,128)(2,1)S(1)}, u32[]{:S(2)}, u32[]{:S(2)}) %collective-permute-start.61) | collective-permute-done | bytes 245792 | tf_op jit(solution)/shard_map/ppermute | solution.py:29
  271.6 1.2 shard_map.239
  272.8 2.5 shard_map.240
  (211 shorter events, 32.5 us)
Async XLA Ops:
  4.7 20.6 %collective-permute-start.9 = (bf16[256,384]{1,0:T(8,128)(2,1)}, bf16[256,384]{1,0:T(8,128)(2,1)}, u32[]{:S(2)}, u32[]{:S(2)}) collective-permute-start(bf16[256,384]{1,0:T(8,128)(2,1)} %shard_map.221.refs_8_), channel_id=1, source_target_pairs={{0,3},{1,2},{2,1},{3,0},{4,7},{5,6},{6,5},{7,4},{8,11},{9,10},{10,... | collective-permute-start | bytes 589832 | tf_op jit(solution)/shard_map/ppermute | solution.py:29
  9.8 17.1 %collective-permute-start.8 = (bf16[256,384]{1,0:T(8,128)(2,1)}, bf16[256,384]{1,0:T(8,128)(2,1)}, u32[]{:S(2)}, u32[]{:S(2)}) collective-permute-start(bf16[256,384]{1,0:T(8,128)(2,1)} %shard_map.221.refs_8_), channel_id=1, source_target_pairs={{0,2},{1,3},{2,0},{3,1},{4,6},{5,7},{6,4},{7,5},{8,10},{9,11},{10,... | collective-permute-start | bytes 589832 | tf_op jit(solution)/shard_map/ppermute | solution.py:29
  9.9 10.2 %collective-permute-start.2 = (bf16[128,960]{1,0:T(8,128)(2,1)S(1)}, bf16[128,960]{1,0:T(8,128)(2,1)S(1)}, u32[]{:S(2)}, u32[]{:S(2)}) collective-permute-start(bf16[128,960]{1,0:T(8,128)(2,1)S(1)} %copy.51.refs_2_), channel_id=1, source_target_pairs={{0,24},{1,25},{2,26},{3,27},{4,28},{5,29},{6,30},{7,31},{8,16},{9,... | collective-permute-start | bytes 737288 | tf_op jit(solution)/shard_map/ppermute | solution.py:29
  12.4 11.9 %collective-permute-start.1 = (bf16[128,960]{1,0:T(8,128)(2,1)S(1)}, bf16[128,960]{1,0:T(8,128)(2,1)}, u32[]{:S(2)}, u32[]{:S(2)}) collective-permute-start(bf16[128,960]{1,0:T(8,128)(2,1)S(1)} %copy.51.refs_2_), channel_id=1, source_target_pairs={{0,16},{1,17},{2,18},{3,19},{4,20},{5,21},{6,22},{7,23},{8,24},{9,... | collective-permute-start | bytes 737288 | tf_op jit(solution)/shard_map/ppermute | solution.py:29
  12.9 11.5 %collective-permute-start = (bf16[128,960]{1,0:T(8,128)(2,1)S(1)}, bf16[128,960]{1,0:T(8,128)(2,1)}, u32[]{:S(2)}, u32[]{:S(2)}) collective-permute-start(bf16[128,960]{1,0:T(8,128)(2,1)S(1)} %copy.51.refs_2_), channel_id=1, source_target_pairs={{0,8},{1,9},{2,10},{3,11},{4,12},{5,13},{6,14},{7,15},{8,0},{9,1},... | collective-permute-start | bytes 737288 | tf_op jit(solution)/shard_map/ppermute | solution.py:29
  20.2 9.8 %collective-permute-start.7 = (bf16[256,384]{1,0:T(8,128)(2,1)}, bf16[256,384]{1,0:T(8,128)(2,1)S(1)}, u32[]{:S(2)}, u32[]{:S(2)}) collective-permute-start(bf16[256,384]{1,0:T(8,128)(2,1)} %shard_map.221.refs_8_), channel_id=1, source_target_pairs={{0,1},{1,0},{2,3},{3,2},{4,5},{5,4},{6,7},{7,6},{8,9},{9,8},{10,11... | collective-permute-start | bytes 589832 | tf_op jit(solution)/shard_map/ppermute | solution.py:29
  24.6 6.8 %collective-permute-start.3 = (bf16[128,960]{1,0:T(8,128)(2,1)S(1)}, bf16[128,960]{1,0:T(8,128)(2,1)S(1)}, u32[]{:S(2)}, u32[]{:S(2)}) collective-permute-start(bf16[128,960]{1,0:T(8,128)(2,1)S(1)} %copy.55.refs_0_), channel_id=1, source_target_pairs={{0,4},{1,5},{2,6},{3,7},{4,0},{5,1},{6,2},{7,3},{8,12},{9,13},{10,... | collective-permute-start | bytes 737288 | tf_op jit(solution)/shard_map/ppermute | solution.py:29
  24.7 6.8 %collective-permute-start.4 = (bf16[128,960]{1,0:T(8,128)(2,1)}, bf16[128,960]{1,0:T(8,128)(2,1)S(1)}, u32[]{:S(2)}, u32[]{:S(2)}) collective-permute-start(bf16[128,960]{1,0:T(8,128)(2,1)} %collective-permute-done.refs_2_), channel_id=1, source_target_pairs={{0,4},{1,5},{2,6},{3,7},{4,0},{5,1},{6,2},{7,3},{8,12},{9,13},{10,... | collective-permute-start | bytes 737288 | tf_op jit(solution)/shard_map/ppermute | solution.py:29
  25.2 6.3 %collective-permute-start.5 = (bf16[128,960]{1,0:T(8,128)(2,1)}, bf16[128,960]{1,0:T(8,128)(2,1)S(1)}, u32[]{:S(2)}, u32[]{:S(2)}) collective-permute-start(bf16[128,960]{1,0:T(8,128)(2,1)} %collective-permute-done.1.refs_4_), channel_id=1, source_target_pairs={{0,4},{1,5},{2,6},{3,7},{4,0},{5,1},{6,2},{7,3},{8,12},{9,13},{10,... | collective-permute-start | bytes 737288 | tf_op jit(solution)/shard_map/ppermute | solution.py:29
  26.9 4.7 %collective-permute-start.6 = (bf16[128,960]{1,0:T(8,128)(2,1)S(1)}, bf16[128,960]{1,0:T(8,128)(2,1)S(1)}, u32[]{:S(2)}, u32[]{:S(2)}) collective-permute-start(bf16[128,960]{1,0:T(8,128)(2,1)S(1)} %collective-permute-done.2.refs_6_), channel_id=1, source_target_pairs={{0,4},{1,5},{2,6},{3,7},{4,0},{5,1},{6,2},{7,3},{8,12},{9,13},{10,... | collective-permute-start | bytes 737288 | tf_op jit(solution)/shard_map/ppermute | solution.py:29
  30.0 9.4 %collective-permute-start.10 = (bf16[64,960]{1,0:T(8,128)(2,1)S(1)}, bf16[64,960]{1,0:T(8,128)(2,1)S(1)}, u32[]{:S(2)}, u32[]{:S(2)}) collective-permute-start(bf16[64,960]{1,0:T(8,128)(2,1)S(1)} %get-tuple-element.167), channel_id=1, source_target_pairs={{0,2},{1,3},{2,0},{3,1},{4,6},{5,7},{6,4},{7,5},{8,10},{9,11},{10,... | collective-permute-start | bytes 368648 | tf_op jit(solution)/shard_map/ppermute | solution.py:29
  39.4 27.8 %collective-permute-start.12 = (bf16[256,1024]{1,0:T(8,128)(2,1)}, bf16[256,1024]{1,0:T(8,128)(2,1)S(1)}, u32[]{:S(2)}, u32[]{:S(2)}) collective-permute-start(bf16[256,1024]{1,0:T(8,128)(2,1)} %get-tuple-element.170.refs_8_), channel_id=1, source_target_pairs={{0,16},{1,17},{2,18},{3,19},{4,20},{5,21},{6,22},{7,23},{8,24},{9,... | collective-permute-start | bytes 1572872 | tf_op jit(solution)/shard_map/ppermute | solution.py:29
  41.0 26.3 %collective-permute-start.11 = (bf16[256,1024]{1,0:T(8,128)(2,1)}, bf16[256,1024]{1,0:T(8,128)(2,1)S(1)}, u32[]{:S(2)}, u32[]{:S(2)}) collective-permute-start(bf16[256,1024]{1,0:T(8,128)(2,1)} %get-tuple-element.170.refs_8_), channel_id=1, source_target_pairs={{0,8},{1,9},{2,10},{3,11},{4,12},{5,13},{6,14},{7,15},{8,0},{9,1},... | collective-permute-start | bytes 1572872 | tf_op jit(solution)/shard_map/ppermute | solution.py:29
  42.0 11.3 %collective-permute-start.15 = (bf16[1024,128]{1,0:T(8,128)(2,1)}, bf16[1024,128]{1,0:T(8,128)(2,1)S(1)}, u32[]{:S(2)}, u32[]{:S(2)}) collective-permute-start(bf16[1024,128]{1,0:T(8,128)(2,1)} %get-tuple-element.172.refs_0_), channel_id=1, source_target_pairs={{0,3},{1,2},{2,1},{3,0},{4,7},{5,6},{6,5},{7,4},{8,11},{9,10},{10,... | collective-permute-start | bytes 786440 | tf_op jit(solution)/shard_map/ppermute | solution.py:29
  43.8 23.5 %collective-permute-start.14 = (bf16[1024,128]{1,0:T(8,128)(2,1)}, bf16[1024,128]{1,0:T(8,128)(2,1)}, u32[]{:S(2)}, u32[]{:S(2)}) collective-permute-start(bf16[1024,128]{1,0:T(8,128)(2,1)} %get-tuple-element.172.refs_0_), channel_id=1, source_target_pairs={{0,2},{1,3},{2,0},{3,1},{4,6},{5,7},{6,4},{7,5},{8,10},{9,11},{10,... | collective-permute-start | bytes 786440 | tf_op jit(solution)/shard_map/ppermute | solution.py:29
  44.2 23.0 %collective-permute-start.13 = (bf16[1024,128]{1,0:T(8,128)(2,1)}, bf16[1024,128]{1,0:T(8,128)(2,1)S(1)}, u32[]{:S(2)}, u32[]{:S(2)}) collective-permute-start(bf16[1024,128]{1,0:T(8,128)(2,1)} %get-tuple-element.172.refs_0_), channel_id=1, source_target_pairs={{0,1},{1,0},{2,3},{3,2},{4,5},{5,4},{6,7},{7,6},{8,9},{9,8},{10,11... | collective-permute-start | bytes 786440 | tf_op jit(solution)/shard_map/ppermute | solution.py:29
  67.3 4.4 %collective-permute-start.16 = (bf16[1024,128]{1,0:T(8,128)(2,1)}, bf16[1024,128]{1,0:T(8,128)(2,1)S(1)}, u32[]{:S(2)}, u32[]{:S(2)}) collective-permute-start(bf16[1024,128]{1,0:T(8,128)(2,1)} %get-tuple-element.172.refs_0_), channel_id=1, source_target_pairs={{0,4},{1,5},{2,6},{3,7},{4,0},{5,1},{6,2},{7,3},{8,12},{9,13},{10,... | collective-permute-start | bytes 786440 | tf_op jit(solution)/shard_map/ppermute | solution.py:29
  67.4 6.0 %collective-permute-start.17 = (bf16[1024,128]{1,0:T(8,128)(2,1)S(1)}, bf16[1024,128]{1,0:T(8,128)(2,1)}, u32[]{:S(2)}, u32[]{:S(2)}) collective-permute-start(bf16[1024,128]{1,0:T(8,128)(2,1)S(1)} %collective-permute-done.13.refs_1_), channel_id=1, source_target_pairs={{0,4},{1,5},{2,6},{3,7},{4,0},{5,1},{6,2},{7,3},{8,12},{9,13},{10,... | collective-permute-start | bytes 786440 | tf_op jit(solution)/shard_map/ppermute | solution.py:29
  67.8 5.5 %collective-permute-start.18 = (bf16[1024,128]{1,0:T(8,128)(2,1)}, bf16[1024,128]{1,0:T(8,128)(2,1)}, u32[]{:S(2)}, u32[]{:S(2)}) collective-permute-start(bf16[1024,128]{1,0:T(8,128)(2,1)} %collective-permute-done.14.refs_2_), channel_id=1, source_target_pairs={{0,4},{1,5},{2,6},{3,7},{4,0},{5,1},{6,2},{7,3},{8,12},{9,13},{10,... | collective-permute-start | bytes 786440 | tf_op jit(solution)/shard_map/ppermute | solution.py:29
  67.9 7.3 %collective-permute-start.19 = (bf16[1024,128]{1,0:T(8,128)(2,1)S(1)}, bf16[1024,128]{1,0:T(8,128)(2,1)}, u32[]{:S(2)}, u32[]{:S(2)}) collective-permute-start(bf16[1024,128]{1,0:T(8,128)(2,1)S(1)} %collective-permute-done.15.refs_3_), channel_id=1, source_target_pairs={{0,4},{1,5},{2,6},{3,7},{4,0},{5,1},{6,2},{7,3},{8,12},{9,13},{10,... | collective-permute-start | bytes 786440 | tf_op jit(solution)/shard_map/ppermute | solution.py:29
  70.7 23.7 %collective-permute-start.23 = (bf16[768,1024]{1,0:T(8,128)(2,1)}, bf16[768,1024]{1,0:T(8,128)(2,1)}, u32[]{:S(2)}, u32[]{:S(2)}) collective-permute-start(bf16[768,1024]{1,0:T(8,128)(2,1)} %pad_maximum_fusion.1), channel_id=1, source_target_pairs={{0,4},{1,5},{2,6},{3,7},{4,0},{5,1},{6,2},{7,3},{8,12},{9,13},{10,... | collective-permute-start | bytes 4718600 | tf_op jit(solution)/shard_map/ppermute | solution.py:29
  72.4 22.0 %collective-permute-start.22 = (bf16[256,1024]{1,0:T(8,128)(2,1)S(1)}, bf16[256,1024]{1,0:T(8,128)(2,1)S(1)}, u32[]{:S(2)}, u32[]{:S(2)}) collective-permute-start(bf16[256,1024]{1,0:T(8,128)(2,1)S(1)} %collective-permute-done.11.refs_9_), channel_id=1, source_target_pairs={{0,16},{1,17},{2,18},{3,19},{4,20},{5,21},{6,22},{7,23},{8,24},{9,... | collective-permute-start | bytes 1572872 | tf_op jit(solution)/shard_map/ppermute | solution.py:29
  73.3 18.1 %collective-permute-start.20 = (bf16[176,960]{1,0:T(8,128)(2,1)S(1)}, bf16[176,960]{1,0:T(8,128)(2,1)S(1)}, u32[]{:S(2)}, u32[]{:S(2)}) collective-permute-start(bf16[176,960]{1,0:T(8,128)(2,1)S(1)} %get-tuple-element.182), channel_id=1, source_target_pairs={{0,2},{1,3},{2,0},{3,1},{4,6},{5,7},{6,4},{7,5},{8,10},{9,11},{10,... | collective-permute-start | bytes 1013768 | tf_op jit(solution)/shard_map/ppermute | solution.py:29
  73.4 21.1 %collective-permute-start.21 = (bf16[240,960]{1,0:T(8,128)(2,1)S(1)}, bf16[240,960]{1,0:T(8,128)(2,1)S(1)}, u32[]{:S(2)}, u32[]{:S(2)}) collective-permute-start(bf16[240,960]{1,0:T(8,128)(2,1)S(1)} %get-tuple-element.183.refs_14_), channel_id=1, source_target_pairs={{0,1},{1,0},{2,3},{3,2},{4,5},{5,4},{6,7},{7,6},{8,9},{9,8},{10,11... | collective-permute-start | bytes 1382408 | tf_op jit(solution)/shard_map/ppermute | solution.py:29
  94.4 14.4 %collective-permute-start.25 = (bf16[176,960]{1,0:T(8,128)(2,1)S(1)}, bf16[176,960]{1,0:T(8,128)(2,1)S(1)}, u32[]{:S(2)}, u32[]{:S(2)}) collective-permute-start(bf16[176,960]{1,0:T(8,128)(2,1)S(1)} %collective-permute-done.20.refs_17_), channel_id=1, source_target_pairs={{0,1},{1,0},{2,3},{3,2},{4,5},{5,4},{6,7},{7,6},{8,9},{9,8},{10,11... | collective-permute-start | bytes 1013768 | tf_op jit(solution)/shard_map/ppermute | solution.py:29
  94.7 12.2 %collective-permute-start.28 = (bf16[1024,128]{1,0:T(8,128)(2,1)S(1)}, bf16[1024,128]{1,0:T(8,128)(2,1)S(1)}, u32[]{:S(2)}, u32[]{:S(2)}) collective-permute-start(bf16[1024,128]{1,0:T(8,128)(2,1)S(1)} %get-tuple-element.190.refs_0_), channel_id=1, source_target_pairs={{0,24},{1,25},{2,26},{3,27},{4,28},{5,29},{6,30},{7,31},{8,16},{9,... | collective-permute-start | bytes 786440 | tf_op jit(solution)/shard_map/ppermute | solution.py:29
  96.2 12.6 %collective-permute-start.27 = (bf16[1024,128]{1,0:T(8,128)(2,1)S(1)}, bf16[1024,128]{1,0:T(8,128)(2,1)S(1)}, u32[]{:S(2)}, u32[]{:S(2)}) collective-permute-start(bf16[1024,128]{1,0:T(8,128)(2,1)S(1)} %get-tuple-element.190.refs_0_), channel_id=1, source_target_pairs={{0,16},{1,17},{2,18},{3,19},{4,20},{5,21},{6,22},{7,23},{8,24},{9,... | collective-permute-start | bytes 786440 | tf_op jit(solution)/shard_map/ppermute | solution.py:29
  96.7 12.1 %collective-permute-start.26 = (bf16[1024,128]{1,0:T(8,128)(2,1)S(1)}, bf16[1024,128]{1,0:T(8,128)(2,1)S(1)}, u32[]{:S(2)}, u32[]{:S(2)}) collective-permute-start(bf16[1024,128]{1,0:T(8,128)(2,1)S(1)} %get-tuple-element.190.refs_0_), channel_id=1, source_target_pairs={{0,8},{1,9},{2,10},{3,11},{4,12},{5,13},{6,14},{7,15},{8,0},{9,1},... | collective-permute-start | bytes 786440 | tf_op jit(solution)/shard_map/ppermute | solution.py:29
  98.2 8.7 %collective-permute-start.24 = (bf16[64,960]{1,0:T(8,128)(2,1)S(1)}, bf16[64,960]{1,0:T(8,128)(2,1)S(1)}, u32[]{:S(2)}, u32[]{:S(2)}) collective-permute-start(bf16[64,960]{1,0:T(8,128)(2,1)S(1)} %collective-permute-done.10.refs_16_), channel_id=1, source_target_pairs={{0,1},{1,0},{2,3},{3,2},{4,5},{5,4},{6,7},{7,6},{8,9},{9,8},{10,11... | collective-permute-start | bytes 368648 | tf_op jit(solution)/shard_map/ppermute | solution.py:29
  108.8 3.4 %collective-permute-start.33 = (bf16[256,1024]{1,0:T(8,128)(2,1)S(1)}, bf16[256,1024]{1,0:T(8,128)(2,1)S(1)}, u32[]{:S(2)}, u32[]{:S(2)}) collective-permute-start(bf16[256,1024]{1,0:T(8,128)(2,1)S(1)} %collective-permute-done.22.refs_11_), channel_id=1, source_target_pairs={{0,4},{1,5},{2,6},{3,7},{4,0},{5,1},{6,2},{7,3},{8,12},{9,13},{10,... | collective-permute-start | bytes 1572872 | tf_op jit(solution)/shard_map/ppermute | solution.py:29
  131.7 2.9 %collective-permute-start.34 = (bf16[512,1024]{1,0:T(8,128)(2,1)}, bf16[512,1024]{1,0:T(8,128)(2,1)S(1)}, u32[]{:S(2)}, u32[]{:S(2)}) collective-permute-start(bf16[512,1024]{1,0:T(8,128)(2,1)} %get-tuple-element.203), channel_id=1, source_target_pairs={{0,4},{1,5},{2,6},{3,7},{4,0},{5,1},{6,2},{7,3},{8,12},{9,13},{10,... | collective-permute-start | bytes 3145736 | tf_op jit(solution)/shard_map/ppermute | solution.py:29
  136.0 15.6 %collective-permute-start.35 = (bf16[240,960]{1,0:T(8,128)(2,1)S(1)}, bf16[240,960]{1,0:T(8,128)(2,1)S(1)}, u32[]{:S(2)}, u32[]{:S(2)}) collective-permute-start(bf16[240,960]{1,0:T(8,128)(2,1)S(1)} %get-tuple-element.205), channel_id=1, source_target_pairs={{0,1},{1,0},{2,3},{3,2},{4,5},{5,4},{6,7},{7,6},{8,9},{9,8},{10,11... | collective-permute-start | bytes 1382408 | tf_op jit(solution)/shard_map/ppermute | solution.py:29
  137.5 9.2 %collective-permute-start.36 = (bf16[128,960]{1,0:T(8,128)(2,1)S(1)}, bf16[128,960]{1,0:T(8,128)(2,1)S(1)}, u32[]{:S(2)}, u32[]{:S(2)}) collective-permute-start(bf16[128,960]{1,0:T(8,128)(2,1)S(1)} %get-tuple-element.206), channel_id=1, source_target_pairs={{0,8},{1,9},{2,10},{3,11},{4,12},{5,13},{6,14},{7,15},{8,0},{9,1},... | collective-permute-start | bytes 737288 | tf_op jit(solution)/shard_map/ppermute | solution.py:29
  138.2 12.4 %collective-permute-start.37 = (bf16[128,960]{1,0:T(8,128)(2,1)S(1)}, bf16[128,960]{1,0:T(8,128)(2,1)S(1)}, u32[]{:S(2)}, u32[]{:S(2)}) collective-permute-start(bf16[128,960]{1,0:T(8,128)(2,1)S(1)} %get-tuple-element.207), channel_id=1, source_target_pairs={{0,16},{1,17},{2,18},{3,19},{4,20},{5,21},{6,22},{7,23},{8,24},{9,... | collective-permute-start | bytes 737288 | tf_op jit(solution)/shard_map/ppermute | solution.py:29
  139.6 12.0 %collective-permute-start.38 = (bf16[128,960]{1,0:T(8,128)(2,1)S(1)}, bf16[128,960]{1,0:T(8,128)(2,1)S(1)}, u32[]{:S(2)}, u32[]{:S(2)}) collective-permute-start(bf16[128,960]{1,0:T(8,128)(2,1)S(1)} %get-tuple-element.208), channel_id=1, source_target_pairs={{0,24},{1,25},{2,26},{3,27},{4,28},{5,29},{6,30},{7,31},{8,16},{9,... | collective-permute-start | bytes 737288 | tf_op jit(solution)/shard_map/ppermute | solution.py:29
  151.6 3.2 %collective-permute-start.40 = (bf16[512,1024]{1,0:T(8,128)(2,1)S(1)}, bf16[512,1024]{1,0:T(8,128)(2,1)S(1)}, u32[]{:S(2)}, u32[]{:S(2)}) collective-permute-start(bf16[512,1024]{1,0:T(8,128)(2,1)S(1)} %copy-done.34), channel_id=1, source_target_pairs={{0,4},{1,5},{2,6},{3,7},{4,0},{5,1},{6,2},{7,3},{8,12},{9,13},{10,... | collective-permute-start | bytes 3145736 | tf_op jit(solution)/shard_map/ppermute | solution.py:29
  154.8 13.5 %collective-permute-start.41 = (bf16[240,960]{1,0:T(8,128)(2,1)S(1)}, bf16[240,960]{1,0:T(8,128)(2,1)S(1)}, u32[]{:S(2)}, u32[]{:S(2)}) collective-permute-start(bf16[240,960]{1,0:T(8,128)(2,1)S(1)} %get-tuple-element.224), channel_id=1, source_target_pairs={{0,1},{1,0},{2,3},{3,2},{4,5},{5,4},{6,7},{7,6},{8,9},{9,8},{10,11... | collective-permute-start | bytes 1382408 | tf_op jit(solution)/shard_map/ppermute | solution.py:29
  155.4 5.9 %collective-permute-start.42 = (bf16[256,256]{1,0:T(8,128)(2,1)S(1)}, bf16[256,256]{1,0:T(8,128)(2,1)S(1)}, u32[]{:S(2)}, u32[]{:S(2)}) collective-permute-start(bf16[256,256]{1,0:T(8,128)(2,1)S(1)} %get-tuple-element.225), channel_id=1, source_target_pairs={{0,8},{1,9},{2,10},{3,11},{4,12},{5,13},{6,14},{7,15},{8,0},{9,1},... | collective-permute-start | bytes 393224 | tf_op jit(solution)/shard_map/ppermute | solution.py:29
  157.0 8.0 %collective-permute-start.43 = (bf16[256,256]{1,0:T(8,128)(2,1)S(1)}, bf16[256,256]{1,0:T(8,128)(2,1)S(1)}, u32[]{:S(2)}, u32[]{:S(2)}) collective-permute-start(bf16[256,256]{1,0:T(8,128)(2,1)S(1)} %get-tuple-element.226), channel_id=1, source_target_pairs={{0,16},{1,17},{2,18},{3,19},{4,20},{5,21},{6,22},{7,23},{8,24},{9,... | collective-permute-start | bytes 393224 | tf_op jit(solution)/shard_map/ppermute | solution.py:29
  157.8 7.2 %collective-permute-start.44 = (bf16[256,256]{1,0:T(8,128)(2,1)S(1)}, bf16[256,256]{1,0:T(8,128)(2,1)S(1)}, u32[]{:S(2)}, u32[]{:S(2)}) collective-permute-start(bf16[256,256]{1,0:T(8,128)(2,1)S(1)} %get-tuple-element.227), channel_id=1, source_target_pairs={{0,24},{1,25},{2,26},{3,27},{4,28},{5,29},{6,30},{7,31},{8,16},{9,... | collective-permute-start | bytes 393224 | tf_op jit(solution)/shard_map/ppermute | solution.py:29
  168.3 22.7 %collective-permute-start.46 = (bf16[128,960]{1,0:T(8,128)(2,1)S(1)}, bf16[128,960]{1,0:T(8,128)(2,1)S(1)}, u32[]{:S(2)}, u32[]{:S(2)}) collective-permute-start(bf16[128,960]{1,0:T(8,128)(2,1)S(1)} %get-tuple-element.239), channel_id=1, source_target_pairs={{0,8},{1,9},{2,10},{3,11},{4,12},{5,13},{6,14},{7,15},{8,0},{9,1},... | collective-permute-start | bytes 737288 | tf_op jit(solution)/shard_map/ppermute | solution.py:29
  169.8 21.2 %collective-permute-start.47 = (bf16[128,960]{1,0:T(8,128)(2,1)S(1)}, bf16[128,960]{1,0:T(8,128)(2,1)S(1)}, u32[]{:S(2)}, u32[]{:S(2)}) collective-permute-start(bf16[128,960]{1,0:T(8,128)(2,1)S(1)} %get-tuple-element.241), channel_id=1, source_target_pairs={{0,16},{1,17},{2,18},{3,19},{4,20},{5,21},{6,22},{7,23},{8,24},{9,... | collective-permute-start | bytes 737288 | tf_op jit(solution)/shard_map/ppermute | solution.py:29
  170.6 20.4 %collective-permute-start.48 = (bf16[128,960]{1,0:T(8,128)(2,1)S(1)}, bf16[128,960]{1,0:T(8,128)(2,1)S(1)}, u32[]{:S(2)}, u32[]{:S(2)}) collective-permute-start(bf16[128,960]{1,0:T(8,128)(2,1)S(1)} %get-tuple-element.243), channel_id=1, source_target_pairs={{0,24},{1,25},{2,26},{3,27},{4,28},{5,29},{6,30},{7,31},{8,16},{9,... | collective-permute-start | bytes 737288 | tf_op jit(solution)/shard_map/ppermute | solution.py:29
  171.8 23.3 %collective-permute-start.45 = (bf16[240,960]{1,0:T(8,128)(2,1)S(1)}, bf16[240,960]{1,0:T(8,128)(2,1)S(1)}, u32[]{:S(2)}, u32[]{:S(2)}) collective-permute-start(bf16[240,960]{1,0:T(8,128)(2,1)S(1)} %shard_map.231), channel_id=1, source_target_pairs={{0,2},{1,3},{2,0},{3,1},{4,6},{5,7},{6,4},{7,5},{8,10},{9,11},{10,... | collective-permute-start | bytes 1382408 | tf_op jit(solution)/shard_map/ppermute | solution.py:29
  195.1 2.7 collective-permute-start.49
  198.2 23.7 %collective-permute-start.51 = (bf16[240,1024]{1,0:T(8,128)(2,1)S(1)}, bf16[240,1024]{1,0:T(8,128)(2,1)S(1)}, u32[]{:S(2)}, u32[]{:S(2)}) collective-permute-start(bf16[240,1024]{1,0:T(8,128)(2,1)S(1)} %shard_map.234.m_ref), channel_id=1, source_target_pairs={{0,16},{1,17},{2,18},{3,19},{4,20},{5,21},{6,22},{7,23},{8,24},{9,... | collective-permute-start | bytes 1474568 | tf_op jit(solution)/shard_map/ppermute | solution.py:29
  199.7 22.2 %collective-permute-start.50 = (bf16[240,1024]{1,0:T(8,128)(2,1)S(1)}, bf16[240,1024]{1,0:T(8,128)(2,1)S(1)}, u32[]{:S(2)}, u32[]{:S(2)}) collective-permute-start(bf16[240,1024]{1,0:T(8,128)(2,1)S(1)} %shard_map.234.m_ref), channel_id=1, source_target_pairs={{0,8},{1,9},{2,10},{3,11},{4,12},{5,13},{6,14},{7,15},{8,0},{9,1},... | collective-permute-start | bytes 1474568 | tf_op jit(solution)/shard_map/ppermute | solution.py:29
  200.5 21.4 %collective-permute-start.52 = (bf16[1024,128]{1,0:T(8,128)(2,1)S(1)}, bf16[1024,128]{1,0:T(8,128)(2,1)S(1)}, u32[]{:S(2)}, u32[]{:S(2)}) collective-permute-start(bf16[1024,128]{1,0:T(8,128)(2,1)S(1)} %get-tuple-element.245), channel_id=1, source_target_pairs={{0,1},{1,0},{2,3},{3,2},{4,5},{5,4},{6,7},{7,6},{8,9},{9,8},{10,11... | collective-permute-start | bytes 786440 | tf_op jit(solution)/shard_map/ppermute | solution.py:29
  200.5 21.4 %collective-permute-start.53 = (bf16[1024,128]{1,0:T(8,128)(2,1)S(1)}, bf16[1024,128]{1,0:T(8,128)(2,1)S(1)}, u32[]{:S(2)}, u32[]{:S(2)}) collective-permute-start(bf16[1024,128]{1,0:T(8,128)(2,1)S(1)} %get-tuple-element.256), channel_id=1, source_target_pairs={{0,2},{1,3},{2,0},{3,1},{4,6},{5,7},{6,4},{7,5},{8,10},{9,11},{10,... | collective-permute-start | bytes 786440 | tf_op jit(solution)/shard_map/ppermute | solution.py:29
  203.2 18.7 %collective-permute-start.54 = (bf16[1024,128]{1,0:T(8,128)(2,1)S(1)}, bf16[1024,128]{1,0:T(8,128)(2,1)S(1)}, u32[]{:S(2)}, u32[]{:S(2)}) collective-permute-start(bf16[1024,128]{1,0:T(8,128)(2,1)S(1)} %get-tuple-element.257), channel_id=1, source_target_pairs={{0,3},{1,2},{2,1},{3,0},{4,7},{5,6},{6,5},{7,4},{8,11},{9,10},{10,... | collective-permute-start | bytes 786440 | tf_op jit(solution)/shard_map/ppermute | solution.py:29
  225.7 2.7 collective-permute-start.55
  225.7 26.1 %collective-permute-start.56 = (bf16[240,1024]{1,0:T(8,128)(2,1)S(1)}, bf16[240,1024]{1,0:T(8,128)(2,1)S(1)}, u32[]{:S(2)}, u32[]{:S(2)}) collective-permute-start(bf16[240,1024]{1,0:T(8,128)(2,1)S(1)} %collective-permute-done.50.x_ref), channel_id=1, source_target_pairs={{0,16},{1,17},{2,18},{3,19},{4,20},{5,21},{6,22},{7,23},{8,24},{9,... | collective-permute-start | bytes 1474568 | tf_op jit(solution)/shard_map/ppermute | solution.py:29
  228.6 23.2 %collective-permute-start.57 = (bf16[256,960]{1,0:T(8,128)(2,1)S(1)}, bf16[256,960]{1,0:T(8,128)(2,1)S(1)}, u32[]{:S(2)}, u32[]{:S(2)}) collective-permute-start(bf16[256,960]{1,0:T(8,128)(2,1)S(1)} %get-tuple-element.273), channel_id=1, source_target_pairs={{0,16},{1,17},{2,18},{3,19},{4,20},{5,21},{6,22},{7,23},{8,24},{9,... | collective-permute-start | bytes 1474568 | tf_op jit(solution)/shard_map/ppermute | solution.py:29
  229.9 13.0 %collective-permute-start.58 = (bf16[256,384]{1,0:T(8,128)(2,1)S(1)}, bf16[256,384]{1,0:T(8,128)(2,1)S(1)}, u32[]{:S(2)}, u32[]{:S(2)}) collective-permute-start(bf16[256,384]{1,0:T(8,128)(2,1)S(1)} %get-tuple-element.274), channel_id=1, source_target_pairs={{0,1},{1,0},{2,3},{3,2},{4,5},{5,4},{6,7},{7,6},{8,9},{9,8},{10,11... | collective-permute-start | bytes 589832 | tf_op jit(solution)/shard_map/ppermute | solution.py:29
  234.7 17.2 %collective-permute-start.59 = (bf16[256,384]{1,0:T(8,128)(2,1)S(1)}, bf16[256,384]{1,0:T(8,128)(2,1)S(1)}, u32[]{:S(2)}, u32[]{:S(2)}) collective-permute-start(bf16[256,384]{1,0:T(8,128)(2,1)S(1)} %get-tuple-element.275), channel_id=1, source_target_pairs={{0,2},{1,3},{2,0},{3,1},{4,6},{5,7},{6,4},{7,5},{8,10},{9,11},{10,... | collective-permute-start | bytes 589832 | tf_op jit(solution)/shard_map/ppermute | solution.py:29
  235.4 16.5 %collective-permute-start.60 = (bf16[256,384]{1,0:T(8,128)(2,1)S(1)}, bf16[256,384]{1,0:T(8,128)(2,1)S(1)}, u32[]{:S(2)}, u32[]{:S(2)}) collective-permute-start(bf16[256,384]{1,0:T(8,128)(2,1)S(1)} %get-tuple-element.276), channel_id=1, source_target_pairs={{0,3},{1,2},{2,1},{3,0},{4,7},{5,6},{6,5},{7,4},{8,11},{9,10},{10,... | collective-permute-start | bytes 589832 | tf_op jit(solution)/shard_map/ppermute | solution.py:29
  252.0 4.4 %collective-permute-start.62 = (bf16[960,1024]{1,0:T(8,128)(2,1)S(1)}, bf16[960,1024]{1,0:T(8,128)(2,1)S(1)}, u32[]{:S(2)}, u32[]{:S(2)}) collective-permute-start(bf16[960,1024]{1,0:T(8,128)(2,1)S(1)} %pad_maximum_fusion), channel_id=1, source_target_pairs={{0,4},{1,5},{2,6},{3,7},{4,0},{5,1},{6,2},{7,3},{8,12},{9,13},{10,... | collective-permute-start | bytes 5898248 | tf_op jit(solution)/shard_map/ppermute | solution.py:29
  252.2 9.9 %collective-permute-start.65 = (bf16[256,384]{1,0:T(8,128)(2,1)S(1)}, bf16[256,384]{1,0:T(8,128)(2,1)S(1)}, u32[]{:S(2)}, u32[]{:S(2)}) collective-permute-start(bf16[256,384]{1,0:T(8,128)(2,1)S(1)} %add_convert_fusion.refs_0_), channel_id=1, source_target_pairs={{0,24},{1,25},{2,26},{3,27},{4,28},{5,29},{6,30},{7,31},{8,16},{9,... | collective-permute-start | bytes 589832 | tf_op jit(solution)/shard_map/ppermute | solution.py:29
  253.7 10.9 %collective-permute-start.64 = (bf16[256,384]{1,0:T(8,128)(2,1)S(1)}, bf16[256,384]{1,0:T(8,128)(2,1)S(1)}, u32[]{:S(2)}, u32[]{:S(2)}) collective-permute-start(bf16[256,384]{1,0:T(8,128)(2,1)S(1)} %add_convert_fusion.refs_0_), channel_id=1, source_target_pairs={{0,16},{1,17},{2,18},{3,19},{4,20},{5,21},{6,22},{7,23},{8,24},{9,... | collective-permute-start | bytes 589832 | tf_op jit(solution)/shard_map/ppermute | solution.py:29
  254.3 10.4 %collective-permute-start.63 = (bf16[256,384]{1,0:T(8,128)(2,1)S(1)}, bf16[256,384]{1,0:T(8,128)(2,1)S(1)}, u32[]{:S(2)}, u32[]{:S(2)}) collective-permute-start(bf16[256,384]{1,0:T(8,128)(2,1)S(1)} %add_convert_fusion.refs_0_), channel_id=1, source_target_pairs={{0,8},{1,9},{2,10},{3,11},{4,12},{5,13},{6,14},{7,15},{8,0},{9,1},... | collective-permute-start | bytes 589832 | tf_op jit(solution)/shard_map/ppermute | solution.py:29
  255.8 13.8 %collective-permute-start.61 = (bf16[128,960]{1,0:T(8,128)(2,1)S(1)}, bf16[128,960]{1,0:T(8,128)(2,1)S(1)}, u32[]{:S(2)}, u32[]{:S(2)}) collective-permute-start(bf16[128,960]{1,0:T(8,128)(2,1)S(1)} %get-tuple-element.279), channel_id=1, source_target_pairs={{0,8},{1,9},{2,10},{3,11},{4,12},{5,13},{6,14},{7,15},{8,0},{9,1},... | collective-permute-start | bytes 737288 | tf_op jit(solution)/shard_map/ppermute | solution.py:29
  269.7 3.1 %collective-permute-start.66 = (bf16[256,384]{1,0:T(8,128)(2,1)S(1)}, bf16[256,384]{1,0:T(8,128)(2,1)S(1)}, u32[]{:S(2)}, u32[]{:S(2)}) collective-permute-start(bf16[256,384]{1,0:T(8,128)(2,1)S(1)} %add_convert_fusion.refs_0_), channel_id=1, source_target_pairs={{0,4},{1,5},{2,6},{3,7},{4,0},{5,1},{6,2},{7,3},{8,12},{9,13},{10,... | collective-permute-start | bytes 589832 | tf_op jit(solution)/shard_map/ppermute | solution.py:29
  269.7 3.1 %collective-permute-start.67 = (bf16[256,384]{1,0:T(8,128)(2,1)S(1)}, bf16[256,384]{1,0:T(8,128)(2,1)S(1)}, u32[]{:S(2)}, u32[]{:S(2)}) collective-permute-start(bf16[256,384]{1,0:T(8,128)(2,1)S(1)} %collective-permute-done.63.refs_2_), channel_id=1, source_target_pairs={{0,4},{1,5},{2,6},{3,7},{4,0},{5,1},{6,2},{7,3},{8,12},{9,13},{10,... | collective-permute-start | bytes 589832 | tf_op jit(solution)/shard_map/ppermute | solution.py:29
  270.2 2.6 collective-permute-start.69
  (48 other events, 538.0 us)

commit v2 on v1

--- a/solution.py
+++ b/solution.py
@@ -45,25 +45,24 @@
     return jax.ShapeDtypeStruct(dims, dtype)
 
 
-def call(kernel, outs, inputs, scalars=1, scratch=(), limit=56, cost=1.0, far=()):
+def call(kernel, outs, inputs, scalars=1, scratch=(), limit=56, cost=1.0, far=(), far_out=()):
     specs = [smem] * scalars + [vmem] * (len(inputs) - scalars)
     for i in far:
         specs[i] = pl.BlockSpec(memory_space=pltpu.HBM)
+    out_specs = [vmem for unused in outs]
+    for i in far_out:
+        out_specs[i] = pl.BlockSpec(memory_space=pltpu.HBM)
     return pl.pallas_call(
         kernel,
         out_shape=tuple(outs),
         in_specs=specs,
-        out_specs=tuple(vmem for unused in outs),
+        out_specs=tuple(out_specs),
         scratch_shapes=list(scratch),
         compiler_params=pltpu.CompilerParams(vmem_limit_bytes=limit * MIB),
         cost_estimate=pl.CostEstimate(
             flops=int(cost * 1e9), bytes_accessed=int(cost * 1e6), transcendentals=0
         ),
     )(*inputs)
-
-
-def early_rows(rows):
-    return rows // 4 // 16 * 16 + 16
 
 
 def one_hot(rows, columns, start):
@@ -178,40 +177,38 @@
     part = ff_z // TP
     own = part * nz
 
-    upper = early_rows(d_rows)
-    lower = d_rows - upper
-
-    def kernel(at_ref, g_ref, u_ref, d_ref, out_ref, upper_ref, lower_ref):
+
+    def kernel(at_ref, g_ref, u_ref, d_ref, out_ref):
         pick = one_hot(ff_z, part, at_ref[0] * part)
         for ref, start in ((g_ref, 0), (u_ref, own)):
             pieces = [nn(ref[:, pl.ds(s * ff_z, ff_z)], pick) for s in range(nz)]
             out_ref[:, pl.ds(start, own)] = jnp.concatenate(pieces, axis=1).astype(bf16)
         pieces = [nn(d_ref[pl.ds(s * d_rows, d_rows), :], pick) for s in range(nz)]
         out_ref[:, pl.ds(2 * own, own)] = jnp.concatenate(pieces, axis=1).astype(bf16)
-        upper_ref[...] = out_ref[pl.ds(0, upper), :]
-        lower_ref[...] = out_ref[pl.ds(upper, lower), :]
-
-    return call(
-        kernel,
-        [shape((rows, 3 * own), bf16) for rows in (d_rows, upper, lower)],
+
+    return call(
+        kernel,
+        [shape((d_rows, 3 * own), bf16)],
         [at, w_gate, w_up, w_down.T],
         limit=16,
         cost=4.0,
-    )
-
-
-def project(at, tokens, packs, cosine, sine, cotangent):
+    )[0]
+
+
+def project_keys(at, tokens, packs, cosine, sine, cotangent):
     local, width = tokens[0].shape
     half_rows = local // 2
     rows = TP * local
     nz = len(packs)
     pack_rows, lanes = packs[0].shape
     d_rows = pack_rows - 16
+    per = 4
+    tiles = 2 * TP // per
 
     def kernel(at_ref, *refs):
         toks, refs = refs[:TP], refs[TP:]
         pack, refs = refs[:nz], refs[nz:]
-        cos_ref, sin_ref, cot_ref, x_ref, hid_ref, qt_ref, kv_ref, w_ref, side_ref, gain_ref, hold = refs
+        cos_ref, sin_ref, cot_ref, hid_ref, kv_ref, w_ref, side_ref, gain_ref, hold, kept, sems = refs
         z = at_ref[1]
         for s in range(nz):
             hold[z ^ s] = pack[s][...]
@@ -225,42 +222,74 @@
             hold[s, pl.ds(0, d_rows), pl.ds(2 * OWN, OWN)].astype(f32) for s in range(nz)
         ]
         side_ref[pl.ds(local, OWN), pl.ds(0, width)] = jnp.concatenate(turned, axis=0).T.astype(bf16)
-        per = 4
-        for tile in range(2 * TP // per):
+        copies = []
+        for tile in range(tiles):
             side, first = (tile * per) // TP, (tile * per) % TP
             at_rows = pl.ds(tile * per * half_rows, per * half_rows)
             block = jnp.concatenate(
                 [toks[first + j][pl.ds(side * half_rows, half_rows), :] for j in range(per)], axis=0
             )
-            x_ref[at_rows, :] = block
             inputs = block.astype(f32)
             hidden = (inputs * norm_scale(inputs) * gain).astype(bf16)
-            hid_ref[at_rows, :] = hidden
-            out = nn(hidden, w_ref[...])
-            cos, sin = cos_ref[at_rows, :], sin_ref[at_rows, :]
-            query = out[:, :OWN]
-            query = query * cos + swap_halves(query) * sin
-            qt_ref[:, at_rows] = (query.astype(bf16).astype(f32) * HEAD**-0.5).T.astype(bf16)
-            pair = out[:, OWN:]
-            turned = pair * cos + swap_halves(pair) * sin
+            kept[at_rows, :] = hidden
+            copy = pltpu.make_async_copy(kept.at[at_rows, :], hid_ref.at[at_rows, :], sems.at[tile])
+            copy.start()
+            copies.append(copy)
+            pair = nn(hidden, w_ref[:, pl.ds(OWN, OWN)])
+            turned = pair * cos_ref[at_rows, :] + swap_halves(pair) * sin_ref[at_rows, :]
             lane = lax.broadcasted_iota(i32, pair.shape, 1)
             kv_ref[at_rows, :] = jnp.where(lane < HEAD, turned, pair).astype(bf16)
+        for copy in copies:
+            copy.wait()
 
     return call(
         kernel,
         [
             shape((rows, width), bf16),
-            shape((rows, width), bf16),
-            shape((OWN, rows), bf16),
             shape((rows, OWN), bf16),
             shape((width, 2 * OWN), bf16),
             shape((local + OWN, TP * OWN), bf16),
             shape((8, width), f32),
         ],
         [at, *tokens, *packs, cosine, sine, cotangent],
-        scratch=[pltpu.VMEM((nz, pack_rows, lanes), bf16)],
+        scratch=[
+            pltpu.VMEM((nz, pack_rows, lanes), bf16),
+            pltpu.VMEM((rows, width), bf16),
+            pltpu.SemaphoreType.DMA((tiles,)),
+        ],
         limit=60,
-        cost=6.0,
+        cost=4.0,
+        far_out=(0,),
+    )
+
+
+def project_queries(tokens, hidden, w_qkv, cosine, sine):
+    local, width = tokens[0].shape
+    half_rows = local // 2
+    rows = TP * local
+    per = 4
+
+    def kernel(*refs):
+        toks, refs = refs[:TP], refs[TP:]
+        hid_ref, w_ref, cos_ref, sin_ref, x_ref, qt_ref = refs
+        for tile in range(2 * TP // per):
+            side, first = (tile * per) // TP, (tile * per) % TP
+            at_rows = pl.ds(tile * per * half_rows, per * half_rows)
+            for j in range(per):
+                x_ref[pl.ds((tile * per + j) * half_rows, half_rows), :] = toks[first + j][
+                    pl.ds(side * half_rows, half_rows), :
+                ]
+            query = nn(hid_ref[at_rows, :], w_ref[:, pl.ds(0, OWN)])
+            query = query * cos_ref[at_rows, :] + swap_halves(query) * sin_ref[at_rows, :]
+            qt_ref[:, at_rows] = (query.astype(bf16).astype(f32) * HEAD**-0.5).T.astype(bf16)
+
+    return call(
+        kernel,
+        [shape((rows, width), bf16), shape((OWN, rows), bf16)],
+        [*tokens, hidden, w_qkv, cosine, sine],
+        scalars=0,
+        limit=60,
+        cost=4.0,
     )
 
 
@@ -346,7 +375,7 @@
             pltpu.VMEM((2, rows), f32),
             pltpu.VMEM((rows, 128), i32),
         ],
-        limit=24,
+        limit=60,
         cost=14.0,
     )
 
@@ -486,47 +515,35 @@
     half_rows = local // 2
     half = rows // 2
     d_rows, lanes = packs[0].shape
-    upper, lower = packs[2].shape[0], packs[3].shape[0]
     ff = lanes // 3
     part_rows = ff // nz
     per = 4
     tile_rows = per * half_rows
+    tiles = 2 * TP // per
 
     def kernel(at_ref, x_ref, *refs):
         att, refs = refs[:TP], refs[TP:]
-        mine, by_x, by_y, by_xy, odd, last_odd = refs[:6]
-        own_pack, one_pack, near_a, near_b, far_a, far_b = refs[6:12]
-        refs = refs[12:]
-        cot_at = pl.ds(0, local)
-        wo_at = pl.ds(local, OWN)
+        extra, refs = refs[:TP], refs[TP:]
+        pack, refs = refs[:nz], refs[nz:]
         gain_ref, refs = refs[0], refs[1:]
-        att_out, wo_out, resid_out, gk_ref, gp_ref, lk_ref, lp_ref, gain_out = refs[:8]
-        targets, refs = refs[8:12], refs[12:]
-        gu_w, dn_w, cot_ref, acc_gu, acc_dn, hold, blocks = refs
+        resid_out, gk_ref, gp_ref, gain_out, dn_w = refs[:5]
+        targets, prod_out, refs = refs[5 : 5 + nz], refs[5 + nz], refs[6 + nz :]
+        att_ref, wo_ref, gu_w, cot_ref, hold, acc_gu, acc_dn, blocks, prod_ref, sems = refs
         tp = at_ref[0]
         z = at_ref[1]
         for j in range(TP):
             columns = pl.ds(pl.multiple_of((tp ^ j) * OWN, OWN), OWN)
-            even = (mine, by_x, by_y, by_xy)[j // 2]
-            from_cot, from_wo = even.at[cot_at, :], even.at[wo_at, :]
-            if j % 2:
-                source, start = (odd, (local + OWN) * (j // 2)) if j < TP - 1 else (last_odd, 0)
-                from_cot = source.at[pl.ds(start, local), :]
-                from_wo = source.at[pl.ds(start + local, OWN), :]
-            wo_out[columns, :] = from_wo[:, pl.ds(0, width)]
+            wo_ref[columns, :] = extra[j][pl.ds(local, OWN), pl.ds(0, width)]
             for side in range(2):
                 for k in range(TP):
-                    att_out[pl.ds(side * half + k * half_rows, half_rows), columns] = att[j][
+                    att_ref[pl.ds(side * half + k * half_rows, half_rows), columns] = att[j][
                         pl.ds(side * half + (k ^ j) * half_rows, half_rows), :
                     ]
-                cot_ref[pl.ds(side * half + j * half_rows, half_rows), :] = from_cot[
+                cot_ref[pl.ds(side * half + j * half_rows, half_rows), :] = extra[j][
                     pl.ds(side * half_rows, half_rows), pl.ds(0, width)
                 ]
-        hold[z] = own_pack[...]
-        hold[z ^ 1] = one_pack[...]
-        for s, first, second in ((2, near_a, near_b), (3, far_a, far_b)):
-            hold[z ^ s, pl.ds(0, upper), :] = first[...]
-            hold[z ^ s, pl.ds(upper, lower), :] = second[...]
+        for s in range(nz):
+            hold[z ^ s] = pack[s][...]
         for s in range(nz):
             rows_at = pl.ds(s * d_rows, d_rows)
             gu_w[rows_at, :] = hold[s, :, pl.ds(0, 2 * ff)]
@@ -542,9 +559,15 @@
         acc_gu[...] = jnp.zeros_like(acc_gu)
         acc_dn[...] = jnp.zeros_like(acc_dn)
 
+        def copy_of(tile):
+            at_rows = pl.ds(pl.multiple_of(tile * tile_rows, tile_rows), tile_rows)
+            return pltpu.make_async_copy(
+                prod_ref.at[at_rows, :], prod_out.at[at_rows, :], sems.at[tile]
+            )
+
         def one_tile(tile, unused):
             at_rows = pl.ds(pl.multiple_of(tile * tile_rows, tile_rows), tile_rows)
-            branch = nt(att_out[at_rows, :][:, :width], wo_out[pl.ds(0, width), :])
+            branch = nt(att_ref[at_rows, :][:, :width], wo_ref[pl.ds(0, width), :])
             resid = x_ref[at_rows, :].astype(f32) + branch
             side = (tile * per) // TP
 
@@ -561,6 +584,8 @@
             sigmoid = 1.0 / (1.0 + jnp.exp(-gate))
             activated = gate * sigmoid
             product = (activated * up).astype(bf16)
+            prod_ref[at_rows, :] = product
+            copy_of(tile).start()
             cotangent = cot_ref[at_rows, :]
             grad_product = nn(cotangent, dn_w[...])
             grad_gate = grad_product * up * sigmoid * (1.0 + gate * (1.0 - sigmoid))
@@ -568,12 +593,11 @@
             partial = nt(grad_gu, gu_w[...])
             gain_out[pl.ds(0, 1), :] += jnp.sum(partial * normal, axis=0, keepdims=True)
             store_blocks(partial, tile, per, half_rows, gk_ref, gp_ref)
-            store_blocks(nt(product, dn_w[...]), tile, per, half_rows, lk_ref, lp_ref)
             acc_gu[...] += tn(hidden, grad_gu)
             acc_dn[...] += tn(cotangent, product)
             return unused
 
-        lax.fori_loop(0, 2 * TP // per, one_tile, 0)
+        lax.fori_loop(0, tiles, one_tile, 0)
         for b in range(nz):
             blocks[b, :, pl.ds(0, 2 * ff)] = acc_gu[pl.ds(b * d_rows, d_rows), :]
             blocks[b, :, pl.ds(2 * ff, ff)] = jnp.concatenate(
@@ -585,37 +609,81 @@
             )
         for s in range(nz):
             targets[s][...] = blocks[z ^ s].astype(targets[s].dtype)
-
-    keep = shape((TP // 2 * local, width), bf16)
-    passed = shape((TP // 2 * local, TP * OWN), bf16)
+        for tile in range(tiles):
+            copy_of(tile).wait()
+
+    return call(
+        kernel,
+        [
+            shape((local, width), f32),
+            shape((TP // 2 * local, width), bf16),
+            shape((TP // 2 * local, TP * OWN), bf16),
+            shape((8, width), f32),
+            shape((width, ff), bf16),
+        ]
+        + [shape((d_rows, lanes), f32 if s % 2 == 0 else bf16) for s in range(nz)]
+        + [shape((rows, ff), bf16)],
+        [at, inputs, *attended, *sides, *packs, gains],
+        scratch=[
+            pltpu.VMEM((rows, TP * OWN), bf16),
+            pltpu.VMEM((TP * OWN, width), bf16),
+            pltpu.VMEM((width, 2 * ff), bf16),
+            pltpu.VMEM((rows, width), bf16),
+            pltpu.VMEM((nz, d_rows, lanes), bf16),
+            pltpu.VMEM((width, 2 * ff), f32),
+            pltpu.VMEM((width, ff), f32),
+            pltpu.VMEM((nz, d_rows, lanes), f32),
+            pltpu.VMEM((rows, ff), bf16),
+            pltpu.SemaphoreType.DMA((tiles,)),
+        ],
+        limit=44,
+        cost=17.0,
+        far_out=(5 + nz,),
+    )
+
+
+def feed_forward_rest(at, attended, sides, product, w_down):
+    rows = attended[0].shape[0]
+    width, ff = w_down.shape
+    local = rows // TP
+    half_rows = local // 2
+    half = rows // 2
+    per = 4
+    tile_rows = per * half_rows
+
+    def kernel(at_ref, *refs):
+        att, refs = refs[:TP], refs[TP:]
+        extra, refs = refs[:TP], refs[TP:]
+        prod_ref, dn_w, att_out, wo_out, lk_ref, lp_ref = refs
+        tp = at_ref[0]
+        for j in range(TP):
+            columns = pl.ds(pl.multiple_of((tp ^ j) * OWN, OWN), OWN)
+            wo_out[columns, :] = extra[j][pl.ds(local, OWN), pl.ds(0, width)]
+            for side in range(2):
+                for k in range(TP):
+                    att_out[pl.ds(side * half + k * half_rows, half_rows), columns] = att[j][
+                        pl.ds(side * half + (k ^ j) * half_rows, half_rows), :
+                    ]
+
+        def one_tile(tile, unused):
+            at_rows = pl.ds(pl.multiple_of(tile * tile_rows, tile_rows), tile_rows)
+            part = nt(prod_ref[at_rows, :], dn_w[...])
+            store_blocks(part, tile, per, half_rows, lk_ref, lp_ref)
+            return unused
+
+        lax.fori_loop(0, 2 * TP // per, one_tile, 0)
+
     return call(
         kernel,
         [
             shape((rows, TP * OWN), bf16),
             shape((TP * OWN, width), bf16),
-            shape((local, width), f32),
-            keep,
-            passed,
-            keep,
-            passed,
-            shape((8, width), f32),
-            shape((d_rows, lanes), f32),
-            shape((d_rows, lanes), bf16),
-            shape((d_rows, lanes), f32),
-            shape((d_rows, lanes), bf16),
+            shape((TP // 2 * local, width), bf16),
+            shape((TP // 2 * local, TP * OWN), bf16),
         ],
-        [at, inputs, *attended, *sides, *packs, gains],
-        scratch=[
-            pltpu.VMEM((width, 2 * ff), bf16),
-            pltpu.VMEM((width, ff), bf16),
-            pltpu.VMEM((rows, width), bf16),
-            pltpu.VMEM((width, 2 * ff), f32),
-            pltpu.VMEM((width, ff), f32),
-            pltpu.VMEM((nz, d_rows, lanes), bf16),
-            pltpu.VMEM((nz, d_rows, lanes), f32),
-        ],
-        limit=44,
-        cost=18.0,
+        [at, *attended, *sides, product, w_down],
+        limit=24,
+        cost=5.0,
     )
 
 
@@ -982,66 +1050,56 @@
     select = jnp.where((2 * tp + jnp.arange(2)) // GROUP == kv_index, 0, 1).astype(i32)
 
     mask_x, mask_y = 2 * nz, 4 * nz
-    pack_two, pack_a, pack_b = pack_two
-    near_a = send(after(pack_a, *pack_one), 2)
-    inputs, hidden_one, turned_query, kv, w_qkv, side, gains = project(
-        after(at, pack_two), token_slots, pack_one, cosine, sine, cotangent
-    )
-    kv, side, near_a = level(kv, side, near_a)
+    hidden_one, kv, w_qkv, side, gains = project_keys(
+        after(at, pack_two, select, key_base, query_base),
+        token_slots,
+        pack_one,
+        cosine,
+        sine,
+        cotangent,
+    )
     own_kv = [kv] + [send(kv, m) for m in group_mask[1:]]
     side_x, side_y = send(side, mask_x), send(side, mask_y)
-    side_x, side_y, *own_kv = level(side_x, side_y, *own_kv)
-    other_kv = level(*[send(slot, nz) for slot in own_kv])
-    one, near_b = send(after(pack_two, *own_kv), 1), send(after(pack_b, *own_kv), 2)
+    inputs, turned_query = project_queries(
+        token_slots, after(hidden_one, kv), w_qkv, cosine, sine
+    )
+    side_x, side_y, inputs, turned_query, *own_kv = level(
+        side_x, side_y, inputs, turned_query, *own_kv
+    )
+    side_odd, *other_kv = level(send(after(side, *own_kv), nz), *[send(slot, nz) for slot in own_kv])
+    one, near = send(after(pack_two, *own_kv), 1), send(after(pack_two, *own_kv), 2)
     side_xy = send(side_x, mask_y)
-    side_odd = send(jnp.concatenate([side, side_x, side_y], axis=0), nz)
+    odd_x, odd_y = send(after(side_x, *other_kv), nz), send(after(side_y, *other_kv), nz)
     attended, attended_own, log_mass = attention_forward(
         select, key_base, query_base, turned_query, own_kv, other_kv, half_rows
     )
-    attended_own, near_b, one, side_xy, side_odd = level(
-        attended_own, near_b, one, side_xy, side_odd
-    )
-    far_a, far_b, side_xy, *even = level(
-        send(after(near_a, attended_own), 1), send(near_b, 1), side_xy, *gather_even(attended_own)
-    )
+    attended_own, near, one, side_xy, odd_x, odd_y = level(
+        attended_own, near, one, side_xy, odd_x, odd_y
+    )
+    far, side_xy, *even = level(send(near, 1), side_xy, *gather_even(attended_own))
     attended_slots = gather_odd(even)
-    packs = [pack_two, one, near_a, near_b, far_a, far_b]
-    sides = [side, side_x, side_y, side_xy, side_odd, send(side_xy, nz)]
-
-    (
-        attended_low,
-        w_out_all,
-        resid,
-        grad_keep,
-        grad_pass,
-        out_keep,
-        out_pass,
-        gain_sums,
-        ff_own,
-        ff_one,
-        ff_two,
-        ff_three,
-    ) = feed_forward(
-        at,
-        inputs,
-        attended_slots,
-        sides,
-        packs,
-        gains,
-        nz,
-    )
+    packs = [pack_two, one, near, far]
+    sides = [side, side_odd, side_x, odd_x, side_y, odd_y, side_xy, send(side_xy, nz)]
+
+    resid, grad_keep, grad_pass, gain_sums, w_down_own, *ff_blocks, product = feed_forward(
+        at, inputs, attended_slots, sides, packs, gains, nz
+    )
+    ff_own, ff_one, ff_two, ff_three = ff_blocks
     first, *rest = add_crossed(grad_keep, send(grad_pass, nz), TP // 2)
-    ff_three, first, *rest = level(send(after(ff_three, first), 1), first, *scatter_far(rest))
+    attended_low, w_out_all, out_keep, out_pass, ff_three, first, *rest = level(
+        *feed_forward_rest(after(at, first), attended_slots, sides, product, w_down_own),
+        send(after(ff_three, first), 1),
+        first,
+        *scatter_far(rest),
+    )
     grad_resid, trade_keep, trade_pass = branch_gradient(
         at, [first, *rest], resid, cotangent, w_out_all, gains
     )
     crossed, out_crossed = level(send(trade_pass, nz), send(after(out_pass, first), nz))
-    ff_one, *pairs = level(
-        send(after(ff_one, crossed), 1),
-        *scatter_far(pair_up(trade_keep, crossed, TP // 2)),
-    )
+    pairs = level(*scatter_far(pair_up(trade_keep, crossed, TP // 2)))
     out_first, *out_rest = add_crossed(out_keep, out_crossed, TP // 2)
-    ff_two = send(after(first_sum(ff_two, ff_three), *pairs), 2)
+    ff_one = send(after(ff_one, crossed), 1)
+    ff_two = send(first_sum(ff_two, ff_three), 2)
     out_rest = scatter_far([after(piece, *pairs) for piece in out_rest])
 
     grad_query, kv_keep, kv_pass, branch_columns = attention_backward(
@@ -1056,10 +1114,11 @@
         log_mass,
         half_rows,
     )
-    kv_pass, ff_two, *out_rest = level(kv_pass, ff_two, *out_rest)
+    kv_pass, ff_one, ff_two, *out_rest = level(kv_pass, ff_one, ff_two, *out_rest)
     kv_crossed = send(kv_pass, nz)
     first, *rest = add_crossed(kv_keep, kv_crossed, groups)
-    ff_total = last_sum(after(ff_own, rest[0]), ff_one, ff_two)
+    grad_out = tn(attended_low[:, :width], after(branch_columns, rest[0]))
+    ff_total = last_sum(after(ff_own, grad_out), ff_one, ff_two)
 
     for step in range(outer.bit_length() - 1):
         crossing = send(ff_total, TP * nz << step).astype(f32)
@@ -1070,7 +1129,6 @@
         send(ff_total, mask_y),
         *[send(piece, m) for piece, m in zip(rest, group_mask[1:])],
     )
-    grad_out = tn(attended_low[:, :width], after(branch_columns, rest[0]))
 
     last_keep, last_pass, last_own, *last_sends = projection_gradient(
         at,

time: 277 us -> 265 us (0.957)
  waiting for transfers between devices: 111 us -> 99.1 us
  Pallas kernels: 78.7 us -> 85.9 us
  starting transfers between devices: 65.3 us -> 62.4 us
    ppermute x70, waiting for transfers between devices: 111 us -> 99.1 us  [exchange(): return lax.ppermute(array, AXES, [(i, i ^ mask) for i in range(count)])]
    pallas_call x20 -> x22, Pallas kernels: 78.7 us -> 85.9 us  [call(): pl.pallas_call(kernel, out_shape=tuple(outs), in_specs=specs, out_specs=t...]
    ppermute x70, starting transfers between devices: 65.3 us -> 62.4 us  [exchange(): return lax.ppermute(array, AXES, [(i, i ^ mask) for i in range(count)])]
    unnamed x86 -> x114, local copies, waits for them, and re-layouts: 9.4 us -> 6.61 us
  transfers between devices with their start and end apart: 70 -> 70, of which waited for: 31 -> 30; matrix products, arithmetic and copies ran while one was open for 3% -> 3% of each run, Pallas kernels for 18% -> 20%
where the time goes in v2:
time: 265 us; the launch traced here: 264 us
  waiting for transfers between devices  99.1 us (37%)
  Pallas kernels  85.9 us (32%)
  starting transfers between devices  62.4 us (24%)
  local copies, waits for them, and re-layouts  9.32 us (4%)
  other arithmetic  4.56 us (2%)
    ppermute x70, waiting for transfers between devices, exchange(): return lax.ppermute(array, AXES, [(i, i ^ mask) for i in range(count)])  99.1 us
    pallas_call x22, Pallas kernels, call(): pl.pallas_call(kernel, out_shape=tuple(outs), in_specs=specs, out_specs=t...  85.9 us
    ppermute x70, starting transfers between devices, exchange(): return lax.ppermute(array, AXES, [(i, i ^ mask) for i in range(count)])  62.4 us
    unnamed x114, local copies, waits for them, and re-layouts  6.61 us
  transfers between devices with their start and end apart: 70, of which 30 were waited for; matrix products, arithmetic and copies ran while one was open for 3% of the time, Pallas kernels for 20%

profile of v2, /device:TPU:0, one launch (start us, length us, event | category | flops | bytes accessed | tf_op | source)
XLA Modules:
  0.0 263.6 jit_solution(13773121172783583547)
XLA Ops:
  1.3 3.3 %shard_map.221.refs_8_ = bf16[256,384]{1,0:T(8,128)(2,1)} custom-call(s32[3]{0:T(128)} %pad_add_fusion.1.at_ref, bf16[240,960]{1,0:T(8,128)(2,1)} %q_ref.1, bf16[320,240]{1,0:T(8,128)(2,1)} %bitcast.21, bf16[320,240]{1,0:T(8,128)(2,1)} %bitcast.22, bf16[240,960]{1,0:T(8,128)(2,1)} %o_ref.1, bf16[240]{0:T(256)(128)(2,1)} %g1_ref.1, bf16[240]{0:T(256)(128)(2,1)} %g2_ref.1), custom_call_target="tpu_custom_call" | custom-call | flops 2000000000 | bytes 2000000 | tf_op jit(solution)/shard_map/pallas_call | solution.py:55
  4.6 5.1 %collective-permute-start.9 = (bf16[256,384]{1,0:T(8,128)(2,1)}, bf16[256,384]{1,0:T(8,128)(2,1)}, u32[]{:S(2)}, u32[]{:S(2)}) collective-permute-start(bf16[256,384]{1,0:T(8,128)(2,1)} %shard_map.221.refs_8_), channel_id=1, source_target_pairs={{0,3},{1,2},{2,1},{3,0},{4,7},{5,6},{6,5},{7,4},{8,11},{9,10},{10,... | collective-permute-start | bytes 589832 | tf_op jit(solution)/shard_map/ppermute | solution.py:29
  9.9 2.5 collective-permute-start.2
  15.4 1.3 copy-done.12
  16.7 2.7 %shard_map.222.refs_16_ = bf16[240,960]{1,0:T(8,128)(2,1)} custom-call(s32[3]{0:T(128)S(1)} %copy-done.8, bf16[240,2560]{1,0:T(8,128)(2,1)S(1)} %copy-done.10, bf16[240,2560]{1,0:T(8,128)(2,1)S(1)} %copy-done.11, bf16[960,640]{1,0:T(8,128)(2,1)S(1)} %bitcast.19), custom_call_target="tpu_custom_call" | custom-call | flops 4000000000 | bytes 4000000 | tf_op jit(solution)/shard_map/pallas_call | solution.py:55
  22.3 2.0 collective-permute-done.1.refs_4_
  25.3 1.6 collective-permute-done.8.refs_10_
  26.9 3.1 %fusion.2 = (f32[1024,128]{1,0:T(8,128)}, f32[1024,128]{1,0:T(8,128)}) fusion(f32[128]{0:T(128)S(1)} %get-tuple-element.313, f32[128]{0:T(128)S(1)} %get-tuple-element.314, f32[1024]{0:T(1024)S(1)} %convert_element_type.30), kind=kLoop, calls=%fused_computation.7 | loop fusion | flops 262144 | bytes 1053696 | tf_op jit(solution)/shard_map/mul | solution.py:1049
  31.8 5.4 %shard_map.223 = (bf16[1024,960]{1,0:T(8,128)(2,1)}, bf16[1024,128]{1,0:T(8,128)(2,1)}, bf16[960,256]{1,0:T(8,128)(2,1)}, bf16[256,1024]{1,0:T(8,128)(2,1)}, f32[8,960]{1,0:T(8,128)}) custom-call(s32[3]{0:T(128)} %pad_add_fusion.1.at_ref, bf16[128,960]{1,0:T(8,128)(2,1)} %copy-done.46, bf16[128,960]{1,0:T(8,128)(2,1)} %copy-done.51, ...), custom_call_target="tpu_custom_call" | custom-call | flops 4000000000 | bytes 4000000 | tf_op jit(solution)/shard_map/pallas_call | solution.py:55
  37.2 1.6 collective-permute-start.11
  38.8 1.1 collective-permute-start.10
  39.9 2.1 collective-permute-start.14
  42.0 2.3 collective-permute-start.12
  44.2 5.0 %shard_map.224 = (bf16[1024,960]{1,0:T(8,128)(2,1)}, bf16[128,1024]{1,0:T(8,128)(2,1)}) custom-call(bf16[128,960]{1,0:T(8,128)(2,1)} %copy-done.46, bf16[128,960]{1,0:T(8,128)(2,1)} %copy-done.51, bf16[128,960]{1,0:T(8,128)(2,1)} %collective-permute-done.refs_2_, bf16[128,960]{1,0:T(8,128)(2,1)} %copy-done.52, ...), custom_call_target="tpu_custom_call" | custom-call | flops 4000000000 | bytes 4000000 | tf_op jit(solution)/shard_map/pallas_call | solution.py:55
  49.2 2.0 collective-permute-done.14.refs_3_
  51.2 12.3 %collective-permute-done.13.refs_2_ = bf16[1024,128]{1,0:T(8,128)(2,1)S(1)} collective-permute-done((bf16[1024,128]{1,0:T(8,128)(2,1)}, bf16[1024,128]{1,0:T(8,128)(2,1)S(1)}, u32[]{:S(2)}, u32[]{:S(2)}) %collective-permute-start.13) | collective-permute-done | bytes 262176 | tf_op jit(solution)/shard_map/ppermute | solution.py:29
  64.8 1.2 collective-permute-done.16.refs_4_
  66.3 2.5 collective-permute-start.20
  68.8 1.3 collective-permute-start.22
  70.8 13.8 %shard_map.225 = (f32[128,1024]{1,0:T(8,128)}, bf16[1024,128]{1,0:T(8,128)(2,1)}, f32[2,1024]{1,0:T(2,128)}) custom-call(s32[2]{0:T(128)} %compare_select_fusion.2.sel_ref, s32[8,16]{1,0:T(8,128)} %reshape.107.key_ref, s32[16]{0:T(128)} %copy-done.6, bf16[128,1024]{1,0:T(8,128)(2,1)} %get-tuple-element.174.q_ref, ...), custom_call_target="tpu_custom_call" | custom-call | flops 14000000000 | bytes 14000000 | tf_op jit(solution)/shard_map/pallas_call | solution.py:55
  84.7 4.8 %collective-permute-done.21.refs_17_ = bf16[240,960]{1,0:T(8,128)(2,1)} collective-permute-done((bf16[240,960]{1,0:T(8,128)(2,1)}, bf16[240,960]{1,0:T(8,128)(2,1)}, u32[]{:S(2)}, u32[]{:S(2)}) %collective-permute-start.21) | collective-permute-done | bytes 460832 | tf_op jit(solution)/shard_map/ppermute | solution.py:29
  89.4 2.0 collective-permute-done.20.refs_18_
  91.5 1.2 collective-permute-start.28
  92.6 1.4 collective-permute-start.27
  95.0 6.9 %collective-permute-done.28.refs_6_ = bf16[1024,128]{1,0:T(8,128)(2,1)S(1)} collective-permute-done((bf16[1024,128]{1,0:T(8,128)(2,1)}, bf16[1024,128]{1,0:T(8,128)(2,1)S(1)}, u32[]{:S(2)}, u32[]{:S(2)}) %collective-permute-start.28) | collective-permute-done | bytes 262176 | tf_op jit(solution)/shard_map/ppermute | solution.py:29
  101.9 3.7 %collective-permute-done.27.refs_4_ = bf16[1024,128]{1,0:T(8,128)(2,1)S(1)} collective-permute-done((bf16[1024,128]{1,0:T(8,128)(2,1)}, bf16[1024,128]{1,0:T(8,128)(2,1)S(1)}, u32[]{:S(2)}, u32[]{:S(2)}) %collective-permute-start.27) | collective-permute-done | bytes 262176 | tf_op jit(solution)/shard_map/ppermute | solution.py:29
  106.7 1.8 collective-permute-done.29.refs_1_
  110.0 18.4 %shard_map.226 = (f32[128,960]{1,0:T(8,128)S(1)}, bf16[512,960]{1,0:T(8,128)(2,1)}, bf16[512,1024]{1,0:T(8,128)(2,1)}, f32[8,960]{1,0:T(8,128)S(1)}, bf16[960,32...) custom-call(s32[3]{0:T(128)S(1)} %copy-done.9, ...), custom_call_target="tpu_custom_call" | custom-call | flops 16999999488 | bytes 17000000 | tf_op jit(solution)/shard_map/pallas_call | solution.py:55
  128.6 2.7 %collective-permute-done.34.cross_ref = bf16[512,1024]{1,0:T(8,128)(2,1)S(1)} collective-permute-done((bf16[512,1024]{1,0:T(8,128)(2,1)}, bf16[512,1024]{1,0:T(8,128)(2,1)S(1)}, u32[]{:S(2)}, u32[]{:S(2)}) %collective-permute-start.34) | collective-permute-done | bytes 1048608 | tf_op jit(solution)/shard_map/ppermute | solution.py:29
  131.3 1.2 copy-done.34
  132.8 1.3 collective-permute-start.36
  134.7 1.7 collective-permute-start.38
  136.7 3.4 %shard_map.228 = (bf16[1024,1024]{1,0:T(8,128)(2,1)S(1)}, bf16[1024,960]{1,0:T(8,128)(2,1)S(1)}, bf16[512,960]{1,0:T(8,128)(2,1)S(1)}, bf16[512,1024]{1,0:T(8,128)(2,1)S(1)}) custom-call(s32[3]{0:T(128)S(1)} %copy-done.9, bf16[1024,128]{1,0:T(8,128)(2,1)S(1)} %copy-done.31, bf16[1024,128]{1,0:T(8,128)(2,1)S(1)} %collective-permute-done.29.refs_1_, ...), custom_call_target="tpu_custom_call" | custom-call | flops 5000000000 | bytes 5000000 | tf_op jit(solution)/shard_map/pallas_call | solution.py:55
  140.1 1.9 collective-permute-done.36.refs_1_
  142.0 5.8 %collective-permute-done.37.refs_2_ = bf16[128,960]{1,0:T(8,128)(2,1)S(1)} collective-permute-done((bf16[128,960]{1,0:T(8,128)(2,1)S(1)}, bf16[128,960]{1,0:T(8,128)(2,1)S(1)}, u32[]{:S(2)}, u32[]{:S(2)}) %collective-permute-start.37) | collective-permute-done | bytes 245792 | tf_op jit(solution)/shard_map/ppermute | solution.py:29
  148.8 1.5 shard_map.229
  150.8 1.2 collective-permute-done.39.cross_ref.refs_9_
  152.0 1.3 collective-permute-start.41
  153.9 1.7 collective-permute-start.43
  155.8 2.8 %collective-permute-start.45 = (bf16[240,960]{1,0:T(8,128)(2,1)S(1)}, bf16[240,960]{1,0:T(8,128)(2,1)S(1)}, u32[]{:S(2)}, u32[]{:S(2)}) collective-permute-start(bf16[240,960]{1,0:T(8,128)(2,1)S(1)} %shard_map.233), channel_id=1, source_target_pairs={{0,2},{1,3},{2,0},{3,1},{4,6},{5,7},{6,4},{7,5},{8,10},{9,11},{10,... | collective-permute-start | bytes 1382408 | tf_op jit(solution)/shard_map/ppermute | solution.py:29
  159.2 2.4 collective-permute-done.42.refs_11_
  162.4 1.2 collective-permute-start.47
  163.6 1.5 collective-permute-start.48
  165.2 17.3 %shard_map.232 = (f32[128,1024]{1,0:T(8,128)S(1)}, f32[4096,128]{1,0:T(8,128)S(1)}, bf16[4096,128]{1,0:T(8,128)(2,1)S(1)}, bf16[1024,128]{1,0:T(8,128)(2,1)S(1)}) custom-call(s32[2]{0:T(128)S(1)} %copy-done.32, s32[8,16]{1,0:T(8,128)S(1)} %copy-done.5, s32[16]{0:T(128)S(1)} %copy-done.7, bf16[128,1024]{1,0:T(8,128)(2,1)S(1)} %copy-done.42, ...), custom_call_target="tpu_custom_call" | custom-call | flops 17999998976 | bytes 18000000 | tf_op jit(solution)/shard_map/pallas_call | solution.py:55
  182.7 2.6 %collective-permute-done.49.cross_ref = bf16[4096,128]{1,0:T(8,128)(2,1)S(1)} collective-permute-done((bf16[4096,128]{1,0:T(8,128)(2,1)S(1)}, bf16[4096,128]{1,0:T(8,128)(2,1)S(1)}, u32[]{:S(2)}, u32[]{:S(2)}) %collective-permute-start.49) | collective-permute-done | bytes 1048608 | tf_op jit(solution)/shard_map/ppermute | solution.py:29
  187.5 1.4 collective-permute-start.50
  188.9 2.7 %collective-permute-start.53 = (bf16[1024,128]{1,0:T(8,128)(2,1)S(1)}, bf16[1024,128]{1,0:T(8,128)(2,1)S(1)}, u32[]{:S(2)}, u32[]{:S(2)}) collective-permute-start(bf16[1024,128]{1,0:T(8,128)(2,1)S(1)} %get-tuple-element.269), channel_id=1, source_target_pairs={{0,2},{1,3},{2,0},{3,1},{4,6},{5,7},{6,4},{7,5},{8,10},{9,11},{10,... | collective-permute-start | bytes 786440 | tf_op jit(solution)/shard_map/ppermute | solution.py:29
  192.4 16.4 %collective-permute-done.53.refs_2_ = bf16[1024,128]{1,0:T(8,128)(2,1)S(1)} collective-permute-done((bf16[1024,128]{1,0:T(8,128)(2,1)S(1)}, bf16[1024,128]{1,0:T(8,128)(2,1)S(1)}, u32[]{:S(2)}, u32[]{:S(2)}) %collective-permute-start.53) | collective-permute-done | bytes 262176 | tf_op jit(solution)/shard_map/ppermute | solution.py:29
  208.8 1.4 collective-permute-done.52.refs_1_
  210.3 3.7 %shard_map.237 = (bf16[512,960]{1,0:T(8,128)(2,1)S(1)}, bf16[512,1024]{1,0:T(8,128)(2,1)S(1)}, f32[256,384]{1,0:T(8,128)S(1)}, bf16[256,384]{1,0:T(8,128)(2,1)S(...) custom-call(s32[3]{0:T(128)S(1)} %copy-done.9, f32[128,1024]{1,0:T(8,128)S(1)} %get-tuple-element.260.dq_ref, ...), custom_call_target="tpu_custom_call" | custom-call | flops 8000000000 | bytes 8000000 | tf_op jit(solution)/shard_map/pallas_call | solution.py:55
  215.0 1.8 collective-permute-done.55.cross_ref
  217.9 4.7 %collective-permute-start.58 = (bf16[256,384]{1,0:T(8,128)(2,1)S(1)}, bf16[256,384]{1,0:T(8,128)(2,1)S(1)}, u32[]{:S(2)}, u32[]{:S(2)}) collective-permute-start(bf16[256,384]{1,0:T(8,128)(2,1)S(1)} %get-tuple-element.282), channel_id=1, source_target_pairs={{0,1},{1,0},{2,3},{3,2},{4,5},{5,4},{6,7},{7,6},{8,9},{9,8},{10,11... | collective-permute-start | bytes 589832 | tf_op jit(solution)/shard_map/ppermute | solution.py:29
  222.5 1.2 collective-permute-start.59
  223.7 1.5 collective-permute-start.60
  225.2 5.8 %collective-permute-done.58 = bf16[256,384]{1,0:T(8,128)(2,1)S(1)} collective-permute-done((bf16[256,384]{1,0:T(8,128)(2,1)S(1)}, bf16[256,384]{1,0:T(8,128)(2,1)S(1)}, u32[]{:S(2)}, u32[]{:S(2)}) %collective-permute-start.58) | collective-permute-done | bytes 196640 | tf_op jit(solution)/shard_map/ppermute | solution.py:29
  230.9 8.7 %collective-permute-done.59 = bf16[256,384]{1,0:T(8,128)(2,1)S(1)} collective-permute-done((bf16[256,384]{1,0:T(8,128)(2,1)S(1)}, bf16[256,384]{1,0:T(8,128)(2,1)S(1)}, u32[]{:S(2)}, u32[]{:S(2)}) %collective-permute-start.59) | collective-permute-done | bytes 196640 | tf_op jit(solution)/shard_map/ppermute | solution.py:29
  240.0 1.3 collective-permute-start.65
  241.4 1.4 collective-permute-start.64
  243.7 1.3 collective-permute-start.61
  245.0 5.6 %shard_map.240 = (f32[240,2560]{1,0:T(8,128)}, f32[240,2560]{1,0:T(8,128)}, f32[960,640]{1,0:T(8,128)}) custom-call(s32[3]{0:T(128)S(1)} %copy-done.9, bf16[240,1024]{1,0:T(8,128)(2,1)S(1)} %shard_map.236.m_ref, bf16[240,1024]{1,0:T(8,128)(2,1)S(1)} %collective-permute-done.50.x_ref, bf16[240,1024]{1,0:T(8,128)(2,1)S(1)} %collective-permute-done.51.y_ref, ...), custom_call_target="tpu_custom_call" | custom-call | flops 7000000000 | bytes 7000000 | tf_op jit(solution)/shard_map/pallas_call | solution.py:55
  250.7 1.9 collective-permute-done.64.refs_4_
  252.7 5.2 %collective-permute-done.61.refs_1_ = bf16[128,960]{1,0:T(8,128)(2,1)S(1)} collective-permute-done((bf16[128,960]{1,0:T(8,128)(2,1)S(1)}, bf16[128,960]{1,0:T(8,128)(2,1)S(1)}, u32[]{:S(2)}, u32[]{:S(2)}) %collective-permute-start.61) | collective-permute-done | bytes 245792 | tf_op jit(solution)/shard_map/ppermute | solution.py:29
  259.8 1.2 shard_map.241
  261.1 2.5 shard_map.242
  (240 shorter events, 28.8 us)
Async XLA Ops:
  4.6 20.6 %collective-permute-start.9 = (bf16[256,384]{1,0:T(8,128)(2,1)}, bf16[256,384]{1,0:T(8,128)(2,1)}, u32[]{:S(2)}, u32[]{:S(2)}) collective-permute-start(bf16[256,384]{1,0:T(8,128)(2,1)} %shard_map.221.refs_8_), channel_id=1, source_target_pairs={{0,3},{1,2},{2,1},{3,0},{4,7},{5,6},{6,5},{7,4},{8,11},{9,10},{10,... | collective-permute-start | bytes 589832 | tf_op jit(solution)/shard_map/ppermute | solution.py:29
  9.7 17.1 %collective-permute-start.8 = (bf16[256,384]{1,0:T(8,128)(2,1)}, bf16[256,384]{1,0:T(8,128)(2,1)}, u32[]{:S(2)}, u32[]{:S(2)}) collective-permute-start(bf16[256,384]{1,0:T(8,128)(2,1)} %shard_map.221.refs_8_), channel_id=1, source_target_pairs={{0,2},{1,3},{2,0},{3,1},{4,6},{5,7},{6,4},{7,5},{8,10},{9,11},{10,... | collective-permute-start | bytes 589832 | tf_op jit(solution)/shard_map/ppermute | solution.py:29
  9.9 11.7 %collective-permute-start.2 = (bf16[128,960]{1,0:T(8,128)(2,1)S(1)}, bf16[128,960]{1,0:T(8,128)(2,1)S(1)}, u32[]{:S(2)}, u32[]{:S(2)}) collective-permute-start(bf16[128,960]{1,0:T(8,128)(2,1)S(1)} %copy.57.refs_2_), channel_id=1, source_target_pairs={{0,24},{1,25},{2,26},{3,27},{4,28},{5,29},{6,30},{7,31},{8,16},{9,... | collective-permute-start | bytes 737288 | tf_op jit(solution)/shard_map/ppermute | solution.py:29
  12.4 11.9 %collective-permute-start.1 = (bf16[128,960]{1,0:T(8,128)(2,1)S(1)}, bf16[128,960]{1,0:T(8,128)(2,1)}, u32[]{:S(2)}, u32[]{:S(2)}) collective-permute-start(bf16[128,960]{1,0:T(8,128)(2,1)S(1)} %copy.57.refs_2_), channel_id=1, source_target_pairs={{0,16},{1,17},{2,18},{3,19},{4,20},{5,21},{6,22},{7,23},{8,24},{9,... | collective-permute-start | bytes 737288 | tf_op jit(solution)/shard_map/ppermute | solution.py:29
  12.9 11.5 %collective-permute-start = (bf16[128,960]{1,0:T(8,128)(2,1)S(1)}, bf16[128,960]{1,0:T(8,128)(2,1)}, u32[]{:S(2)}, u32[]{:S(2)}) collective-permute-start(bf16[128,960]{1,0:T(8,128)(2,1)S(1)} %copy.57.refs_2_), channel_id=1, source_target_pairs={{0,8},{1,9},{2,10},{3,11},{4,12},{5,13},{6,14},{7,15},{8,0},{9,1},... | collective-permute-start | bytes 737288 | tf_op jit(solution)/shard_map/ppermute | solution.py:29
  21.6 9.1 %collective-permute-start.7 = (bf16[256,384]{1,0:T(8,128)(2,1)}, bf16[256,384]{1,0:T(8,128)(2,1)S(1)}, u32[]{:S(2)}, u32[]{:S(2)}) collective-permute-start(bf16[256,384]{1,0:T(8,128)(2,1)} %shard_map.221.refs_8_), channel_id=1, source_target_pairs={{0,1},{1,0},{2,3},{3,2},{4,5},{5,4},{6,7},{7,6},{8,9},{9,8},{10,11... | collective-permute-start | bytes 589832 | tf_op jit(solution)/shard_map/ppermute | solution.py:29
  24.6 6.1 %collective-permute-start.3 = (bf16[128,960]{1,0:T(8,128)(2,1)S(1)}, bf16[128,960]{1,0:T(8,128)(2,1)S(1)}, u32[]{:S(2)}, u32[]{:S(2)}) collective-permute-start(bf16[128,960]{1,0:T(8,128)(2,1)S(1)} %copy.61.refs_0_), channel_id=1, source_target_pairs={{0,4},{1,5},{2,6},{3,7},{4,0},{5,1},{6,2},{7,3},{8,12},{9,13},{10,... | collective-permute-start | bytes 737288 | tf_op jit(solution)/shard_map/ppermute | solution.py:29
  24.7 6.1 %collective-permute-start.4 = (bf16[128,960]{1,0:T(8,128)(2,1)}, bf16[128,960]{1,0:T(8,128)(2,1)S(1)}, u32[]{:S(2)}, u32[]{:S(2)}) collective-permute-start(bf16[128,960]{1,0:T(8,128)(2,1)} %collective-permute-done.refs_2_), channel_id=1, source_target_pairs={{0,4},{1,5},{2,6},{3,7},{4,0},{5,1},{6,2},{7,3},{8,12},{9,13},{10,... | collective-permute-start | bytes 737288 | tf_op jit(solution)/shard_map/ppermute | solution.py:29
  25.2 5.6 %collective-permute-start.5 = (bf16[128,960]{1,0:T(8,128)(2,1)}, bf16[128,960]{1,0:T(8,128)(2,1)S(1)}, u32[]{:S(2)}, u32[]{:S(2)}) collective-permute-start(bf16[128,960]{1,0:T(8,128)(2,1)} %collective-permute-done.1.refs_4_), channel_id=1, source_target_pairs={{0,4},{1,5},{2,6},{3,7},{4,0},{5,1},{6,2},{7,3},{8,12},{9,13},{10,... | collective-permute-start | bytes 737288 | tf_op jit(solution)/shard_map/ppermute | solution.py:29
  26.9 4.0 %collective-permute-start.6 = (bf16[128,960]{1,0:T(8,128)(2,1)S(1)}, bf16[128,960]{1,0:T(8,128)(2,1)S(1)}, u32[]{:S(2)}, u32[]{:S(2)}) collective-permute-start(bf16[128,960]{1,0:T(8,128)(2,1)S(1)} %collective-permute-done.2.refs_6_), channel_id=1, source_target_pairs={{0,4},{1,5},{2,6},{3,7},{4,0},{5,1},{6,2},{7,3},{8,12},{9,13},{10,... | collective-permute-start | bytes 737288 | tf_op jit(solution)/shard_map/ppermute | solution.py:29
  37.2 26.3 %collective-permute-start.11 = (bf16[256,1024]{1,0:T(8,128)(2,1)}, bf16[256,1024]{1,0:T(8,128)(2,1)S(1)}, u32[]{:S(2)}, u32[]{:S(2)}) collective-permute-start(bf16[256,1024]{1,0:T(8,128)(2,1)} %get-tuple-element.179.refs_8_), channel_id=1, source_target_pairs={{0,16},{1,17},{2,18},{3,19},{4,20},{5,21},{6,22},{7,23},{8,24},{9,... | collective-permute-start | bytes 1572872 | tf_op jit(solution)/shard_map/ppermute | solution.py:29
  38.8 24.8 %collective-permute-start.10 = (bf16[256,1024]{1,0:T(8,128)(2,1)}, bf16[256,1024]{1,0:T(8,128)(2,1)S(1)}, u32[]{:S(2)}, u32[]{:S(2)}) collective-permute-start(bf16[256,1024]{1,0:T(8,128)(2,1)} %get-tuple-element.179.refs_8_), channel_id=1, source_target_pairs={{0,8},{1,9},{2,10},{3,11},{4,12},{5,13},{6,14},{7,15},{8,0},{9,1},... | collective-permute-start | bytes 1572872 | tf_op jit(solution)/shard_map/ppermute | solution.py:29
  39.9 11.4 %collective-permute-start.14 = (bf16[1024,128]{1,0:T(8,128)(2,1)}, bf16[1024,128]{1,0:T(8,128)(2,1)S(1)}, u32[]{:S(2)}, u32[]{:S(2)}) collective-permute-start(bf16[1024,128]{1,0:T(8,128)(2,1)} %get-tuple-element.175.refs_0_), channel_id=1, source_target_pairs={{0,3},{1,2},{2,1},{3,0},{4,7},{5,6},{6,5},{7,4},{8,11},{9,10},{10,... | collective-permute-start | bytes 786440 | tf_op jit(solution)/shard_map/ppermute | solution.py:29
  42.0 21.6 %collective-permute-start.13 = (bf16[1024,128]{1,0:T(8,128)(2,1)}, bf16[1024,128]{1,0:T(8,128)(2,1)S(1)}, u32[]{:S(2)}, u32[]{:S(2)}) collective-permute-start(bf16[1024,128]{1,0:T(8,128)(2,1)} %get-tuple-element.175.refs_0_), channel_id=1, source_target_pairs={{0,2},{1,3},{2,0},{3,1},{4,6},{5,7},{6,4},{7,5},{8,10},{9,11},{10,... | collective-permute-start | bytes 786440 | tf_op jit(solution)/shard_map/ppermute | solution.py:29
  42.0 21.6 %collective-permute-start.12 = (bf16[1024,128]{1,0:T(8,128)(2,1)}, bf16[1024,128]{1,0:T(8,128)(2,1)S(1)}, u32[]{:S(2)}, u32[]{:S(2)}) collective-permute-start(bf16[1024,128]{1,0:T(8,128)(2,1)} %get-tuple-element.175.refs_0_), channel_id=1, source_target_pairs={{0,1},{1,0},{2,3},{3,2},{4,5},{5,4},{6,7},{7,6},{8,9},{9,8},{10,11... | collective-permute-start | bytes 786440 | tf_op jit(solution)/shard_map/ppermute | solution.py:29
  63.6 6.5 %collective-permute-start.15 = (bf16[256,1024]{1,0:T(8,128)(2,1)S(1)}, bf16[256,1024]{1,0:T(8,128)(2,1)S(1)}, u32[]{:S(2)}, u32[]{:S(2)}) collective-permute-start(bf16[256,1024]{1,0:T(8,128)(2,1)S(1)} %copy-done.13), channel_id=1, source_target_pairs={{0,4},{1,5},{2,6},{3,7},{4,0},{5,1},{6,2},{7,3},{8,12},{9,13},{10,... | collective-permute-start | bytes 1572872 | tf_op jit(solution)/shard_map/ppermute | solution.py:29
  64.3 4.6 %collective-permute-start.18 = (bf16[1024,128]{1,0:T(8,128)(2,1)S(1)}, bf16[1024,128]{1,0:T(8,128)(2,1)S(1)}, u32[]{:S(2)}, u32[]{:S(2)}) collective-permute-start(bf16[1024,128]{1,0:T(8,128)(2,1)S(1)} %collective-permute-done.13.refs_2_), channel_id=1, source_target_pairs={{0,4},{1,5},{2,6},{3,7},{4,0},{5,1},{6,2},{7,3},{8,12},{9,13},{10,... | collective-permute-start | bytes 786440 | tf_op jit(solution)/shard_map/ppermute | solution.py:29
  64.7 5.4 %collective-permute-start.19 = (bf16[1024,128]{1,0:T(8,128)(2,1)S(1)}, bf16[1024,128]{1,0:T(8,128)(2,1)S(1)}, u32[]{:S(2)}, u32[]{:S(2)}) collective-permute-start(bf16[1024,128]{1,0:T(8,128)(2,1)S(1)} %collective-permute-done.14.refs_3_), channel_id=1, source_target_pairs={{0,4},{1,5},{2,6},{3,7},{4,0},{5,1},{6,2},{7,3},{8,12},{9,13},{10,... | collective-permute-start | bytes 786440 | tf_op jit(solution)/shard_map/ppermute | solution.py:29
  66.0 23.4 %collective-permute-start.21 = (bf16[240,960]{1,0:T(8,128)(2,1)}, bf16[240,960]{1,0:T(8,128)(2,1)}, u32[]{:S(2)}, u32[]{:S(2)}) collective-permute-start(bf16[240,960]{1,0:T(8,128)(2,1)} %shard_map.222.refs_16_), channel_id=1, source_target_pairs={{0,1},{1,0},{2,3},{3,2},{4,5},{5,4},{6,7},{7,6},{8,9},{9,8},{10,11... | collective-permute-start | bytes 1382408 | tf_op jit(solution)/shard_map/ppermute | solution.py:29
  66.3 25.1 %collective-permute-start.20 = (bf16[240,960]{1,0:T(8,128)(2,1)}, bf16[240,960]{1,0:T(8,128)(2,1)}, u32[]{:S(2)}, u32[]{:S(2)}) collective-permute-start(bf16[240,960]{1,0:T(8,128)(2,1)} %shard_map.222.refs_16_), channel_id=1, source_target_pairs={{0,2},{1,3},{2,0},{3,1},{4,6},{5,7},{6,4},{7,5},{8,10},{9,11},{10,... | collective-permute-start | bytes 1382408 | tf_op jit(solution)/shard_map/ppermute | solution.py:29
  68.8 22.6 %collective-permute-start.22 = (bf16[256,1024]{1,0:T(8,128)(2,1)S(1)}, bf16[256,1024]{1,0:T(8,128)(2,1)S(1)}, u32[]{:S(2)}, u32[]{:S(2)}) collective-permute-start(bf16[256,1024]{1,0:T(8,128)(2,1)S(1)} %collective-permute-done.10.refs_10_), channel_id=1, source_target_pairs={{0,16},{1,17},{2,18},{3,19},{4,20},{5,21},{6,22},{7,23},{8,24},{9,... | collective-permute-start | bytes 1572872 | tf_op jit(solution)/shard_map/ppermute | solution.py:29
  70.1 21.3 %collective-permute-start.23 = (bf16[256,1024]{1,0:T(8,128)(2,1)S(1)}, bf16[256,1024]{1,0:T(8,128)(2,1)S(1)}, u32[]{:S(2)}, u32[]{:S(2)}) collective-permute-start(bf16[256,1024]{1,0:T(8,128)(2,1)S(1)} %collective-permute-done.10.refs_10_), channel_id=1, source_target_pairs={{0,4},{1,5},{2,6},{3,7},{4,0},{5,1},{6,2},{7,3},{8,12},{9,13},{10,... | collective-permute-start | bytes 1572872 | tf_op jit(solution)/shard_map/ppermute | solution.py:29
  70.8 20.6 %collective-permute-start.24 = (bf16[256,1024]{1,0:T(8,128)(2,1)S(1)}, bf16[256,1024]{1,0:T(8,128)(2,1)S(1)}, u32[]{:S(2)}, u32[]{:S(2)}) collective-permute-start(bf16[256,1024]{1,0:T(8,128)(2,1)S(1)} %collective-permute-done.11.refs_12_), channel_id=1, source_target_pairs={{0,4},{1,5},{2,6},{3,7},{4,0},{5,1},{6,2},{7,3},{8,12},{9,13},{10,... | collective-permute-start | bytes 1572872 | tf_op jit(solution)/shard_map/ppermute | solution.py:29
  91.4 14.2 %collective-permute-start.25 = (bf16[240,960]{1,0:T(8,128)(2,1)}, bf16[240,960]{1,0:T(8,128)(2,1)S(1)}, u32[]{:S(2)}, u32[]{:S(2)}) collective-permute-start(bf16[240,960]{1,0:T(8,128)(2,1)} %collective-permute-done.20.refs_18_), channel_id=1, source_target_pairs={{0,1},{1,0},{2,3},{3,2},{4,5},{5,4},{6,7},{7,6},{8,9},{9,8},{10,11... | collective-permute-start | bytes 1382408 | tf_op jit(solution)/shard_map/ppermute | solution.py:29
  91.5 10.4 %collective-permute-start.28 = (bf16[1024,128]{1,0:T(8,128)(2,1)}, bf16[1024,128]{1,0:T(8,128)(2,1)S(1)}, u32[]{:S(2)}, u32[]{:S(2)}) collective-permute-start(bf16[1024,128]{1,0:T(8,128)(2,1)} %get-tuple-element.193.refs_0_), channel_id=1, source_target_pairs={{0,24},{1,25},{2,26},{3,27},{4,28},{5,29},{6,30},{7,31},{8,16},{9,... | collective-permute-start | bytes 786440 | tf_op jit(solution)/shard_map/ppermute | solution.py:29
  92.6 13.0 %collective-permute-start.27 = (bf16[1024,128]{1,0:T(8,128)(2,1)}, bf16[1024,128]{1,0:T(8,128)(2,1)S(1)}, u32[]{:S(2)}, u32[]{:S(2)}) collective-permute-start(bf16[1024,128]{1,0:T(8,128)(2,1)} %get-tuple-element.193.refs_0_), channel_id=1, source_target_pairs={{0,16},{1,17},{2,18},{3,19},{4,20},{5,21},{6,22},{7,23},{8,24},{9,... | collective-permute-start | bytes 786440 | tf_op jit(solution)/shard_map/ppermute | solution.py:29
  94.1 11.5 %collective-permute-start.26 = (bf16[1024,128]{1,0:T(8,128)(2,1)}, bf16[1024,128]{1,0:T(8,128)(2,1)S(1)}, u32[]{:S(2)}, u32[]{:S(2)}) collective-permute-start(bf16[1024,128]{1,0:T(8,128)(2,1)} %get-tuple-element.193.refs_0_), channel_id=1, source_target_pairs={{0,8},{1,9},{2,10},{3,11},{4,12},{5,13},{6,14},{7,15},{8,0},{9,1},... | collective-permute-start | bytes 786440 | tf_op jit(solution)/shard_map/ppermute | solution.py:29
  105.6 3.4 %collective-permute-start.33 = (bf16[256,1024]{1,0:T(8,128)(2,1)S(1)}, bf16[256,1024]{1,0:T(8,128)(2,1)S(1)}, u32[]{:S(2)}, u32[]{:S(2)}) collective-permute-start(bf16[256,1024]{1,0:T(8,128)(2,1)S(1)} %collective-permute-done.22.refs_14_), channel_id=1, source_target_pairs={{0,4},{1,5},{2,6},{3,7},{4,0},{5,1},{6,2},{7,3},{8,12},{9,13},{10,... | collective-permute-start | bytes 1572872 | tf_op jit(solution)/shard_map/ppermute | solution.py:29
  105.6 2.8 %collective-permute-start.29 = (bf16[1024,128]{1,0:T(8,128)(2,1)}, bf16[1024,128]{1,0:T(8,128)(2,1)S(1)}, u32[]{:S(2)}, u32[]{:S(2)}) collective-permute-start(bf16[1024,128]{1,0:T(8,128)(2,1)} %get-tuple-element.193.refs_0_), channel_id=1, source_target_pairs={{0,4},{1,5},{2,6},{3,7},{4,0},{5,1},{6,2},{7,3},{8,12},{9,13},{10,... | collective-permute-start | bytes 786440 | tf_op jit(solution)/shard_map/ppermute | solution.py:29
  128.4 2.9 %collective-permute-start.34 = (bf16[512,1024]{1,0:T(8,128)(2,1)}, bf16[512,1024]{1,0:T(8,128)(2,1)S(1)}, u32[]{:S(2)}, u32[]{:S(2)}) collective-permute-start(bf16[512,1024]{1,0:T(8,128)(2,1)} %get-tuple-element.205), channel_id=1, source_target_pairs={{0,4},{1,5},{2,6},{3,7},{4,0},{5,1},{6,2},{7,3},{8,12},{9,13},{10,... | collective-permute-start | bytes 3145736 | tf_op jit(solution)/shard_map/ppermute | solution.py:29
  132.8 9.2 %collective-permute-start.36 = (bf16[128,960]{1,0:T(8,128)(2,1)S(1)}, bf16[128,960]{1,0:T(8,128)(2,1)S(1)}, u32[]{:S(2)}, u32[]{:S(2)}) collective-permute-start(bf16[128,960]{1,0:T(8,128)(2,1)S(1)} %get-tuple-element.216), channel_id=1, source_target_pairs={{0,8},{1,9},{2,10},{3,11},{4,12},{5,13},{6,14},{7,15},{8,0},{9,1},... | collective-permute-start | bytes 737288 | tf_op jit(solution)/shard_map/ppermute | solution.py:29
  134.1 13.7 %collective-permute-start.37 = (bf16[128,960]{1,0:T(8,128)(2,1)S(1)}, bf16[128,960]{1,0:T(8,128)(2,1)S(1)}, u32[]{:S(2)}, u32[]{:S(2)}) collective-permute-start(bf16[128,960]{1,0:T(8,128)(2,1)S(1)} %get-tuple-element.217), channel_id=1, source_target_pairs={{0,16},{1,17},{2,18},{3,19},{4,20},{5,21},{6,22},{7,23},{8,24},{9,... | collective-permute-start | bytes 737288 | tf_op jit(solution)/shard_map/ppermute | solution.py:29
  134.7 13.1 %collective-permute-start.38 = (bf16[128,960]{1,0:T(8,128)(2,1)S(1)}, bf16[128,960]{1,0:T(8,128)(2,1)S(1)}, u32[]{:S(2)}, u32[]{:S(2)}) collective-permute-start(bf16[128,960]{1,0:T(8,128)(2,1)S(1)} %get-tuple-element.218), channel_id=1, source_target_pairs={{0,24},{1,25},{2,26},{3,27},{4,28},{5,29},{6,30},{7,31},{8,16},{9,... | collective-permute-start | bytes 737288 | tf_op jit(solution)/shard_map/ppermute | solution.py:29
  136.3 12.4 %collective-permute-start.35 = (bf16[240,960]{1,0:T(8,128)(2,1)S(1)}, bf16[240,960]{1,0:T(8,128)(2,1)S(1)}, u32[]{:S(2)}, u32[]{:S(2)}) collective-permute-start(bf16[240,960]{1,0:T(8,128)(2,1)S(1)} %get-tuple-element.215), channel_id=1, source_target_pairs={{0,1},{1,0},{2,3},{3,2},{4,5},{5,4},{6,7},{7,6},{8,9},{9,8},{10,11... | collective-permute-start | bytes 1382408 | tf_op jit(solution)/shard_map/ppermute | solution.py:29
  148.7 3.2 %collective-permute-start.40 = (bf16[512,1024]{1,0:T(8,128)(2,1)S(1)}, bf16[512,1024]{1,0:T(8,128)(2,1)S(1)}, u32[]{:S(2)}, u32[]{:S(2)}) collective-permute-start(bf16[512,1024]{1,0:T(8,128)(2,1)S(1)} %get-tuple-element.228), channel_id=1, source_target_pairs={{0,4},{1,5},{2,6},{3,7},{4,0},{5,1},{6,2},{7,3},{8,12},{9,13},{10,... | collective-permute-start | bytes 3145736 | tf_op jit(solution)/shard_map/ppermute | solution.py:29
  152.0 7.2 %collective-permute-start.41 = (bf16[256,256]{1,0:T(8,128)(2,1)S(1)}, bf16[256,256]{1,0:T(8,128)(2,1)S(1)}, u32[]{:S(2)}, u32[]{:S(2)}) collective-permute-start(bf16[256,256]{1,0:T(8,128)(2,1)S(1)} %get-tuple-element.234), channel_id=1, source_target_pairs={{0,8},{1,9},{2,10},{3,11},{4,12},{5,13},{6,14},{7,15},{8,0},{9,1},... | collective-permute-start | bytes 393224 | tf_op jit(solution)/shard_map/ppermute | solution.py:29
  153.3 8.3 %collective-permute-start.42 = (bf16[256,256]{1,0:T(8,128)(2,1)S(1)}, bf16[256,256]{1,0:T(8,128)(2,1)S(1)}, u32[]{:S(2)}, u32[]{:S(2)}) collective-permute-start(bf16[256,256]{1,0:T(8,128)(2,1)S(1)} %get-tuple-element.235), channel_id=1, source_target_pairs={{0,16},{1,17},{2,18},{3,19},{4,20},{5,21},{6,22},{7,23},{8,24},{9,... | collective-permute-start | bytes 393224 | tf_op jit(solution)/shard_map/ppermute | solution.py:29
  153.9 7.7 %collective-permute-start.43 = (bf16[256,256]{1,0:T(8,128)(2,1)S(1)}, bf16[256,256]{1,0:T(8,128)(2,1)S(1)}, u32[]{:S(2)}, u32[]{:S(2)}) collective-permute-start(bf16[256,256]{1,0:T(8,128)(2,1)S(1)} %get-tuple-element.236), channel_id=1, source_target_pairs={{0,24},{1,25},{2,26},{3,27},{4,28},{5,29},{6,30},{7,31},{8,16},{9,... | collective-permute-start | bytes 393224 | tf_op jit(solution)/shard_map/ppermute | solution.py:29
  155.8 26.7 %collective-permute-start.45 = (bf16[240,960]{1,0:T(8,128)(2,1)S(1)}, bf16[240,960]{1,0:T(8,128)(2,1)S(1)}, u32[]{:S(2)}, u32[]{:S(2)}) collective-permute-start(bf16[240,960]{1,0:T(8,128)(2,1)S(1)} %shard_map.233), channel_id=1, source_target_pairs={{0,2},{1,3},{2,0},{3,1},{4,6},{5,7},{6,4},{7,5},{8,10},{9,11},{10,... | collective-permute-start | bytes 1382408 | tf_op jit(solution)/shard_map/ppermute | solution.py:29
  158.8 23.8 %collective-permute-start.44 = (bf16[240,960]{1,0:T(8,128)(2,1)S(1)}, bf16[240,960]{1,0:T(8,128)(2,1)S(1)}, u32[]{:S(2)}, u32[]{:S(2)}) collective-permute-start(bf16[240,960]{1,0:T(8,128)(2,1)S(1)} %get-tuple-element.245), channel_id=1, source_target_pairs={{0,1},{1,0},{2,3},{3,2},{4,5},{5,4},{6,7},{7,6},{8,9},{9,8},{10,11... | collective-permute-start | bytes 1382408 | tf_op jit(solution)/shard_map/ppermute | solution.py:29
  161.6 20.9 %collective-permute-start.46 = (bf16[128,960]{1,0:T(8,128)(2,1)S(1)}, bf16[128,960]{1,0:T(8,128)(2,1)S(1)}, u32[]{:S(2)}, u32[]{:S(2)}) collective-permute-start(bf16[128,960]{1,0:T(8,128)(2,1)S(1)} %get-tuple-element.249), channel_id=1, source_target_pairs={{0,8},{1,9},{2,10},{3,11},{4,12},{5,13},{6,14},{7,15},{8,0},{9,1},... | collective-permute-start | bytes 737288 | tf_op jit(solution)/shard_map/ppermute | solution.py:29
  162.4 20.2 %collective-permute-start.47 = (bf16[128,960]{1,0:T(8,128)(2,1)S(1)}, bf16[128,960]{1,0:T(8,128)(2,1)S(1)}, u32[]{:S(2)}, u32[]{:S(2)}) collective-permute-start(bf16[128,960]{1,0:T(8,128)(2,1)S(1)} %get-tuple-element.251), channel_id=1, source_target_pairs={{0,16},{1,17},{2,18},{3,19},{4,20},{5,21},{6,22},{7,23},{8,24},{9,... | collective-permute-start | bytes 737288 | tf_op jit(solution)/shard_map/ppermute | solution.py:29
  163.6 19.0 %collective-permute-start.48 = (bf16[128,960]{1,0:T(8,128)(2,1)S(1)}, bf16[128,960]{1,0:T(8,128)(2,1)S(1)}, u32[]{:S(2)}, u32[]{:S(2)}) collective-permute-start(bf16[128,960]{1,0:T(8,128)(2,1)S(1)} %get-tuple-element.253), channel_id=1, source_target_pairs={{0,24},{1,25},{2,26},{3,27},{4,28},{5,29},{6,30},{7,31},{8,16},{9,... | collective-permute-start | bytes 737288 | tf_op jit(solution)/shard_map/ppermute | solution.py:29
  182.6 2.7 %collective-permute-start.49 = (bf16[4096,128]{1,0:T(8,128)(2,1)S(1)}, bf16[4096,128]{1,0:T(8,128)(2,1)S(1)}, u32[]{:S(2)}, u32[]{:S(2)}) collective-permute-start(bf16[4096,128]{1,0:T(8,128)(2,1)S(1)} %get-tuple-element.254), channel_id=1, source_target_pairs={{0,4},{1,5},{2,6},{3,7},{4,0},{5,1},{6,2},{7,3},{8,12},{9,13},{10,... | collective-permute-start | bytes 3145736 | tf_op jit(solution)/shard_map/ppermute | solution.py:29
  186.9 23.4 %collective-permute-start.51 = (bf16[240,1024]{1,0:T(8,128)(2,1)S(1)}, bf16[240,1024]{1,0:T(8,128)(2,1)S(1)}, u32[]{:S(2)}, u32[]{:S(2)}) collective-permute-start(bf16[240,1024]{1,0:T(8,128)(2,1)S(1)} %shard_map.236.m_ref), channel_id=1, source_target_pairs={{0,16},{1,17},{2,18},{3,19},{4,20},{5,21},{6,22},{7,23},{8,24},{9,... | collective-permute-start | bytes 1474568 | tf_op jit(solution)/shard_map/ppermute | solution.py:29
  187.5 22.8 %collective-permute-start.50 = (bf16[240,1024]{1,0:T(8,128)(2,1)S(1)}, bf16[240,1024]{1,0:T(8,128)(2,1)S(1)}, u32[]{:S(2)}, u32[]{:S(2)}) collective-permute-start(bf16[240,1024]{1,0:T(8,128)(2,1)S(1)} %shard_map.236.m_ref), channel_id=1, source_target_pairs={{0,8},{1,9},{2,10},{3,11},{4,12},{5,13},{6,14},{7,15},{8,0},{9,1},... | collective-permute-start | bytes 1474568 | tf_op jit(solution)/shard_map/ppermute | solution.py:29
  188.9 19.9 %collective-permute-start.53 = (bf16[1024,128]{1,0:T(8,128)(2,1)S(1)}, bf16[1024,128]{1,0:T(8,128)(2,1)S(1)}, u32[]{:S(2)}, u32[]{:S(2)}) collective-permute-start(bf16[1024,128]{1,0:T(8,128)(2,1)S(1)} %get-tuple-element.269), channel_id=1, source_target_pairs={{0,2},{1,3},{2,0},{3,1},{4,6},{5,7},{6,4},{7,5},{8,10},{9,11},{10,... | collective-permute-start | bytes 786440 | tf_op jit(solution)/shard_map/ppermute | solution.py:29
  191.6 17.2 %collective-permute-start.54 = (bf16[1024,128]{1,0:T(8,128)(2,1)S(1)}, bf16[1024,128]{1,0:T(8,128)(2,1)S(1)}, u32[]{:S(2)}, u32[]{:S(2)}) collective-permute-start(bf16[1024,128]{1,0:T(8,128)(2,1)S(1)} %get-tuple-element.270), channel_id=1, source_target_pairs={{0,3},{1,2},{2,1},{3,0},{4,7},{5,6},{6,5},{7,4},{8,11},{9,10},{10,... | collective-permute-start | bytes 786440 | tf_op jit(solution)/shard_map/ppermute | solution.py:29
  191.6 18.6 %collective-permute-start.52 = (bf16[1024,128]{1,0:T(8,128)(2,1)S(1)}, bf16[1024,128]{1,0:T(8,128)(2,1)S(1)}, u32[]{:S(2)}, u32[]{:S(2)}) collective-permute-start(bf16[1024,128]{1,0:T(8,128)(2,1)S(1)} %get-tuple-element.255), channel_id=1, source_target_pairs={{0,1},{1,0},{2,3},{3,2},{4,5},{5,4},{6,7},{7,6},{8,9},{9,8},{10,11... | collective-permute-start | bytes 786440 | tf_op jit(solution)/shard_map/ppermute | solution.py:29
  214.0 2.7 %collective-permute-start.55 = (bf16[512,1024]{1,0:T(8,128)(2,1)S(1)}, bf16[512,1024]{1,0:T(8,128)(2,1)S(1)}, u32[]{:S(2)}, u32[]{:S(2)}) collective-permute-start(bf16[512,1024]{1,0:T(8,128)(2,1)S(1)} %get-tuple-element.276), channel_id=1, source_target_pairs={{0,4},{1,5},{2,6},{3,7},{4,0},{5,1},{6,2},{7,3},{8,12},{9,13},{10,... | collective-permute-start | bytes 3145736 | tf_op jit(solution)/shard_map/ppermute | solution.py:29
  214.1 25.6 %collective-permute-start.56 = (bf16[240,1024]{1,0:T(8,128)(2,1)S(1)}, bf16[240,1024]{1,0:T(8,128)(2,1)S(1)}, u32[]{:S(2)}, u32[]{:S(2)}) collective-permute-start(bf16[240,1024]{1,0:T(8,128)(2,1)S(1)} %collective-permute-done.50.x_ref), channel_id=1, source_target_pairs={{0,16},{1,17},{2,18},{3,19},{4,20},{5,21},{6,22},{7,23},{8,24},{9,... | collective-permute-start | bytes 1474568 | tf_op jit(solution)/shard_map/ppermute | solution.py:29
  217.0 22.7 %collective-permute-start.57 = (bf16[256,960]{1,0:T(8,128)(2,1)S(1)}, bf16[256,960]{1,0:T(8,128)(2,1)S(1)}, u32[]{:S(2)}, u32[]{:S(2)}) collective-permute-start(bf16[256,960]{1,0:T(8,128)(2,1)S(1)} %get-tuple-element.281), channel_id=1, source_target_pairs={{0,16},{1,17},{2,18},{3,19},{4,20},{5,21},{6,22},{7,23},{8,24},{9,... | collective-permute-start | bytes 1474568 | tf_op jit(solution)/shard_map/ppermute | solution.py:29
  217.9 13.1 %collective-permute-start.58 = (bf16[256,384]{1,0:T(8,128)(2,1)S(1)}, bf16[256,384]{1,0:T(8,128)(2,1)S(1)}, u32[]{:S(2)}, u32[]{:S(2)}) collective-permute-start(bf16[256,384]{1,0:T(8,128)(2,1)S(1)} %get-tuple-element.282), channel_id=1, source_target_pairs={{0,1},{1,0},{2,3},{3,2},{4,5},{5,4},{6,7},{7,6},{8,9},{9,8},{10,11... | collective-permute-start | bytes 589832 | tf_op jit(solution)/shard_map/ppermute | solution.py:29
  222.5 17.2 %collective-permute-start.59 = (bf16[256,384]{1,0:T(8,128)(2,1)S(1)}, bf16[256,384]{1,0:T(8,128)(2,1)S(1)}, u32[]{:S(2)}, u32[]{:S(2)}) collective-permute-start(bf16[256,384]{1,0:T(8,128)(2,1)S(1)} %get-tuple-element.283), channel_id=1, source_target_pairs={{0,2},{1,3},{2,0},{3,1},{4,6},{5,7},{6,4},{7,5},{8,10},{9,11},{10,... | collective-permute-start | bytes 589832 | tf_op jit(solution)/shard_map/ppermute | solution.py:29
  223.7 16.0 %collective-permute-start.60 = (bf16[256,384]{1,0:T(8,128)(2,1)S(1)}, bf16[256,384]{1,0:T(8,128)(2,1)S(1)}, u32[]{:S(2)}, u32[]{:S(2)}) collective-permute-start(bf16[256,384]{1,0:T(8,128)(2,1)S(1)} %get-tuple-element.284), channel_id=1, source_target_pairs={{0,3},{1,2},{2,1},{3,0},{4,7},{5,6},{6,5},{7,4},{8,11},{9,10},{10,... | collective-permute-start | bytes 589832 | tf_op jit(solution)/shard_map/ppermute | solution.py:29
  239.9 5.1 %collective-permute-start.62 = (bf16[960,1024]{1,0:T(8,128)(2,1)S(1)}, bf16[960,1024]{1,0:T(8,128)(2,1)S(1)}, u32[]{:S(2)}, u32[]{:S(2)}) collective-permute-start(bf16[960,1024]{1,0:T(8,128)(2,1)S(1)} %pad_maximum_fusion), channel_id=1, source_target_pairs={{0,4},{1,5},{2,6},{3,7},{4,0},{5,1},{6,2},{7,3},{8,12},{9,13},{10,... | collective-permute-start | bytes 5898248 | tf_op jit(solution)/shard_map/ppermute | solution.py:29
  240.0 10.6 %collective-permute-start.65 = (bf16[256,384]{1,0:T(8,128)(2,1)S(1)}, bf16[256,384]{1,0:T(8,128)(2,1)S(1)}, u32[]{:S(2)}, u32[]{:S(2)}) collective-permute-start(bf16[256,384]{1,0:T(8,128)(2,1)S(1)} %add_convert_fusion.refs_0_), channel_id=1, source_target_pairs={{0,24},{1,25},{2,26},{3,27},{4,28},{5,29},{6,30},{7,31},{8,16},{9,... | collective-permute-start | bytes 589832 | tf_op jit(solution)/shard_map/ppermute | solution.py:29
  241.4 11.1 %collective-permute-start.64 = (bf16[256,384]{1,0:T(8,128)(2,1)S(1)}, bf16[256,384]{1,0:T(8,128)(2,1)S(1)}, u32[]{:S(2)}, u32[]{:S(2)}) collective-permute-start(bf16[256,384]{1,0:T(8,128)(2,1)S(1)} %add_convert_fusion.refs_0_), channel_id=1, source_target_pairs={{0,16},{1,17},{2,18},{3,19},{4,20},{5,21},{6,22},{7,23},{8,24},{9,... | collective-permute-start | bytes 589832 | tf_op jit(solution)/shard_map/ppermute | solution.py:29
  242.8 9.9 %collective-permute-start.63 = (bf16[256,384]{1,0:T(8,128)(2,1)S(1)}, bf16[256,384]{1,0:T(8,128)(2,1)S(1)}, u32[]{:S(2)}, u32[]{:S(2)}) collective-permute-start(bf16[256,384]{1,0:T(8,128)(2,1)S(1)} %add_convert_fusion.refs_0_), channel_id=1, source_target_pairs={{0,8},{1,9},{2,10},{3,11},{4,12},{5,13},{6,14},{7,15},{8,0},{9,1},... | collective-permute-start | bytes 589832 | tf_op jit(solution)/shard_map/ppermute | solution.py:29
  243.7 14.2 %collective-permute-start.61 = (bf16[128,960]{1,0:T(8,128)(2,1)S(1)}, bf16[128,960]{1,0:T(8,128)(2,1)S(1)}, u32[]{:S(2)}, u32[]{:S(2)}) collective-permute-start(bf16[128,960]{1,0:T(8,128)(2,1)S(1)} %get-tuple-element.287), channel_id=1, source_target_pairs={{0,8},{1,9},{2,10},{3,11},{4,12},{5,13},{6,14},{7,15},{8,0},{9,1},... | collective-permute-start | bytes 737288 | tf_op jit(solution)/shard_map/ppermute | solution.py:29
  257.9 3.1 %collective-permute-start.66 = (bf16[256,384]{1,0:T(8,128)(2,1)S(1)}, bf16[256,384]{1,0:T(8,128)(2,1)S(1)}, u32[]{:S(2)}, u32[]{:S(2)}) collective-permute-start(bf16[256,384]{1,0:T(8,128)(2,1)S(1)} %add_convert_fusion.refs_0_), channel_id=1, source_target_pairs={{0,4},{1,5},{2,6},{3,7},{4,0},{5,1},{6,2},{7,3},{8,12},{9,13},{10,... | collective-permute-start | bytes 589832 | tf_op jit(solution)/shard_map/ppermute | solution.py:29
  257.9 3.1 %collective-permute-start.67 = (bf16[256,384]{1,0:T(8,128)(2,1)S(1)}, bf16[256,384]{1,0:T(8,128)(2,1)S(1)}, u32[]{:S(2)}, u32[]{:S(2)}) collective-permute-start(bf16[256,384]{1,0:T(8,128)(2,1)S(1)} %collective-permute-done.63.refs_2_), channel_id=1, source_target_pairs={{0,4},{1,5},{2,6},{3,7},{4,0},{5,1},{6,2},{7,3},{8,12},{9,13},{10,... | collective-permute-start | bytes 589832 | tf_op jit(solution)/shard_map/ppermute | solution.py:29
  258.4 2.6 collective-permute-start.68
  258.4 2.6 collective-permute-start.69
  (62 other events, 583.0 us)
